TPU v7x, 128 devices: a whole 4x4x4 slice. The times are simulated.
128 devices in a mesh: lat: 32 (over x, z_lo, y), lon: 4 (over z_hi, core).
Axes of the slice: x: 4, y: 4, z: 4 (z_hi: 2, z_lo: 2; z = z_hi * 2 + z_lo), core: 2. Of those that a mesh axis runs over, the one named last changes fastest.
Arguments:
- ocean_state: bfloat16 [76, 256, 4096], P(None, 'lat', 'lon'), may hold values from -6 to 6
- sea_mask: int32 [256, 4096], P('lat', 'lon'), may hold values 0 or 1
- ocean_w1: bfloat16 [64, 76, 3, 3], replicated, may hold values from -0.21875 to 0.21875
- ocean_b1: float32 [64], replicated, may hold values from -3 to 3
- ocean_w2: bfloat16 [64, 64, 3, 3], replicated, may hold values from -0.25 to 0.25
- ocean_b2: float32 [64], replicated, may hold values from -3 to 3
- regrid_weight: bfloat16 [8192, 2, 128, 128], P(('lat', 'lon')), may hold values from -0.5 to 0.5
- route_dev: int32 [8192, 2], P(('lat', 'lon')), may hold values from 0 to 127, as said below
- route_row: int32 [8192, 2], P(('lat', 'lon')), may hold values from 0 to 63
- atmos_state: bfloat16 [64, 2048, 512], P(None, 'lat', 'lon'), may hold values from -6 to 6
- atmos_w1: bfloat16 [64, 64, 3, 3], replicated, may hold values from -0.25 to 0.25
- atmos_b1: float32 [64], replicated, may hold values from -3 to 3
- atmos_w2: bfloat16 [64, 64, 3, 3], replicated, may hold values from -0.25 to 0.25
- atmos_b2: float32 [64], replicated, may hold values from -3 to 3
Outputs:
- ocean_next: bfloat16 [64, 256, 4096], P(None, 'lat', 'lon')
- atmos_next: bfloat16 [64, 2048, 512], P(None, 'lat', 'lon')
Inputs may be any that keep to these rules, and one draw needn't show every extreme that they name: `route_dev`: every intersection of a block of device d = a * 4 + e names a device whose latitude index (device // 4) is a - 1, a or a + 1. In the rows of one device (aligned blocks of 64 rows) no device number appears more than 32 times, and some number appears exactly 32 times; the 2 intersections of one block name different devices.
All inputs are finite; a program needn't handle non-finite values. No bound on the sum of `sea_mask` on one device may be relied on, other than what follows from the above.
Results may differ from a plain program's by a relative error of at most 0.01.
Values may be sent and summed in bfloat16 or wider, within the bound.
A program may use at most 192 MiB of HBM per device.

v0:
```python
import functools

import jax
import jax.numpy as jnp
from jax import lax
from jax.experimental import pallas as pl
from jax.experimental.pallas import tpu as pltpu
from jax.sharding import PartitionSpec as P

MESH = pl.DeviceIdType.MESH
F32 = jnp.float32
BF16 = jnp.bfloat16
CAP = 32
VMEM_LIMIT = 56 * 1024 * 1024


def silu(v):
    return 0.5 * v * (1.0 + jnp.tanh(0.5 * v))


def shifted_sum(taps):
    out = taps.shape[0] // 3
    columns = taps.shape[1]
    return (
        pltpu.roll(taps[0:out], 1, 1)
        + taps[out : 2 * out]
        + pltpu.roll(taps[2 * out :], columns - 1, 1)
    )


def stacked_weight(weight, padded_in):
    out, inn = weight.shape[:2]
    weight = jnp.pad(weight, ((0, 0), (0, padded_in - inn), (0, 0), (0, 0)))
    return weight.transpose(3, 0, 2, 1).reshape(3 * out, 3 * padded_in)


def ocean_kernel(
    place,
    x_ref,
    side_ref,
    top_ref,
    bottom_ref,
    w1_ref,
    b1_ref,
    w2_ref,
    b2_ref,
    regrid_ref,
    next_ref,
    slots_ref,
    tall,
    hidden,
):
    row = lax.rem(pl.program_id(0), 16)
    rows, channels, cols = x_ref.shape
    mask_at = 76

    def first_conv(j):
        field = jnp.concatenate([tall[j], tall[j + 1], tall[j + 2]], axis=0)
        taps = jnp.dot(w1_ref[...], field, preferred_element_type=F32)
        mask = tall[j + 1, mask_at : mask_at + 1, :].astype(F32)
        hidden[j] = (silu(shifted_sum(taps) + b1_ref[...]) * mask).astype(BF16)

    @pl.when(row == 0)
    def _():
        tall[0:2] = top_ref[...]
        tall[2 : 2 + rows, :, 0:cols] = x_ref[...]
        tall[2 : 2 + rows, :, cols:] = side_ref[...]
        tall[2 + rows :] = bottom_ref[...]
        first_conv(0)
        first_conv(1)

    first_conv(lax.rem(row + 2, 16))
    field = jnp.concatenate([hidden[row], hidden[row + 1], hidden[row + 2]], axis=0)
    taps = jnp.dot(w2_ref[...], field, preferred_element_type=F32)
    mask = tall[row + 2, mask_at : mask_at + 1, :].astype(F32)
    result = ((shifted_sum(taps) + b2_ref[...]) * mask).astype(BF16)[:, :cols]
    next_ref[0] = result
    blocks = regrid_ref.shape[0]
    for q in range(blocks):
        field = result[:, q * 128 : (q + 1) * 128]
        both = lax.dot_general(
            field, regrid_ref[q], (((1,), (1,)), ((), ())), preferred_element_type=F32
        ).astype(BF16)
        for k in range(2):
            slots_ref[place[(row * blocks + q) * 2 + k]] = both[:, k * 128 : (k + 1) * 128]


def ocean_step(place, x, side, top, bottom, w1, b1, w2, b2, regrid, slots):
    rows, channels, cols = x.shape
    wide = cols + 128
    out = w2.shape[0] // 3

    def whole(array):
        zeros = (0,) * array.ndim
        return pl.BlockSpec(array.shape, lambda r, place: zeros)

    blocks = regrid.shape[0] // rows
    return pl.pallas_call(
        ocean_kernel,
        out_shape=(
            jax.ShapeDtypeStruct((rows, out, cols), BF16),
            jax.ShapeDtypeStruct((slots, out, 128), BF16),
        ),
        grid_spec=pltpu.PrefetchScalarGridSpec(
            num_scalar_prefetch=1,
            grid=(rows,),
            in_specs=[whole(a) for a in (x, side, top, bottom, w1, b1, w2, b2)]
            + [pl.BlockSpec((blocks, 256, 128), lambda r, place: (r, 0, 0))],
            out_specs=[
                pl.BlockSpec((1, out, cols), lambda r, place: (r, 0, 0)),
                pl.BlockSpec((slots, out, 128), lambda r, place: (0, 0, 0)),
            ],
            scratch_shapes=[
                pltpu.VMEM((rows + 4, channels, wide), BF16),
                pltpu.VMEM((rows + 2, out, wide), BF16),
            ],
        ),
        compiler_params=pltpu.CompilerParams(vmem_limit_bytes=VMEM_LIMIT),
        name="ocean",
    )(place, x, side, top, bottom, w1, b1, w2, b2, regrid)


def exchange_kernel(
    lat_count, lon_count, data, rows, data_in, rows_in, send_sem, recv_sem, row_send, row_recv
):
    lat, lon = lax.axis_index("lat"), lax.axis_index("lon")
    barrier = pltpu.get_barrier_semaphore()

    def partners():
        for offset in (0, -1, 1):
            for step in range(lon_count):
                if offset == 0 and step == 0:
                    continue
                there = lax.rem(lon + step, lon_count)
                ok = jnp.logical_and(lat + offset >= 0, lat + offset < lat_count)
                yield offset, step, there, ok

    def copies(offset, there):
        target = {"lat": lat + offset, "lon": there}
        source = (offset + 1) * lon_count + there
        slot = (1 - offset) * lon_count + lon
        return (
            pltpu.make_async_remote_copy(
                src_ref=data.at[source],
                dst_ref=data_in.at[slot],
                send_sem=send_sem.at[source],
                recv_sem=recv_sem.at[slot],
                device_id=target,
                device_id_type=MESH,
            ),
            pltpu.make_async_remote_copy(
                src_ref=rows.at[source],
                dst_ref=rows_in.at[slot],
                send_sem=row_send.at[source],
                recv_sem=row_recv.at[slot],
                device_id=target,
                device_id_type=MESH,
            ),
        )

    def arrivals(offset, there):
        slot = (offset + 1) * lon_count + there
        return (
            pltpu.make_async_copy(data_in.at[slot], data_in.at[slot], recv_sem.at[slot]),
            pltpu.make_async_copy(rows_in.at[slot], rows_in.at[slot], row_recv.at[slot]),
        )

    for offset, step, there, ok in partners():

        @pl.when(ok)
        def _():
            pl.semaphore_signal(
                barrier, inc=1, device_id={"lat": lat + offset, "lon": there}, device_id_type=MESH
            )

    edge = jnp.logical_or(lat == 0, lat == lat_count - 1)
    pl.semaphore_wait(barrier, jnp.where(edge, 2 * lon_count - 1, 3 * lon_count - 1))

    for offset, step, there, ok in partners():

        @pl.when(ok)
        def _():
            for copy in copies(offset, there):
                copy.start()

    own = lon_count + lon
    local = (
        pltpu.make_async_copy(data.at[own], data_in.at[own], recv_sem.at[own]),
        pltpu.make_async_copy(rows.at[own], rows_in.at[own], row_recv.at[own]),
    )
    for copy in local:
        copy.start()
    for copy in local:
        copy.wait()

    for offset, step, there, ok in partners():

        @pl.when(ok)
        def _():
            for copy in copies(offset, there):
                copy.wait_send()
            for copy in arrivals(offset, there):
                copy.wait()


def exchange(data, rows, lat_count, lon_count):
    count = 3 * lon_count
    return pl.pallas_call(
        functools.partial(exchange_kernel, lat_count, lon_count),
        out_shape=(
            jax.ShapeDtypeStruct(data.shape, data.dtype),
            jax.ShapeDtypeStruct(rows.shape, rows.dtype),
        ),
        in_specs=[pl.BlockSpec(memory_space=pl.ANY)] * 2,
        out_specs=[pl.BlockSpec(memory_space=pl.ANY)] * 2,
        scratch_shapes=[pltpu.SemaphoreType.DMA((count,))] * 4,
        compiler_params=pltpu.CompilerParams(collective_id=0, has_side_effects=True),
        name="exchange",
    )(data, rows)


def merge_kernel(rows, counts, data_ref, atmos_ref, first_ref, edge_ref, total):
    step = pl.program_id(0)

    @pl.when(step == 0)
    def _():
        total[...] = atmos_ref[...].astype(F32)

    def add(s, carry):
        r = rows[step * CAP + s]
        total[r] = total[r] + data_ref[0, s].astype(F32)
        return carry

    lax.fori_loop(0, counts[step], add, 0)

    @pl.when(step == pl.num_programs(0) - 1)
    def _():
        count, channels, cols = first_ref.shape
        lane = lax.broadcasted_iota(jnp.int32, (channels, cols), 1)
        for tile in range(count // 32):
            edge = jnp.zeros((channels, cols), F32)
            for k in range(32):
                v = total[tile * 32 + k]
                first_ref[tile * 32 + k] = v.astype(BF16)
                edge = jnp.where(lane // 4 == k, pltpu.roll(v, (4 * k + 2) % cols, 1), edge)
            edge_ref[tile] = edge.astype(BF16)


def merge(rows, counts, data, atmos):
    steps = data.shape[0]
    count, channels, cols = atmos.shape
    return pl.pallas_call(
        merge_kernel,
        out_shape=(
            jax.ShapeDtypeStruct(atmos.shape, BF16),
            jax.ShapeDtypeStruct((count // 32, channels, cols), BF16),
        ),
        grid_spec=pltpu.PrefetchScalarGridSpec(
            num_scalar_prefetch=2,
            grid=(steps,),
            in_specs=[
                pl.BlockSpec((1,) + data.shape[1:], lambda s, a, b: (s, 0, 0, 0)),
                pl.BlockSpec(atmos.shape, lambda s, a, b: (0, 0, 0)),
            ],
            out_specs=[
                pl.BlockSpec(atmos.shape, lambda s, a, b: (0, 0, 0)),
                pl.BlockSpec((count // 32, channels, cols), lambda s, a, b: (0, 0, 0)),
            ],
            scratch_shapes=[pltpu.VMEM(atmos.shape, F32)],
        ),
        compiler_params=pltpu.CompilerParams(vmem_limit_bytes=VMEM_LIMIT),
        name="merge",
    )(rows, counts, data, atmos)


def atmos_kernel(
    inside, a_ref, top_ref, bottom_ref, side_ref, w1_ref, b1_ref, w2_ref, b2_ref, out_ref, tall, second
):
    count, channels, cols = a_ref.shape
    group = 2

    tall[0:2, :, 0:cols] = top_ref[...]
    tall[2 : 2 + count, :, 0:cols] = a_ref[...]
    tall[2 + count :, :, 0:cols] = bottom_ref[...]
    for j in range(count + 4):
        r = j - 2
        tile, k = (r // 32 + 1, r % 32)
        v = side_ref[tile].astype(F32)
        tall[j, :, cols:] = pltpu.roll(v, (126 - 4 * k) % cols, 1).astype(BF16)

    def conv(source, weight, start):
        fields = [
            jnp.concatenate([source[start + i + d] for d in range(3)], axis=0)
            for i in range(group)
        ]
        return jnp.dot(weight, jnp.concatenate(fields, axis=1), preferred_element_type=F32)

    def first(step, carry):
        start = step * group
        taps = conv(tall, w1_ref[...], start)
        for i in range(group):
            j = start + i
            value = silu(shifted_sum(taps[:, i * 2 * cols : (i + 1) * 2 * cols]) + b1_ref[...])
            keep = jnp.where(
                j == 0, inside[0], jnp.where(j == count + 1, inside[1], 1)
            ).astype(F32)
            second[j] = (value * keep).astype(BF16)
        return carry

    lax.fori_loop(0, (count + 2) // group, first, 0)

    def last(step, carry):
        start = step * group
        taps = conv(second, w2_ref[...], start)
        for i in range(group):
            j = start + i
            value = shifted_sum(taps[:, i * 2 * cols : (i + 1) * 2 * cols])[:, :cols]
            out_ref[j] = (a_ref[j].astype(F32) + (value + b2_ref[...])).astype(BF16)
        return carry

    lax.fori_loop(0, count // group, last, 0)


def atmos_step(inside, a, top, bottom, side, w1, b1, w2, b2):
    count, channels, cols = a.shape
    vmem = pl.BlockSpec(memory_space=pltpu.VMEM)
    return pl.pallas_call(
        atmos_kernel,
        out_shape=jax.ShapeDtypeStruct(a.shape, BF16),
        in_specs=[pl.BlockSpec(memory_space=pltpu.SMEM)] + [vmem] * 8,
        out_specs=vmem,
        scratch_shapes=[
            pltpu.VMEM((count + 4, channels, 2 * cols), BF16),
            pltpu.VMEM((count + 2, channels, 2 * cols), BF16),
        ],
        compiler_params=pltpu.CompilerParams(vmem_limit_bytes=VMEM_LIMIT),
        name="atmos",
    )(inside, a, top, bottom, side, w1, b1, w2, b2)


def from_left(value, axis, periodic):
    count = lax.axis_size(axis)
    pairs = [(i, i + 1) for i in range(count - 1)] + ([(count - 1, 0)] if periodic else [])
    return lax.ppermute(value, axis, pairs)


def from_right(value, axis, periodic):
    count = lax.axis_size(axis)
    pairs = [(i + 1, i) for i in range(count - 1)] + ([(0, count - 1)] if periodic else [])
    return lax.ppermute(value, axis, pairs)


def per_device(
    ocean_state,
    sea_mask,
    ocean_w1,
    ocean_b1,
    ocean_w2,
    ocean_b2,
    regrid_weight,
    route_dev,
    route_row,
    atmos_state,
    atmos_w1,
    atmos_b1,
    atmos_w2,
    atmos_b2,
):
    lat_count, lon_count = lax.axis_size("lat"), lax.axis_size("lon")
    lat, lon = lax.axis_index("lat"), lax.axis_index("lon")
    buckets = 3 * lon_count

    field = jnp.concatenate(
        [
            ocean_state,
            sea_mask.astype(BF16)[None],
            jnp.zeros((3,) + sea_mask.shape, BF16),
        ],
        axis=0,
    ).transpose(1, 0, 2)
    left = from_left(field[:, :, -128:], "lon", True)
    right = from_right(field[:, :, :128], "lon", True)
    lane = jnp.arange(128, dtype=jnp.int32)
    side = jnp.where(lane[None, None, :] < 64, right, left)
    top = from_left(jnp.concatenate([field[-2:], side[-2:]], axis=2), "lat", False)
    bottom = from_right(jnp.concatenate([field[:2], side[:2]], axis=2), "lat", False)

    target = route_dev.reshape(-1)
    slots = target.shape[0]
    bucket = (target // lon_count - lat + 1) * lon_count + target % lon_count
    order = jnp.arange(slots, dtype=jnp.int32)
    earlier = (bucket[:, None] == bucket[None, :]) & (order[None, :] < order[:, None])
    place = bucket * CAP + jnp.sum(earlier.astype(jnp.int32), axis=1)
    hit = jnp.arange(buckets * CAP, dtype=jnp.int32)[:, None] == place[None, :]
    rows_out = jnp.max(jnp.where(hit, route_row.reshape(-1)[None, :], -1), axis=1)
    rows_out = jnp.pad(
        rows_out.reshape(buckets, 1, CAP), ((0, 0), (0, 7), (0, 128 - CAP)), constant_values=-1
    )

    ocean_next, outgoing = ocean_step(
        place,
        field,
        side,
        top,
        bottom,
        stacked_weight(ocean_w1, 80),
        ocean_b1[:, None],
        stacked_weight(ocean_w2, 64),
        ocean_b2[:, None],
        regrid_weight.reshape(-1, 256, 128),
        buckets * CAP,
    )
    incoming, rows_in = exchange(
        outgoing.reshape((buckets, CAP) + outgoing.shape[1:]), rows_out, lat_count, lon_count
    )
    source_lat = lat + jnp.arange(buckets, dtype=jnp.int32) // lon_count - 1
    there = (source_lat >= 0) & (source_lat < lat_count)
    rows_in = rows_in[:, 0, :CAP]
    counts = jnp.where(there, jnp.sum((rows_in >= 0).astype(jnp.int32), axis=1), 0)

    first, edge = merge(rows_in.reshape(-1), counts, incoming, atmos_state.transpose(1, 0, 2))
    left = from_left(edge, "lon", True)
    right = from_right(edge, "lon", True)
    side = jnp.where(lane[None, None, :] % 4 < 2, left, right)
    top = from_left(jnp.concatenate([first[-2:], side[1:]], axis=0), "lat", False)
    bottom = from_right(jnp.concatenate([first[:2], side[:1]], axis=0), "lat", False)
    side = jnp.concatenate([top[2:], side, bottom[2:]], axis=0)
    inside = jnp.stack([lat > 0, lat < lat_count - 1]).astype(jnp.int32)
    atmos_next = atmos_step(
        inside,
        first,
        top[:2],
        bottom[:2],
        side,
        stacked_weight(atmos_w1, 64),
        atmos_b1[:, None],
        stacked_weight(atmos_w2, 64),
        atmos_b2[:, None],
    )
    return ocean_next.transpose(1, 0, 2), atmos_next.transpose(1, 0, 2)


def solution(mesh):
    in_specs = (
        P(None, "lat", "lon"),
        P("lat", "lon"),
        P(),
        P(),
        P(),
        P(),
        P(("lat", "lon"), None, None, None),
        P(("lat", "lon"), None),
        P(("lat", "lon"), None),
        P(None, "lat", "lon"),
        P(),
        P(),
        P(),
        P(),
    )
    out_specs = (P(None, "lat", "lon"), P(None, "lat", "lon"))
    return jax.shard_map(
        per_device, mesh=mesh, in_specs=in_specs, out_specs=out_specs, check_vma=False
    )
```

profile of v0, /device:TPU:3, one launch (start us, length us, event | category | flops | bytes accessed | tf_op | source)
XLA Modules:
  0.0 189.2 jit_solution(10357166179923132348)
XLA Ops:
  0.6 2.0 %copy.46 = bf16[76,8,1024]{2,0,1:T(8,128)(2,1)S(1)} copy(bf16[76,8,1024]{2,1,0:T(8,128)(2,1)} %param.14) | data formatting | bytes 2490368 | tf_op args[0]
  2.8 0.5 maximum_bitcast_fusion.x_ref
  3.4 0.7 collective-permute-start
  4.1 3.6 %collective-permute-start.1 = (bf16[8,80,128]{2,1,0:T(8,128)(2,1)S(1)}, bf16[8,80,128]{2,1,0:T(8,128)(2,1)S(1)}, u32[]{:S(2)}, u32[]{:S(2)}) collective-permute-start(bf16[8,80,128]{2,1,0:T(8,128)(2,1)S(1)} %get-tuple-element.24), channel_id=1, source_target_pairs={{0,1},{1,2},{2,3},{3,0},{4,5},{5,6},{6,7},{7,4},{8,9},{9,10},{10,1... | collective-permute-start | bytes 491528 | tf_op jit(solution)/shard_map/ppermute | solution.py:344
  7.8 0.1 copy.45
  7.9 0.1 reshape.177
  8.1 0.1 copy.48
  8.2 0.8 reshape.178.w1_ref
  9.0 0.1 copy.49
  9.2 0.8 reshape.179.w2_ref
  10.0 0.7 copy.50.b1_ref
  10.7 0.7 copy.51.b2_ref
  11.4 0.1 copy.52
  11.5 0.1 broadcast_in_dim.63
  11.6 0.2 convert_reduce_fusion
  11.9 5.1 %collective-permute-start.3 = (bf16[2,80,1152]{2,1,0:T(8,128)(2,1)S(1)}, bf16[2,80,1152]{2,1,0:T(8,128)(2,1)S(1)}, u32[]{:S(2)}, u32[]{:S(2)}) collective-permute-start(bf16[2,80,1152]{2,1,0:T(8,128)(2,1)S(1)} %pad_maximum_fusion.1), channel_id=1, source_target_pairs={{4,0},{8,4},{12,8},{16,12},{20,16},{24,20},{28,24},{32,28},{36,32}... | collective-permute-start | bytes 1105928 | tf_op jit(solution)/shard_map/ppermute | solution.py:350
  17.0 1.9 %collective-permute-start.2 = (bf16[2,80,1152]{2,1,0:T(8,128)(2,1)S(1)}, bf16[2,80,1152]{2,1,0:T(8,128)(2,1)S(1)}, u32[]{:S(2)}, u32[]{:S(2)}) collective-permute-start(bf16[2,80,1152]{2,1,0:T(8,128)(2,1)S(1)} %pad_maximum_fusion), channel_id=1, source_target_pairs={{0,4},{4,8},{8,12},{12,16},{16,20},{20,24},{24,28},{28,32},{32,36}... | collective-permute-start | bytes 1105928 | tf_op jit(solution)/shard_map/ppermute | solution.py:344
  19.0 0.1 select_reduce_fusion
  19.2 1.6 copy.61
  20.9 0.6 pad.9.rows
  21.5 1.4 collective-permute-done.3.bottom_ref
  22.9 6.9 %collective-permute-done.2.top_ref = bf16[2,80,1152]{2,1,0:T(8,128)(2,1)S(1)} collective-permute-done((bf16[2,80,1152]{2,1,0:T(8,128)(2,1)S(1)}, bf16[2,80,1152]{2,1,0:T(8,128)(2,1)S(1)}, u32[]{:S(2)}, u32[]{:S(2)}) %collective-permute-start.2) | collective-permute-done | bytes 368672 | tf_op jit(solution)/shard_map/ppermute | solution.py:344
  29.8 0.7 copy-done.5
  30.6 14.1 %ocean.1 = (bf16[8,64,1024]{2,1,0:T(8,128)(2,1)}, bf16[384,64,128]{2,1,0:T(8,128)(2,1)}) custom-call(s32[128]{0:T(128)} %copy-done.11, bf16[8,80,1024]{2,1,0:T(8,128)(2,1)} %copy-done, bf16[8,80,128]{2,1,0:T(8,128)(2,1)} %copy-done.3, bf16[2,80,1152]{2,1,0:T(8,128)(2,1)} %copy-done.5, bf16[2,80,1152]{2,1,0:T(8,128)(2,1)} %copy-done.4, ...), custom_call_target="tpu_custom_call" | custom-call | tf_op jit(solution)/shard_map/ocean/pallas_call | solution.py:98
  44.7 89.0 %exchange.1 = (bf16[12,32,64,128]{3,2,1,0:T(8,128)(2,1)}, s32[12,8,128]{2,1,0:T(8,128)}) custom-call(bf16[12,32,64,128]{3,2,1,0:T(8,128)(2,1)} %bitcast.22, s32[12,8,128]{2,1,0:T(8,128)} %pad.9.rows), custom_call_target="tpu_custom_call" | custom-call | tf_op jit(solution)/shard_map/exchange/pallas_call | solution.py:208
  133.7 1.1 fusion.1
  134.8 0.6 and_select_fusion.1.counts
  135.4 0.7 reshape_squeeze.3.rows
  136.1 10.0 %merge.1 = (bf16[64,64,128]{2,1,0:T(8,128)(2,1)}, bf16[2,64,128]{2,1,0:T(8,128)(2,1)}) custom-call(s32[384]{0:T(512)} %reshape_squeeze.3.rows, s32[12]{0:T(128)} %and_select_fusion.1.counts, bf16[12,32,64,128]{3,2,1,0:T(8,128)(2,1)} %get-tuple-element.11.data_ref, bf16[64,64,128]{2,1,0:T(8,128)(2,1)} %bitcast.25), custom_call_target="tpu_custom_call" | custom-call | tf_op jit(solution)/shard_map/merge/pallas_call | solution.py:252
  146.1 0.5 collective-permute-start.5
  146.6 0.8 fusion.8
  147.4 0.1 collective-permute-done.4
  147.6 3.7 %collective-permute-done.5 = bf16[2,64,128]{2,1,0:T(8,128)(2,1)S(1)} collective-permute-done((bf16[2,64,128]{2,1,0:T(8,128)(2,1)}, bf16[2,64,128]{2,1,0:T(8,128)(2,1)S(1)}, u32[]{:S(2)}, u32[]{:S(2)}) %collective-permute-start.5) | collective-permute-done | bytes 32800 | tf_op jit(solution)/shard_map/ppermute | solution.py:350
  151.3 2.9 %collective-permute-start.7 = (bf16[3,64,128]{2,1,0:T(8,128)(2,1)S(1)}, bf16[3,64,128]{2,1,0:T(8,128)(2,1)S(1)}, u32[]{:S(2)}, u32[]{:S(2)}) collective-permute-start(bf16[3,64,128]{2,1,0:T(8,128)(2,1)S(1)} %pad_maximum_fusion.4), channel_id=1, source_target_pairs={{4,0},{8,4},{12,8},{16,12},{20,16},{24,20},{28,24},{32,28},{36,32}... | collective-permute-start | bytes 147464 | tf_op jit(solution)/shard_map/ppermute | solution.py:350
  154.2 2.4 %collective-permute-start.6 = (bf16[3,64,128]{2,1,0:T(8,128)(2,1)S(1)}, bf16[3,64,128]{2,1,0:T(8,128)(2,1)S(1)}, u32[]{:S(2)}, u32[]{:S(2)}) collective-permute-start(bf16[3,64,128]{2,1,0:T(8,128)(2,1)S(1)} %pad_maximum_fusion.3), channel_id=1, source_target_pairs={{0,4},{4,8},{8,12},{12,16},{16,20},{20,24},{24,28},{28,32},{32,36}... | collective-permute-start | bytes 147464 | tf_op jit(solution)/shard_map/ppermute | solution.py:344
  156.6 0.6 add_convert_fusion.inside
  157.2 0.1 copy.54
  157.4 0.8 reshape.183.w1_ref
  158.2 0.1 copy.55
  158.3 0.8 reshape.184.w2_ref
  159.1 0.7 copy.56.b1_ref
  159.8 0.7 copy.57.b2_ref
  160.5 1.5 copy.58
  162.1 0.6 pad_maximum_fusion.2.side_ref
  162.7 0.6 slice.69.bottom_ref
  163.3 0.6 slice.67.top_ref
  163.9 22.4 %atmos.1 = bf16[64,64,128]{2,1,0:T(8,128)(2,1)} custom-call(s32[2]{0:T(128)} %add_convert_fusion.inside, bf16[64,64,128]{2,1,0:T(8,128)(2,1)} %get-tuple-element.12.a_ref, bf16[2,64,128]{2,1,0:T(8,128)(2,1)} %slice.67.top_ref, bf16[2,64,128]{2,1,0:T(8,128)(2,1)} %slice.69.bottom_ref, bf16[4,64,128]{2,1,0:T(8,128)(2,1)} %pad_maximum_fusion.2.side_ref, ...), custom_call_target="tpu_custom_call" | custom-call | tf_op jit(solution)/shard_map/atmos/pallas_call | solution.py:327
  186.3 2.9 %copy.59 = bf16[64,64,128]{2,1,0:T(8,128)(2,1)} copy(bf16[64,64,128]{2,0,1:T(8,128)(2,1)} %bitcast.24) | data formatting | bytes 2097152
  (62 shorter events, 0.7 us)
Async XLA Ops:
  0.6 2.0 %copy-start.10 = (s32[8,1024]{1,0:T(8,128)S(1)}, s32[8,1024]{1,0:T(8,128)}, u32[]{:S(2)}) copy-start(s32[8,1024]{1,0:T(8,128)} %param.15) | copy-start | bytes 98308
  3.3 5.0 %copy-start = (bf16[8,80,1024]{2,1,0:T(8,128)(2,1)}, bf16[8,80,1024]{2,1,0:T(8,128)(2,1)S(1)}, u32[]{:S(2)}) copy-start(bf16[8,80,1024]{2,1,0:T(8,128)(2,1)S(1)} %maximum_bitcast_fusion.x_ref) | copy-start | bytes 3932164
  3.3 4.5 %copy-start.12 = (s32[64,2]{0,1:T(2,128)S(1)}, s32[64,2]{0,1:T(2,128)}, u32[]{:S(2)}) copy-start(s32[64,2]{0,1:T(2,128)} %param.21) | copy-start | bytes 1540
  3.3 4.7 %copy-start.6 = (bf16[64,76,3,3]{1,0,3,2:T(8,128)(2,1)S(1)}, bf16[64,76,3,3]{1,0,3,2:T(8,128)(2,1)}, u32[]{:S(2)}) copy-start(bf16[64,76,3,3]{1,0,3,2:T(8,128)(2,1)} %param.16) | copy-start | bytes 262660
  3.4 5.7 %copy-start.7 = (bf16[64,64,3,3]{1,0,3,2:T(8,128)(2,1)S(1)}, bf16[64,64,3,3]{1,0,3,2:T(8,128)(2,1)}, u32[]{:S(2)}) copy-start(bf16[64,64,3,3]{1,0,3,2:T(8,128)(2,1)} %param.18) | copy-start | bytes 221188
  3.4 8.4 %collective-permute-start = (bf16[8,80,128]{2,1,0:T(8,128)(2,1)S(1)}, bf16[8,80,128]{2,1,0:T(8,128)(2,1)S(1)}, u32[]{:S(2)}, u32[]{:S(2)}) collective-permute-start(bf16[8,80,128]{2,1,0:T(8,128)(2,1)S(1)} %get-tuple-element.25), channel_id=1, source_target_pairs={{1,0},{2,1},{3,2},{0,3},{5,4},{6,5},{7,6},{4,7},{9,8},{10,9},{11,1... | collective-permute-start | bytes 491528 | tf_op jit(solution)/shard_map/ppermute | solution.py:350
  4.1 5.8 %copy-start.14 = (f32[64]{0:T(128)S(1)}, f32[64]{0:T(128)}, u32[]{:S(2)}) copy-start(f32[64]{0:T(128)} %param.17) | copy-start | bytes 772
  4.1 6.5 %copy-start.15 = (f32[64]{0:T(128)S(1)}, f32[64]{0:T(128)}, u32[]{:S(2)}) copy-start(f32[64]{0:T(128)} %param.19) | copy-start | bytes 772
  4.1 7.2 %copy-start.13 = (s32[64,2]{0,1:T(2,128)S(1)}, s32[64,2]{0,1:T(2,128)}, u32[]{:S(2)}) copy-start(s32[64,2]{0,1:T(2,128)} %param.22) | copy-start | bytes 1540
  4.1 7.7 %collective-permute-start.1 = (bf16[8,80,128]{2,1,0:T(8,128)(2,1)S(1)}, bf16[8,80,128]{2,1,0:T(8,128)(2,1)S(1)}, u32[]{:S(2)}, u32[]{:S(2)}) collective-permute-start(bf16[8,80,128]{2,1,0:T(8,128)(2,1)S(1)} %get-tuple-element.24), channel_id=1, source_target_pairs={{0,1},{1,2},{2,3},{3,0},{4,5},{5,6},{6,7},{7,4},{8,9},{9,10},{10,1... | collective-permute-start | bytes 491528 | tf_op jit(solution)/shard_map/ppermute | solution.py:344
  9.2 10.0 %copy-start.1 = (bf16[64,64,128]{2,1,0:T(8,128)(2,1)S(1)}, bf16[64,64,128]{2,1,0:T(8,128)(2,1)}, u32[]{:S(2)}) copy-start(bf16[64,64,128]{2,1,0:T(8,128)(2,1)} %param.23) | copy-start | bytes 3145732
  11.8 9.0 %copy-start.3 = (bf16[8,80,128]{2,1,0:T(8,128)(2,1)}, bf16[8,80,128]{2,1,0:T(8,128)(2,1)S(1)}, u32[]{:S(2)}) copy-start(bf16[8,80,128]{2,1,0:T(8,128)(2,1)S(1)} %broadcast_select_fusion.side_ref) | copy-start | bytes 491524
  11.9 11.0 %collective-permute-start.3 = (bf16[2,80,1152]{2,1,0:T(8,128)(2,1)S(1)}, bf16[2,80,1152]{2,1,0:T(8,128)(2,1)S(1)}, u32[]{:S(2)}, u32[]{:S(2)}) collective-permute-start(bf16[2,80,1152]{2,1,0:T(8,128)(2,1)S(1)} %pad_maximum_fusion.1), channel_id=1, source_target_pairs={{4,0},{8,4},{12,8},{16,12},{20,16},{24,20},{28,24},{32,28},{36,32}... | collective-permute-start | bytes 1105928 | tf_op jit(solution)/shard_map/ppermute | solution.py:350
  17.0 12.8 %collective-permute-start.2 = (bf16[2,80,1152]{2,1,0:T(8,128)(2,1)S(1)}, bf16[2,80,1152]{2,1,0:T(8,128)(2,1)S(1)}, u32[]{:S(2)}, u32[]{:S(2)}) collective-permute-start(bf16[2,80,1152]{2,1,0:T(8,128)(2,1)S(1)} %pad_maximum_fusion), channel_id=1, source_target_pairs={{0,4},{4,8},{8,12},{12,16},{16,20},{20,24},{24,28},{28,32},{32,36}... | collective-permute-start | bytes 1105928 | tf_op jit(solution)/shard_map/ppermute | solution.py:344
  19.0 10.9 %copy-start.11 = (s32[128]{0:T(128)}, s32[128]{0:T(128)S(1)}, u32[]{:S(2)}) copy-start(s32[128]{0:T(128)S(1)} %multiply_add_fusion.place) | copy-start | bytes 1540
  22.9 6.9 %copy-start.4 = (bf16[2,80,1152]{2,1,0:T(8,128)(2,1)}, bf16[2,80,1152]{2,1,0:T(8,128)(2,1)S(1)}, u32[]{:S(2)}) copy-start(bf16[2,80,1152]{2,1,0:T(8,128)(2,1)S(1)} %collective-permute-done.3.bottom_ref) | copy-start | bytes 1105924
  29.8 0.8 copy-start.5
  136.1 21.2 %copy-start.8 = (bf16[64,64,3,3]{1,0,3,2:T(8,128)(2,1)S(1)}, bf16[64,64,3,3]{1,0,3,2:T(8,128)(2,1)}, u32[]{:S(2)}) copy-start(bf16[64,64,3,3]{1,0,3,2:T(8,128)(2,1)} %param.24) | copy-start | bytes 221188
  136.1 22.1 %copy-start.9 = (bf16[64,64,3,3]{1,0,3,2:T(8,128)(2,1)S(1)}, bf16[64,64,3,3]{1,0,3,2:T(8,128)(2,1)}, u32[]{:S(2)}) copy-start(bf16[64,64,3,3]{1,0,3,2:T(8,128)(2,1)} %param.26) | copy-start | bytes 221188
  146.1 13.0 %copy-start.16 = (f32[64]{0:T(128)S(1)}, f32[64]{0:T(128)}, u32[]{:S(2)}) copy-start(f32[64]{0:T(128)} %param.25) | copy-start | bytes 772
  146.1 13.7 %copy-start.17 = (f32[64]{0:T(128)S(1)}, f32[64]{0:T(128)}, u32[]{:S(2)}) copy-start(f32[64]{0:T(128)} %param.27) | copy-start | bytes 772
  146.1 14.4 %copy-start.2 = (bf16[8,64,1024]{2,1,0:T(8,128)(2,1)S(1)}, bf16[8,64,1024]{2,1,0:T(8,128)(2,1)}, u32[]{:S(2)}) copy-start(bf16[8,64,1024]{2,1,0:T(8,128)(2,1)} %get-tuple-element.8) | copy-start | bytes 3145732
  146.1 1.5 collective-permute-start.4
  146.1 5.1 %collective-permute-start.5 = (bf16[2,64,128]{2,1,0:T(8,128)(2,1)}, bf16[2,64,128]{2,1,0:T(8,128)(2,1)S(1)}, u32[]{:S(2)}, u32[]{:S(2)}) collective-permute-start(bf16[2,64,128]{2,1,0:T(8,128)(2,1)} %get-tuple-element.13), channel_id=1, source_target_pairs={{1,0},{2,1},{3,2},{0,3},{5,4},{6,5},{7,6},{4,7},{9,8},{10,9},{11,1... | collective-permute-start | bytes 98312 | tf_op jit(solution)/shard_map/ppermute | solution.py:350
  151.3 10.7 %collective-permute-start.7 = (bf16[3,64,128]{2,1,0:T(8,128)(2,1)S(1)}, bf16[3,64,128]{2,1,0:T(8,128)(2,1)S(1)}, u32[]{:S(2)}, u32[]{:S(2)}) collective-permute-start(bf16[3,64,128]{2,1,0:T(8,128)(2,1)S(1)} %pad_maximum_fusion.4), channel_id=1, source_target_pairs={{4,0},{8,4},{12,8},{16,12},{20,16},{24,20},{28,24},{32,28},{36,32}... | collective-permute-start | bytes 147464 | tf_op jit(solution)/shard_map/ppermute | solution.py:350
  154.2 7.9 %collective-permute-start.6 = (bf16[3,64,128]{2,1,0:T(8,128)(2,1)S(1)}, bf16[3,64,128]{2,1,0:T(8,128)(2,1)S(1)}, u32[]{:S(2)}, u32[]{:S(2)}) collective-permute-start(bf16[3,64,128]{2,1,0:T(8,128)(2,1)S(1)} %pad_maximum_fusion.3), channel_id=1, source_target_pairs={{0,4},{4,8},{8,12},{12,16},{16,20},{20,24},{24,28},{28,32},{32,36}... | collective-permute-start | bytes 147464 | tf_op jit(solution)/shard_map/ppermute | solution.py:344
where the time goes:
time: 191 us; the launch traced here: 189 us
  Pallas kernels  136 us (71%)
  local copies, waits for them, and re-layouts  19.4 us (10%)
  starting transfers between devices  17.2 us (9%)
  waiting for transfers between devices  12.2 us (6%)
  other arithmetic  3.9 us (2%)
    pallas_call x1, Pallas kernels, exchange(): pl.pallas_call(functools.partial(exchange_kernel, lat_count, lon_count),...  89 us
    pallas_call x1, Pallas kernels, atmos_step(): pl.pallas_call(atmos_kernel, out_shape=jax.ShapeDtypeStruct(a.shape, BF16...  22.4 us
    pallas_call x1, Pallas kernels, ocean_step(): pl.pallas_call(ocean_kernel, out_shape=(jax.ShapeDtypeStruct((rows, out,...  14.1 us
    pallas_call x1, Pallas kernels, merge(): pl.pallas_call(merge_kernel, out_shape=(jax.ShapeDtypeStruct(atmos.shape,...  9.98 us
    ppermute x4, starting transfers between devices, from_right(): return lax.ppermute(value, axis, pairs)  9.18 us
    unnamed x42, local copies, waits for them, and re-layouts  9.07 us
    ppermute x4, starting transfers between devices, from_left(): return lax.ppermute(value, axis, pairs)  8 us
    ppermute x4, waiting for transfers between devices, from_left(): return lax.ppermute(value, axis, pairs)  7.01 us
  transfers between devices with their start and end apart: 8, of which 4 were waited for; matrix products, arithmetic and copies ran while one was open for 7% of the time, Pallas kernels for 0%

commit v1 on v0

v1 whole, which is shorter than its diff:
```python
import functools

import jax
import jax.numpy as jnp
from jax import lax
from jax.experimental import pallas as pl
from jax.experimental.pallas import tpu as pltpu
from jax.sharding import PartitionSpec as P

MESH = pl.DeviceIdType.MESH
F32 = jnp.float32
BF16 = jnp.bfloat16
VMEM_LIMIT = 56 * 1024 * 1024


def silu(v):
    return 0.5 * v * (1.0 + jnp.tanh(0.5 * v))


def shifted_sum(taps):
    out = taps.shape[0] // 3
    columns = taps.shape[1]
    return (
        pltpu.roll(taps[0:out], 1, 1)
        + taps[out : 2 * out]
        + pltpu.roll(taps[2 * out :], columns - 1, 1)
    )


def stacked_weight(weight, padded_in):
    out, inn = weight.shape[:2]
    weight = jnp.pad(weight, ((0, 0), (0, padded_in - inn), (0, 0), (0, 0)))
    return weight.transpose(3, 0, 2, 1).reshape(3 * out, 3 * padded_in)


def column(bias):
    n = bias.shape[1]
    at = lax.broadcasted_iota(jnp.int32, (n, n), 0) == lax.broadcasted_iota(jnp.int32, (n, n), 1)
    return jnp.sum(jnp.where(at, bias, 0.0), axis=1, keepdims=True)


def remote(src, dst, send_sem, recv_sem, lat, lon):
    return pltpu.make_async_remote_copy(
        src_ref=src,
        dst_ref=dst,
        send_sem=send_sem,
        recv_sem=recv_sem,
        device_id={"lat": lat, "lon": lon},
        device_id_type=MESH,
    )


def landed(ref, sem):
    return pltpu.make_async_copy(ref, ref, sem)


def greet(partners, waits):
    barrier = pltpu.get_barrier_semaphore()
    for lat, lon, ok in partners:

        @pl.when(ok)
        def _():
            pl.semaphore_signal(
                barrier, inc=1, device_id={"lat": lat, "lon": lon}, device_id_type=MESH
            )

    pl.semaphore_wait(barrier, waits)


def whole_any(count):
    return [pl.BlockSpec(memory_space=pl.ANY)] * count


def ocean_halo_kernel(
    lat_count, lon_count, field, top, bottom, left, right, send_sem, recv_sem
):
    lat, lon = lax.axis_index("lat"), lax.axis_index("lon")
    rows, _, cols = field.shape
    west = lax.rem(lon + lon_count - 1, lon_count)
    east = lax.rem(lon + 1, lon_count)
    up, down, always = lat > 0, lat < lat_count - 1, lat >= 0
    edge = jnp.logical_or(lat == 0, lat == lat_count - 1)
    partners = [(lat, west, always), (lat, east, always)]
    for there, ok in ((lat - 1, up), (lat + 1, down)):
        partners += [(there, side, ok) for side in (west, lon, east)]
    greet(partners, jnp.where(edge, 5, 8))

    lo, hi = pl.ds(0, 128), pl.ds(cols - 128, 128)
    first, last = pl.ds(0, 2), pl.ds(rows - 2, 2)
    own, above, below = pl.ds(2, rows), pl.ds(0, 2), pl.ds(rows + 2, 2)
    moves = [
        (field.at[:, :, lo], right.at[own], lat, west, always),
        (field.at[:, :, hi], left.at[own], lat, east, always),
        (field.at[first], bottom, lat - 1, lon, up),
        (field.at[last], top, lat + 1, lon, down),
        (field.at[first, :, lo], right.at[below], lat - 1, west, up),
        (field.at[first, :, hi], left.at[below], lat - 1, east, up),
        (field.at[last, :, lo], right.at[above], lat + 1, west, down),
        (field.at[last, :, hi], left.at[above], lat + 1, east, down),
    ]
    arrives = [always, always, down, up, down, down, up, up]
    copies = [
        (remote(src, dst, send_sem.at[i], recv_sem.at[i], a, b), ok)
        for i, (src, dst, a, b, ok) in enumerate(moves)
    ]
    for copy, ok in copies:
        pl.when(ok)(copy.start)
    for i, (copy, ok) in enumerate(copies):
        pl.when(ok)(copy.wait_send)
        pl.when(arrives[i])(landed(moves[i][1], recv_sem.at[i]).wait)


def ocean_halo(field, lat_count, lon_count):
    rows, channels, cols = field.shape
    shapes = [(2, channels, cols)] * 2 + [(rows + 4, channels, 128)] * 2
    return pl.pallas_call(
        functools.partial(ocean_halo_kernel, lat_count, lon_count),
        out_shape=[jax.ShapeDtypeStruct(s, BF16) for s in shapes],
        in_specs=whole_any(1),
        out_specs=whole_any(4),
        scratch_shapes=[pltpu.SemaphoreType.DMA((8,))] * 2,
        compiler_params=pltpu.CompilerParams(collective_id=0, has_side_effects=True),
        name="ocean_halo",
    )(field)


def ocean_kernel(
    lat_count,
    meta,
    x_ref,
    top_ref,
    bottom_ref,
    left_ref,
    right_ref,
    w1_ref,
    b1_ref,
    w2_ref,
    b2_ref,
    regrid_ref,
    next_ref,
    lists,
    codes,
    tall,
    hidden,
    contrib,
    filled,
    sem,
):
    row = lax.rem(pl.program_id(0), 16)
    rows, channels, cols = x_ref.shape
    mask_at = 76
    b1, b2 = column(b1_ref[...]), column(b2_ref[...])

    def first_conv(j):
        field = jnp.concatenate([tall[j], tall[j + 1], tall[j + 2]], axis=0)
        taps = jnp.dot(w1_ref[...], field, preferred_element_type=F32)
        mask = tall[j + 1, mask_at : mask_at + 1, :].astype(F32)
        hidden[j] = (silu(shifted_sum(taps) + b1) * mask).astype(BF16)

    @pl.when(row == 0)
    def _():
        lat = lax.axis_index("lat")
        lane = lax.broadcasted_iota(jnp.int32, (channels, 128), 1)
        tall[2 : 2 + rows, :, 0:cols] = x_ref[...]
        for j in range(rows + 4):
            side = jnp.where(lane < 64, right_ref[j], left_ref[j])
            if j < 2 or j >= rows + 2:
                inside = lat > 0 if j < 2 else lat < lat_count - 1
                main = top_ref[j] if j < 2 else bottom_ref[j - rows - 2]
                tall[j, :, 0:cols] = jnp.where(inside, main, jnp.zeros_like(main))
                side = jnp.where(inside, side, jnp.zeros_like(side))
            tall[j, :, cols:] = side
        for i in range(3):
            filled[i] = 0
        first_conv(0)
        first_conv(1)

    first_conv(lax.rem(row + 2, 16))
    field = jnp.concatenate([hidden[row], hidden[row + 1], hidden[row + 2]], axis=0)
    taps = jnp.dot(w2_ref[...], field, preferred_element_type=F32)
    mask = tall[row + 2, mask_at : mask_at + 1, :].astype(F32)
    result = ((shifted_sum(taps) + b2) * mask).astype(BF16)[:, :cols]
    next_ref[0] = result
    blocks = regrid_ref.shape[0]
    capacity = lists.shape[1]
    for q in range(blocks):
        field = result[:, q * 128 : (q + 1) * 128]
        both = lax.dot_general(
            field, regrid_ref[q], (((1,), (1,)), ((), ())), preferred_element_type=F32
        ).astype(BF16)
        for k in range(2):
            i = (row * blocks + q) * 2 + k
            contrib[i] = both[:, k * 128 : (k + 1) * 128]
            which = meta[i] // 256
            at = filled[which]
            filled[which] = at + 1
            codes[which, 0, at] = lax.rem(meta[i], 256)
            pltpu.make_async_copy(contrib.at[i], lists.at[which, at], sem).start()

    @pl.when(row == rows - 1)
    def _():
        for i in range(3):
            codes[i, 1, 0] = filled[i]
        pltpu.make_async_copy(contrib, contrib, sem).wait()


def ocean_step(meta, x, top, bottom, left, right, w1, b1, w2, b2, regrid, lat_count):
    rows, channels, cols = x.shape
    wide = cols + 128
    out = w2.shape[0] // 3
    slots = meta.shape[0]

    def whole(array):
        zeros = (0,) * array.ndim
        return pl.BlockSpec(array.shape, lambda r, meta: zeros)

    blocks = regrid.shape[0] // rows
    return pl.pallas_call(
        functools.partial(ocean_kernel, lat_count),
        out_shape=(
            jax.ShapeDtypeStruct((rows, out, cols), BF16),
            jax.ShapeDtypeStruct((3, slots, out, 128), BF16),
            jax.ShapeDtypeStruct((3, 8, 128), jnp.int32),
        ),
        grid_spec=pltpu.PrefetchScalarGridSpec(
            num_scalar_prefetch=1,
            grid=(rows,),
            in_specs=[whole(a) for a in (x, top, bottom, left, right, w1, b1, w2, b2)]
            + [pl.BlockSpec((blocks, 256, 128), lambda r, meta: (r, 0, 0))],
            out_specs=[
                pl.BlockSpec((1, out, cols), lambda r, meta: (r, 0, 0)),
                pl.BlockSpec(memory_space=pl.ANY),
                pl.BlockSpec(memory_space=pltpu.SMEM),
            ],
            scratch_shapes=[
                pltpu.VMEM((rows + 4, channels, wide), BF16),
                pltpu.VMEM((rows + 2, out, wide), BF16),
                pltpu.VMEM((slots, out, 128), BF16),
                pltpu.SMEM((3,), jnp.int32),
                pltpu.SemaphoreType.DMA,
            ],
        ),
        compiler_params=pltpu.CompilerParams(vmem_limit_bytes=VMEM_LIMIT),
        name="ocean",
    )(meta, x, top, bottom, left, right, w1, b1, w2, b2, regrid)


def lists_kernel(lat_count, count, lists, codes, north, north_codes, south, south_codes, send, recv):
    lat, lon = lax.axis_index("lat"), lax.axis_index("lon")
    up, down = lat > 0, lat < lat_count - 1
    greet([(lat - 1, lon, up), (lat + 1, lon, down)], jnp.where(jnp.logical_and(up, down), 2, 1))
    some = pl.ds(0, count)
    moves = [
        (lists.at[0, some], south.at[some], lat - 1, up, down),
        (codes.at[0], south_codes, lat - 1, up, down),
        (lists.at[2, some], north.at[some], lat + 1, down, up),
        (codes.at[2], north_codes, lat + 1, down, up),
    ]
    copies = [
        remote(src, dst, send.at[i], recv.at[i], there, lon)
        for i, (src, dst, there, _, _) in enumerate(moves)
    ]
    for copy, move in zip(copies, moves):
        pl.when(move[3])(copy.start)
    for i, (copy, move) in enumerate(zip(copies, moves)):
        pl.when(move[3])(copy.wait_send)
        pl.when(move[4])(landed(move[1], recv.at[i]).wait)


def send_lists(lists, codes, count, collective_id, lat_count):
    one = jax.ShapeDtypeStruct(lists.shape[1:], BF16)
    code = jax.ShapeDtypeStruct(codes.shape[1:], jnp.int32)
    return pl.pallas_call(
        functools.partial(lists_kernel, lat_count, count),
        out_shape=[one, code, one, code],
        in_specs=whole_any(2),
        out_specs=whole_any(4),
        scratch_shapes=[pltpu.SemaphoreType.DMA((4,))] * 2,
        compiler_params=pltpu.CompilerParams(collective_id=collective_id, has_side_effects=True),
        name="send_lists",
    )(lists, codes)


PIECE = 16


def merge_kernel(
    lat_count, own_codes, north_codes, south_codes, lists, north, south, out, slots, total, packed, sem, out_sem
):
    lat = lax.axis_index("lat")
    own_count = own_codes[1, 1, 0]
    north_count = jnp.where(lat > 0, north_codes[1, 0], 0)
    south_count = jnp.where(lat < lat_count - 1, south_codes[1, 0], 0)
    capacity = slots.shape[1]
    sources = (
        (lists.at[1], lambda s: own_codes[1, 0, s], own_count),
        (north, lambda s: north_codes[0, s], north_count),
        (south, lambda s: south_codes[0, s], south_count),
    )

    def pieces(i, action):
        for p in range(capacity // PIECE):
            some = pl.ds(p * PIECE, PIECE)
            copy = pltpu.make_async_copy(sources[i][0].at[some], slots.at[i, some], sem.at[i, p])
            pl.when(sources[i][2] > p * PIECE)(getattr(copy, action))

    for i in range(3):
        pieces(i, "start")
    total[...] = jnp.zeros_like(total)
    for i in range(3):
        pieces(i, "wait")
        _, code, count = sources[i]

        def add(s, carry):
            r = code(s)
            total[r] = total[r] + slots[i, s].astype(F32)
            return carry

        lax.fori_loop(0, count, add, 0)
    parts, rows = out.shape[:2]
    copies = []
    for e in range(parts):
        packed[e] = total[e * rows : (e + 1) * rows].astype(BF16)
        copies.append(pltpu.make_async_copy(packed.at[e], out.at[e], out_sem.at[e]))
        copies[-1].start()
    for copy in copies:
        copy.wait()


def merge(codes, lists, north, north_codes, south, south_codes, lat_count, lon_count, rows):
    slots, channels, cols = lists.shape[1:]
    smem = pl.BlockSpec(memory_space=pltpu.SMEM)
    shape = (lon_count, rows, channels, cols)
    return pl.pallas_call(
        functools.partial(merge_kernel, lat_count),
        out_shape=jax.ShapeDtypeStruct(shape, BF16),
        in_specs=[smem] * 3 + whole_any(3),
        out_specs=pl.BlockSpec(memory_space=pl.ANY),
        scratch_shapes=[
            pltpu.VMEM((3, slots, channels, cols), BF16),
            pltpu.VMEM((lon_count * rows, channels, cols), F32),
            pltpu.VMEM(shape, BF16),
            pltpu.SemaphoreType.DMA((3, slots // PIECE)),
            pltpu.SemaphoreType.DMA((lon_count,)),
        ],
        compiler_params=pltpu.CompilerParams(vmem_limit_bytes=VMEM_LIMIT),
        name="merge",
    )(codes, north_codes, south_codes, lists, north, south)


def gather_kernel(
    lat_count,
    lon_count,
    dense,
    atmos,
    first,
    top,
    bottom,
    left,
    right,
    mine,
    from_core,
    to_z,
    from_z,
    edges,
    load_sem,
    core_send,
    core_recv,
    z_send,
    z_recv,
    halo_send,
    halo_recv,
):
    lat, lon = lax.axis_index("lat"), lax.axis_index("lon")
    west = lax.rem(lon + lon_count - 1, lon_count)
    east = lax.rem(lon + 1, lon_count)
    across = lax.rem(lon + 2, lon_count)
    core = lax.rem(lon, 2)
    beside = lon + 1 - 2 * core
    beside_across = lax.rem(beside + 2, lon_count)
    up, down, always = lat > 0, lat < lat_count - 1, lat >= 0
    edge = jnp.logical_or(lat == 0, lat == lat_count - 1)
    partners = [(lat, there, always) for there in (west, east, across)]
    for there, ok in ((lat - 1, up), (lat + 1, down)):
        partners += [(there, side, ok) for side in (west, lon, east)]
    greet(partners, jnp.where(edge, 6, 9))

    rows, channels, cols = first.shape
    chunks = to_z.shape[0] // 16
    some = [pl.ds(c * 16, 16) for c in range(chunks)]
    core_copies, loads = [], []
    for part, (theirs, ours) in enumerate(((beside_across, across), (beside, lon))):
        for c in range(chunks):
            core_copies.append(
                remote(
                    dense.at[theirs, some[c]],
                    from_core.at[part, some[c]],
                    core_send.at[part, c],
                    core_recv.at[part, c],
                    lat,
                    beside,
                )
            )
            loads.append(
                pltpu.make_async_copy(
                    dense.at[ours, some[c]], mine.at[part, some[c]], load_sem.at[part, c]
                )
            )
    for a, b in zip(core_copies, loads):
        a.start()
        b.start()
    z_copies = []
    for c in range(chunks):
        loads[c].wait()
        landed(from_core.at[0, some[c]], core_recv.at[0, c]).wait()
        to_z[some[c]] = (
            mine[0, some[c]].astype(F32) + from_core[0, some[c]].astype(F32)
        ).astype(BF16)
        z_copies.append(
            remote(to_z.at[some[c]], from_z.at[some[c]], z_send.at[c], z_recv.at[c], lat, across)
        )
        z_copies[c].start()
    for c in range(chunks):
        loads[chunks + c].wait()
        landed(from_core.at[1, some[c]], core_recv.at[1, c]).wait()
    lane = lax.broadcasted_iota(jnp.int32, (channels, cols), 1)
    for c in range(chunks):
        landed(from_z.at[some[c]], z_recv.at[c]).wait()
        tile = c * 16 // 32
        part = jnp.zeros((channels, cols), F32) if c % 2 == 0 else part
        for k in range(16):
            r = c * 16 + k
            flux = mine[1, r].astype(F32) + from_core[1, r].astype(F32) + from_z[r].astype(F32)
            v = (atmos[r].astype(F32) + flux).astype(BF16)
            first[r] = v
            at = r % 32
            part = jnp.where(
                lane // 4 == at, pltpu.roll(v.astype(F32), (4 * at + 2) % cols, 1), part
            )
        if c % 2 == 1:
            edges[tile] = part.astype(BF16)
    tiles = edges.shape[0]
    lo, hi = edges.at[0], edges.at[tiles - 1]
    moves = [
        (edges, right.at[pl.ds(1, tiles)], lat, west, always, always),
        (edges, left.at[pl.ds(1, tiles)], lat, east, always, always),
        (first.at[pl.ds(0, 2)], bottom, lat - 1, lon, up, down),
        (first.at[pl.ds(rows - 2, 2)], top, lat + 1, lon, down, up),
        (lo, right.at[tiles + 1], lat - 1, west, up, down),
        (lo, left.at[tiles + 1], lat - 1, east, up, down),
        (hi, right.at[0], lat + 1, west, down, up),
        (hi, left.at[0], lat + 1, east, down, up),
    ]
    copies = [
        remote(src, dst, halo_send.at[i], halo_recv.at[i], a, b)
        for i, (src, dst, a, b, _, _) in enumerate(moves)
    ]
    for copy, move in zip(copies, moves):
        pl.when(move[4])(copy.start)
    for copy in core_copies + z_copies:
        copy.wait_send()
    for i, (copy, move) in enumerate(zip(copies, moves)):
        pl.when(move[4])(copy.wait_send)
        pl.when(move[5])(landed(move[1], halo_recv.at[i]).wait)


def gather(dense, atmos, lat_count, lon_count):
    rows, channels, cols = atmos.shape
    tiles = rows // 32
    vmem = pl.BlockSpec(memory_space=pltpu.VMEM)
    dma = pltpu.SemaphoreType.DMA
    shapes = [(rows, channels, cols)] + [(2, channels, cols)] * 2 + [(tiles + 2, channels, cols)] * 2
    return pl.pallas_call(
        functools.partial(gather_kernel, lat_count, lon_count),
        out_shape=[jax.ShapeDtypeStruct(s, BF16) for s in shapes],
        in_specs=whole_any(1) + [vmem],
        out_specs=[vmem] + whole_any(4),
        scratch_shapes=[
            pltpu.VMEM((2, rows, channels, cols), BF16),
            pltpu.VMEM((2, rows, channels, cols), BF16),
            pltpu.VMEM((rows, channels, cols), BF16),
            pltpu.VMEM((rows, channels, cols), BF16),
            pltpu.VMEM((tiles, channels, cols), BF16),
            dma((2, rows // 16)),
            dma((2, rows // 16)),
            dma((2, rows // 16)),
            dma((rows // 16,)),
            dma((rows // 16,)),
            dma((8,)),
            dma((8,)),
        ],
        compiler_params=pltpu.CompilerParams(
            collective_id=1, has_side_effects=True, vmem_limit_bytes=VMEM_LIMIT
        ),
        name="gather",
    )(dense, atmos)


def atmos_kernel(
    lat_count, a_ref, top_ref, bottom_ref, left_ref, right_ref, w1_ref, b1_ref, w2_ref, b2_ref, out_ref, tall, second
):
    count, channels, cols = a_ref.shape
    group = 2
    lat = lax.axis_index("lat")
    b1, b2 = column(b1_ref[...]), column(b2_ref[...])

    tall[2 : 2 + count, :, 0:cols] = a_ref[...]
    lane = lax.broadcasted_iota(jnp.int32, (channels, cols), 1)
    for tile in range(count // 32 + 2):
        side = jnp.where(lane % 4 < 2, left_ref[tile], right_ref[tile]).astype(F32)
        for k in range(32):
            r = tile * 32 - 32 + k
            if r < -2 or r >= count + 2:
                continue
            v = pltpu.roll(side, (126 - 4 * k) % cols, 1).astype(BF16)
            if r < 0 or r >= count:
                inside = lat > 0 if r < 0 else lat < lat_count - 1
                main = top_ref[r + 2] if r < 0 else bottom_ref[r - count]
                tall[r + 2, :, 0:cols] = jnp.where(inside, main, jnp.zeros_like(main))
                v = jnp.where(inside, v, jnp.zeros_like(v))
            tall[r + 2, :, cols:] = v

    def conv(source, weight, start):
        fields = [
            jnp.concatenate([source[start + i + d] for d in range(3)], axis=0)
            for i in range(group)
        ]
        return jnp.dot(weight, jnp.concatenate(fields, axis=1), preferred_element_type=F32)

    def first(step, carry):
        start = step * group
        taps = conv(tall, w1_ref[...], start)
        for i in range(group):
            j = start + i
            value = silu(shifted_sum(taps[:, i * 2 * cols : (i + 1) * 2 * cols]) + b1)
            outside = jnp.logical_or(
                jnp.logical_and(j == 0, lat == 0),
                jnp.logical_and(j == count + 1, lat == lat_count - 1),
            )
            second[j] = jnp.where(outside, 0.0, value).astype(BF16)
        return carry

    lax.fori_loop(0, (count + 2) // group, first, 0)

    def last(step, carry):
        start = step * group
        taps = conv(second, w2_ref[...], start)
        for i in range(group):
            j = start + i
            value = shifted_sum(taps[:, i * 2 * cols : (i + 1) * 2 * cols])[:, :cols]
            out_ref[j] = (a_ref[j].astype(F32) + (value + b2)).astype(BF16)
        return carry

    lax.fori_loop(0, count // group, last, 0)


def atmos_step(a, top, bottom, left, right, w1, b1, w2, b2, lat_count):
    count, channels, cols = a.shape
    vmem = pl.BlockSpec(memory_space=pltpu.VMEM)
    return pl.pallas_call(
        functools.partial(atmos_kernel, lat_count),
        out_shape=jax.ShapeDtypeStruct(a.shape, BF16),
        in_specs=[vmem] * 9,
        out_specs=vmem,
        scratch_shapes=[
            pltpu.VMEM((count + 4, channels, 2 * cols), BF16),
            pltpu.VMEM((count + 2, channels, 2 * cols), BF16),
        ],
        compiler_params=pltpu.CompilerParams(vmem_limit_bytes=VMEM_LIMIT),
        name="atmos",
    )(a, top, bottom, left, right, w1, b1, w2, b2)


def per_device(
    ocean_state,
    sea_mask,
    ocean_w1,
    ocean_b1,
    ocean_w2,
    ocean_b2,
    regrid_weight,
    route_dev,
    route_row,
    atmos_state,
    atmos_w1,
    atmos_b1,
    atmos_w2,
    atmos_b2,
):
    lat_count, lon_count = lax.axis_size("lat"), lax.axis_size("lon")
    lat = lax.axis_index("lat")
    atmos_rows = atmos_state.shape[1]

    field = jnp.concatenate(
        [
            ocean_state,
            sea_mask.astype(BF16)[None],
            jnp.zeros((3,) + sea_mask.shape, BF16),
        ],
        axis=0,
    ).transpose(1, 0, 2)
    top, bottom, left, right = ocean_halo(field, lat_count, lon_count)

    meta = (route_dev - (lat - 1) * lon_count) * atmos_rows + route_row

    ocean_next, lists, codes = ocean_step(
        meta.reshape(-1),
        field,
        top,
        bottom,
        left,
        right,
        stacked_weight(ocean_w1, 80),
        ocean_b1[None, :],
        stacked_weight(ocean_w2, 64),
        ocean_b2[None, :],
        regrid_weight.reshape(-1, 256, 128),
        lat_count,
    )
    north, north_codes, south, south_codes = send_lists(
        lists, codes, lists.shape[1], 2, lat_count
    )
    dense = merge(
        codes, lists, north, north_codes, south, south_codes, lat_count, lon_count, atmos_rows
    )
    first, top, bottom, left, right = gather(
        dense, atmos_state.transpose(1, 0, 2), lat_count, lon_count
    )
    atmos_next = atmos_step(
        first,
        top,
        bottom,
        left,
        right,
        stacked_weight(atmos_w1, 64),
        atmos_b1[None, :],
        stacked_weight(atmos_w2, 64),
        atmos_b2[None, :],
        lat_count,
    )
    return ocean_next.transpose(1, 0, 2), atmos_next.transpose(1, 0, 2)


def solution(mesh):
    in_specs = (
        P(None, "lat", "lon"),
        P("lat", "lon"),
        P(),
        P(),
        P(),
        P(),
        P(("lat", "lon"), None, None, None),
        P(("lat", "lon"), None),
        P(("lat", "lon"), None),
        P(None, "lat", "lon"),
        P(),
        P(),
        P(),
        P(),
    )
    out_specs = (P(None, "lat", "lon"), P(None, "lat", "lon"))
    return jax.shard_map(
        per_device, mesh=mesh, in_specs=in_specs, out_specs=out_specs, check_vma=False
    )
```

time: 191 us -> 171 us (0.90)
  starting transfers between devices: 17.2 us -> 0 us
  Pallas kernels: 136 us -> 153 us
  waiting for transfers between devices: 12.2 us -> 0 us
  local copies, waits for them, and re-layouts: 19.4 us -> 13.9 us
    pallas_call x4 -> x6, Pallas kernels: 136 us -> 153 us  [the longest x1 50.3 us: send_lists(): pl.pallas_call(functools.partial(lists_kernel, lat_count, count), out_sha...]
    ppermute x8 -> x0, starting transfers between devices: 17.2 us -> none  [the longest x4 9.18 us: from_right(): return lax.ppermute(value, axis, pairs)]
    ppermute x8 -> x0, waiting for transfers between devices: 12.2 us -> none  [the longest x4 7.01 us: from_left(): return lax.ppermute(value, axis, pairs)]
    broadcast_in_dim x5 -> x0, local copies, waits for them, and re-layouts: 2.92 us -> none  [the longest x1 0.7 us: per_device(): atmos_b2[:, None]]
    slice x9 -> x0, local copies, waits for them, and re-layouts: 2.11 us -> none  [the longest x1 0.78 us: per_device(): first[:2]]
    unnamed x42 -> x14, local copies, waits for them, and re-layouts: 9.07 us -> 9.3 us
  transfers between devices with their start and end apart: 8 -> 0, of which waited for: 4 -> 0; matrix products, arithmetic and copies ran while one was open for 7% -> 0% of each run, Pallas kernels for 0% -> 0%
where the time goes in v1:
time: 171 us
  Pallas kernels  153 us (89%)
  local copies, waits for them, and re-layouts  13.9 us (8%)
  other arithmetic  3.04 us (2%)
    pallas_call x1, Pallas kernels, send_lists(): pl.pallas_call(functools.partial(lists_kernel, lat_count, count), out_sha...  50.3 us
    pallas_call x1, Pallas kernels, gather(): pl.pallas_call(functools.partial(gather_kernel, lat_count, lon_count), ou...  38.4 us
    pallas_call x1, Pallas kernels, atmos_step(): pl.pallas_call(functools.partial(atmos_kernel, lat_count), out_shape=jax....  22.7 us
    pallas_call x1, Pallas kernels, ocean_halo(): pl.pallas_call(functools.partial(ocean_halo_kernel, lat_count, lon_count)...  21.6 us
    pallas_call x1, Pallas kernels, ocean_step(): pl.pallas_call(functools.partial(ocean_kernel, lat_count), out_shape=(jax...  14.2 us
    unnamed x14, local copies, waits for them, and re-layouts  9.3 us
    pallas_call x1, Pallas kernels, merge(): pl.pallas_call(functools.partial(merge_kernel, lat_count), out_shape=jax....  5.97 us

profile of v1, /device:TPU:3, one launch (start us, length us, event | category | flops | bytes accessed | tf_op | source)
XLA Modules:
  0.0 171.0 jit_solution(17601255526299564695)
XLA Ops:
  0.6 0.7 multiply_add_fusion
  1.3 0.1 copy.25
  1.4 0.6 reshape.22.meta
  2.1 0.8 convert_bitcast_fusion
  2.9 2.0 %copy.26 = bf16[76,8,1024]{2,0,1:T(8,128)(2,1)S(1)} copy(bf16[76,8,1024]{2,1,0:T(8,128)(2,1)} %param.14) | data formatting | bytes 2490368 | tf_op args[0]
  4.8 0.0 copy-start.1
  4.9 0.1 pad.7.clone
  4.9 0.0 copy-start.2
  4.9 1.6 maximum_bitcast_fusion.field.x_ref
  6.5 21.6 %ocean_halo.1 = (bf16[2,80,1024]{2,1,0:T(8,128)(2,1)}, bf16[2,80,1024]{2,1,0:T(8,128)(2,1)}, bf16[12,80,128]{2,1,0:T(8,128)(2,1)}, bf16[12,80,128]{2,1,0:T(8,128)(2,1)}) custom-call(bf16[8,80,1024]{2,1,0:T(8,128)(2,1)} %maximum_bitcast_fusion.field.x_ref), custom_call_target="tpu_custom_call" | custom-call | tf_op jit(solution)/shard_map/ocean_halo/pallas_call | solution.py:116
  28.2 0.0 copy-done.1
  28.2 0.1 copy.28
  28.4 0.8 reshape.23.w1_ref
  29.1 0.0 copy-done.2
  29.1 0.1 copy.29
  29.3 0.8 reshape.24.w2_ref
  30.1 14.2 %ocean.1 = (bf16[8,64,1024]{2,1,0:T(8,128)(2,1)}, bf16[3,128,64,128]{3,2,1,0:T(8,128)(2,1)}, s32[3,8,128]{2,1,0:T(8,128)}) custom-call(s32[128]{0:T(128)} %reshape.22.meta, bf16[8,80,1024]{2,1,0:T(8,128)(2,1)} %maximum_bitcast_fusion.field.x_ref, bf16[2,80,1024]{2,1,0:T(8,128)(2,1)} %get-tuple-element.18.top_ref, ...), custom_call_target="tpu_custom_call" | custom-call | tf_op jit(solution)/shard_map/ocean/pallas_call | solution.py:218
  44.3 2.8 %copy.33 = bf16[64,8,1024]{2,1,0:T(8,128)(2,1)} copy(bf16[64,8,1024]{2,0,1:T(8,128)(2,1)} %bitcast.22) | data formatting | bytes 2097152
  47.1 50.3 %send_lists.1 = (bf16[128,64,128]{2,1,0:T(8,128)(2,1)}, s32[8,128]{1,0:T(8,128)}, bf16[128,64,128]{2,1,0:T(8,128)(2,1)}, s32[8,128]{1,0:T(8,128)}) custom-call(bf16[3,128,64,128]{3,2,1,0:T(8,128)(2,1)} %get-tuple-element.24.lists, s32[3,8,128]{2,1,0:T(8,128)} %get-tuple-element.23.codes.own_codes), custom_call_target="tpu_custom_call" | custom-call | tf_op jit(solution)/shard_map/send_lists/pallas_call | solution.py:273
  97.4 0.0 copy-start
  97.4 6.0 %merge.1.dense = bf16[4,64,64,128]{3,2,1,0:T(8,128)(2,1)} custom-call(s32[3,8,128]{2,1,0:T(8,128)} %get-tuple-element.23.codes.own_codes, s32[8,128]{1,0:T(8,128)} %get-tuple-element.25.north_codes, s32[8,128]{1,0:T(8,128)} %get-tuple-element.26.south_codes, bf16[3,128,64,128]{3,2,1,0:T(8,128)(2,1)} %get-tuple-element.24.lists, ...), custom_call_target="tpu_custom_call" | custom-call | tf_op jit(solution)/shard_map/merge/pallas_call | solution.py:334
  103.4 0.0 copy-done
  103.4 1.6 copy.36
  105.1 0.0 copy-start.3
  105.1 0.0 copy-start.4
  105.1 38.4 %gather.1 = (bf16[64,64,128]{2,1,0:T(8,128)(2,1)}, bf16[2,64,128]{2,1,0:T(8,128)(2,1)}, bf16[2,64,128]{2,1,0:T(8,128)(2,1)}, bf16[4,64,128]{2,1,0:T(8,128)(2,1)}, bf16[4,64,128]{2,1,0:T(8,128)(2,1)}) custom-call(bf16[4,64,64,128]{3,2,1,0:T(8,128)(2,1)} %merge.1.dense, bf16[64,64,128]{2,1,0:T(8,128)(2,1)} %bitcast.20), custom_call_target="tpu_custom_call" | custom-call | tf_op jit(solution)/shard_map/gather/pallas_call | solution.py:473
  143.5 0.0 copy-done.3
  143.5 0.1 copy.31
  143.6 0.8 reshape.26.w1_ref
  144.4 0.0 copy-done.4
  144.5 0.1 copy.32
  144.6 0.8 reshape.27.w2_ref
  145.4 22.7 %atmos.1 = bf16[64,64,128]{2,1,0:T(8,128)(2,1)} custom-call(bf16[64,64,128]{2,1,0:T(8,128)(2,1)} %get-tuple-element.29.a_ref, bf16[2,64,128]{2,1,0:T(8,128)(2,1)} %get-tuple-element.30.top_ref, bf16[2,64,128]{2,1,0:T(8,128)(2,1)} %get-tuple-element.31.bottom_ref, bf16[4,64,128]{2,1,0:T(8,128)(2,1)} %get-tuple-element.32.left_ref, ...), custom_call_target="tpu_custom_call" | custom-call | tf_op jit(solution)/shard_map/atmos/pallas_call | solution.py:560
  168.1 2.9 %copy.34 = bf16[64,64,128]{2,1,0:T(8,128)(2,1)} copy(bf16[64,64,128]{2,0,1:T(8,128)(2,1)} %bitcast.21) | data formatting | bytes 2097152
  (3 shorter events, 0.1 us)
Async XLA Ops:
  4.8 23.3 %copy-start.1 = (bf16[64,76,3,3]{1,0,3,2:T(8,128)(2,1)S(1)}, bf16[64,76,3,3]{1,0,3,2:T(8,128)(2,1)}, u32[]{:S(2)}) copy-start(bf16[64,76,3,3]{1,0,3,2:T(8,128)(2,1)} %param.16) | copy-start | bytes 262660
  4.9 24.2 %copy-start.2 = (bf16[64,64,3,3]{1,0,3,2:T(8,128)(2,1)S(1)}, bf16[64,64,3,3]{1,0,3,2:T(8,128)(2,1)}, u32[]{:S(2)}) copy-start(bf16[64,64,3,3]{1,0,3,2:T(8,128)(2,1)} %param.18) | copy-start | bytes 221188
  97.4 6.0 %copy-start = (bf16[64,64,128]{2,1,0:T(8,128)(2,1)S(1)}, bf16[64,64,128]{2,1,0:T(8,128)(2,1)}, u32[]{:S(2)}) copy-start(bf16[64,64,128]{2,1,0:T(8,128)(2,1)} %param.23) | copy-start | bytes 3145732
  105.1 38.4 %copy-start.3 = (bf16[64,64,3,3]{1,0,3,2:T(8,128)(2,1)S(1)}, bf16[64,64,3,3]{1,0,3,2:T(8,128)(2,1)}, u32[]{:S(2)}) copy-start(bf16[64,64,3,3]{1,0,3,2:T(8,128)(2,1)} %param.24) | copy-start | bytes 221188
  105.1 39.4 %copy-start.4 = (bf16[64,64,3,3]{1,0,3,2:T(8,128)(2,1)S(1)}, bf16[64,64,3,3]{1,0,3,2:T(8,128)(2,1)}, u32[]{:S(2)}) copy-start(bf16[64,64,3,3]{1,0,3,2:T(8,128)(2,1)} %param.26) | copy-start | bytes 221188

commit v2 on v1

v2 whole, which is shorter than its diff:
```python
import functools

import jax
import jax.numpy as jnp
from jax import lax
from jax.experimental import pallas as pl
from jax.experimental.pallas import tpu as pltpu
from jax.sharding import PartitionSpec as P

MESH = pl.DeviceIdType.MESH
F32 = jnp.float32
BF16 = jnp.bfloat16
VMEM_LIMIT = 56 * 1024 * 1024
GROUPS = 4


def silu(v):
    return 0.5 * v * (1.0 + jnp.tanh(0.5 * v))


def shifted_sum(taps):
    out = taps.shape[0] // 3
    columns = taps.shape[1]
    return (
        pltpu.roll(taps[0:out], 1, 1)
        + taps[out : 2 * out]
        + pltpu.roll(taps[2 * out :], columns - 1, 1)
    )


def stacked_weight(weight, padded_in):
    out, inn = weight.shape[:2]
    weight = jnp.pad(weight, ((0, 0), (0, padded_in - inn), (0, 0), (0, 0)))
    return weight.transpose(3, 0, 2, 1).reshape(3 * out, 3 * padded_in)


def column(bias):
    n = bias.shape[1]
    at = lax.broadcasted_iota(jnp.int32, (n, n), 0) == lax.broadcasted_iota(jnp.int32, (n, n), 1)
    return jnp.sum(jnp.where(at, bias, 0.0), axis=1, keepdims=True)


def remote(src, dst, send_sem, recv_sem, lat, lon):
    return pltpu.make_async_remote_copy(
        src_ref=src,
        dst_ref=dst,
        send_sem=send_sem,
        recv_sem=recv_sem,
        device_id={"lat": lat, "lon": lon},
        device_id_type=MESH,
    )


def landed(ref, sem):
    return pltpu.make_async_copy(ref, ref, sem)


def greet(partners, waits):
    barrier = pltpu.get_barrier_semaphore()
    for lat, lon, ok in partners:

        @pl.when(ok)
        def _():
            pl.semaphore_signal(
                barrier, inc=1, device_id={"lat": lat, "lon": lon}, device_id_type=MESH
            )

    pl.semaphore_wait(barrier, waits)


def whole_any(count):
    return [pl.BlockSpec(memory_space=pl.ANY)] * count


def ocean_halo_kernel(
    lat_count,
    lon_count,
    field,
    index,
    top,
    bottom,
    left,
    right,
    north_index,
    south_index,
    send_sem,
    recv_sem,
):
    lat, lon = lax.axis_index("lat"), lax.axis_index("lon")
    rows, _, cols = field.shape
    west = lax.rem(lon + lon_count - 1, lon_count)
    east = lax.rem(lon + 1, lon_count)
    up, down, always = lat > 0, lat < lat_count - 1, lat >= 0
    edge = jnp.logical_or(lat == 0, lat == lat_count - 1)
    partners = [(lat, west, always), (lat, east, always)]
    for there, ok in ((lat - 1, up), (lat + 1, down)):
        partners += [(there, side, ok) for side in (west, lon, east)]
    greet(partners, jnp.where(edge, 5, 8))

    lo, hi = pl.ds(0, 128), pl.ds(cols - 128, 128)
    first, last = pl.ds(0, 2), pl.ds(rows - 2, 2)
    own, above, below = pl.ds(2, rows), pl.ds(0, 2), pl.ds(rows + 2, 2)
    moves = [
        (field.at[:, :, lo], right.at[own], lat, west, always),
        (field.at[:, :, hi], left.at[own], lat, east, always),
        (field.at[first], bottom, lat - 1, lon, up),
        (field.at[last], top, lat + 1, lon, down),
        (field.at[first, :, lo], right.at[below], lat - 1, west, up),
        (field.at[first, :, hi], left.at[below], lat - 1, east, up),
        (field.at[last, :, lo], right.at[above], lat + 1, west, down),
        (field.at[last, :, hi], left.at[above], lat + 1, east, down),
        (index.at[0], south_index, lat - 1, lon, up),
        (index.at[2], north_index, lat + 1, lon, down),
    ]
    arrives = [always, always, down, up, down, down, up, up, down, up]
    copies = [
        (remote(src, dst, send_sem.at[i], recv_sem.at[i], a, b), ok)
        for i, (src, dst, a, b, ok) in enumerate(moves)
    ]
    for copy, ok in copies:
        pl.when(ok)(copy.start)
    for i, (copy, ok) in enumerate(copies):
        pl.when(ok)(copy.wait_send)
        pl.when(arrives[i])(landed(moves[i][1], recv_sem.at[i]).wait)


def ocean_halo(field, index, lat_count, lon_count):
    rows, channels, cols = field.shape
    shapes = [(2, channels, cols)] * 2 + [(rows + 4, channels, 128)] * 2
    table = jax.ShapeDtypeStruct(index.shape[1:], jnp.int32)
    return pl.pallas_call(
        functools.partial(ocean_halo_kernel, lat_count, lon_count),
        out_shape=[jax.ShapeDtypeStruct(s, BF16) for s in shapes] + [table] * 2,
        in_specs=whole_any(2),
        out_specs=whole_any(6),
        scratch_shapes=[pltpu.SemaphoreType.DMA((10,))] * 2,
        compiler_params=pltpu.CompilerParams(collective_id=0, has_side_effects=True),
        name="ocean_halo",
    )(field, index)


def ocean_kernel(
    lat_count,
    meta,
    x_ref,
    top_ref,
    bottom_ref,
    left_ref,
    right_ref,
    w1_ref,
    b1_ref,
    w2_ref,
    b2_ref,
    regrid_ref,
    next_ref,
    slots_ref,
    tall,
    hidden,
    sums,
):
    row = lax.rem(pl.program_id(0), 16)
    rows, channels, cols = x_ref.shape
    mask_at = 76
    b1, b2 = column(b1_ref[...]), column(b2_ref[...])

    def first_conv(j):
        field = jnp.concatenate([tall[j], tall[j + 1], tall[j + 2]], axis=0)
        taps = jnp.dot(w1_ref[...], field, preferred_element_type=F32)
        mask = tall[j + 1, mask_at : mask_at + 1, :].astype(F32)
        hidden[j] = (silu(shifted_sum(taps) + b1) * mask).astype(BF16)

    @pl.when(row == 0)
    def _():
        lat = lax.axis_index("lat")
        lane = lax.broadcasted_iota(jnp.int32, (channels, 128), 1)
        tall[2 : 2 + rows, :, 0:cols] = x_ref[...]
        for j in range(rows + 4):
            side = jnp.where(lane < 64, right_ref[j], left_ref[j])
            if j < 2 or j >= rows + 2:
                inside = lat > 0 if j < 2 else lat < lat_count - 1
                main = top_ref[j] if j < 2 else bottom_ref[j - rows - 2]
                tall[j, :, 0:cols] = jnp.where(inside, main, jnp.zeros_like(main))
                side = jnp.where(inside, side, jnp.zeros_like(side))
            tall[j, :, cols:] = side
        first_conv(0)
        first_conv(1)

    first_conv(lax.rem(row + 2, 16))
    field = jnp.concatenate([hidden[row], hidden[row + 1], hidden[row + 2]], axis=0)
    taps = jnp.dot(w2_ref[...], field, preferred_element_type=F32)
    mask = tall[row + 2, mask_at : mask_at + 1, :].astype(F32)
    result = ((shifted_sum(taps) + b2) * mask).astype(BF16)[:, :cols]
    next_ref[0] = result
    blocks = regrid_ref.shape[0]
    for q in range(blocks):
        field = result[:, q * 128 : (q + 1) * 128]
        both = lax.dot_general(
            field, regrid_ref[q], (((1,), (1,)), ((), ())), preferred_element_type=F32
        ).astype(BF16)
        for k in range(2):
            what = meta[(row * blocks + q) * 2 + k]
            at = what // 2
            value = both[:, k * 128 : (k + 1) * 128].astype(F32)
            sums[at] = jnp.where(lax.rem(what, 2) == 1, value, sums[at] + value)

    @pl.when(row == rows - 1)
    def _():
        groups, slots, size = slots_ref.shape[:3]

        def rounded(i, carry):
            for g in range(groups):
                slots_ref[g, i] = sums[i, g * size : (g + 1) * size].astype(BF16)
            return carry

        lax.fori_loop(0, slots, rounded, 0)


def ocean_step(meta, x, top, bottom, left, right, w1, b1, w2, b2, regrid, lat_count):
    rows, channels, cols = x.shape
    wide = cols + 128
    out = w2.shape[0] // 3
    slots = meta.shape[0]

    def whole(array):
        zeros = (0,) * array.ndim
        return pl.BlockSpec(array.shape, lambda r, meta: zeros)

    blocks = regrid.shape[0] // rows
    return pl.pallas_call(
        functools.partial(ocean_kernel, lat_count),
        out_shape=(
            jax.ShapeDtypeStruct((rows, out, cols), BF16),
            jax.ShapeDtypeStruct((GROUPS, slots, out // GROUPS, 128), BF16),
        ),
        grid_spec=pltpu.PrefetchScalarGridSpec(
            num_scalar_prefetch=1,
            grid=(rows,),
            in_specs=[whole(a) for a in (x, top, bottom, left, right, w1, b1, w2, b2)]
            + [pl.BlockSpec((blocks, 256, 128), lambda r, meta: (r, 0, 0))],
            out_specs=[
                pl.BlockSpec((1, out, cols), lambda r, meta: (r, 0, 0)),
                pl.BlockSpec((GROUPS, slots, out // GROUPS, 128), lambda r, meta: (0, 0, 0, 0)),
            ],
            scratch_shapes=[
                pltpu.VMEM((rows + 4, channels, wide), BF16),
                pltpu.VMEM((rows + 2, out, wide), BF16),
                pltpu.VMEM((slots, out, 128), F32),
            ],
        ),
        compiler_params=pltpu.CompilerParams(vmem_limit_bytes=VMEM_LIMIT),
        name="ocean",
    )(meta, x, top, bottom, left, right, w1, b1, w2, b2, regrid)


def couple_kernel(
    lat_count,
    lon_count,
    count,
    own_index,
    north_index,
    south_index,
    slots,
    atmos,
    first,
    top,
    bottom,
    left,
    right,
    *scratch,
):
    lat, lon = lax.axis_index("lat"), lax.axis_index("lon")
    west = lax.rem(lon + lon_count - 1, lon_count)
    east = lax.rem(lon + 1, lon_count)
    across = lax.rem(lon + 2, lon_count)
    beside = lon + 1 - 2 * lax.rem(lon, 2)
    beside_across = lax.rem(beside + 2, lon_count)
    up, down, always = lat > 0, lat < lat_count - 1, lat >= 0
    edge = jnp.logical_or(lat == 0, lat == lat_count - 1)
    partners = [(lat, there, always) for there in (west, east, across)]
    for there, ok in ((lat - 1, up), (lat + 1, down)):
        partners += [(there, side, ok) for side in (west, lon, east)]
    greet(partners, jnp.where(edge, 6, 9))

    groups, total, size, cols = slots.shape
    rows, channels = first.shape[:2]
    own, north, south = (scratch[i * groups : (i + 1) * groups] for i in range(3))
    away, mine, from_core, to_z, from_z, edges = scratch[3 * groups : 3 * groups + 6]
    load_sem, y_send, y_recv, core_send, core_recv, z_send, z_recv, halo_send, halo_recv = scratch[
        3 * groups + 6 :
    ]
    low, high = pl.ds(0, count), pl.ds(total - count, count)
    everything = pl.ds(0, total)
    to_south, to_north, loads = [], [], []
    for g in range(groups):
        to_south.append(
            remote(
                slots.at[g, high], north[g].at[high], y_send.at[0, g], y_recv.at[0, g], lat + 1, lon
            )
        )
        to_north.append(
            remote(
                slots.at[g, low], south[g].at[low], y_send.at[1, g], y_recv.at[1, g], lat - 1, lon
            )
        )
        loads.append(
            pltpu.make_async_copy(slots.at[g], own[g].at[everything], load_sem.at[g])
        )
        pl.when(down)(to_south[g].start)
        pl.when(up)(to_north[g].start)
        loads[g].start()
    for buffer in (own, north, south):
        for g in range(groups):
            buffer[g][total] = jnp.zeros((size, cols), BF16)

    def dense(g, lon_there, store):
        def row(t, carry):
            at = lon_there * rows + t
            i, j = at // 128, lax.rem(at, 128)
            a = own_index[1, i, j]
            b = jnp.where(up, north_index[i, j], total)
            c = jnp.where(down, south_index[i, j], total)
            value = own[g][a].astype(F32) + north[g][b].astype(F32) + south[g][c].astype(F32)
            store(t, value.astype(BF16))
            return carry

        lax.fori_loop(0, rows, row, 0, unroll=8)

    core_copies, z_copies = [], []
    for g in range(groups):
        loads[g].wait()
        pl.when(up)(landed(north[g].at[high], y_recv.at[0, g]).wait)
        pl.when(down)(landed(south[g].at[low], y_recv.at[1, g]).wait)
        for part, (theirs, ours) in enumerate(((beside_across, across), (beside, lon))):

            def put_away(t, value):
                away[part, g, t] = value

            def put_mine(t, value):
                mine[part, g, t] = value

            dense(g, theirs, put_away)
            copy = remote(
                away.at[part, g],
                from_core.at[part, g],
                core_send.at[part, g],
                core_recv.at[part, g],
                lat,
                beside,
            )
            copy.start()
            core_copies.append(copy)
            dense(g, ours, put_mine)
            if part == 0:
                landed(from_core.at[0, g], core_recv.at[0, g]).wait()
                to_z[g] = (mine[0, g].astype(F32) + from_core[0, g].astype(F32)).astype(BF16)
                copy = remote(
                    to_z.at[g], from_z.at[g], z_send.at[g], z_recv.at[g], lat, across
                )
                copy.start()
                z_copies.append(copy)

    lane = lax.broadcasted_iota(jnp.int32, (size, cols), 1)
    tiles = edges.shape[0]
    for g in range(groups):
        landed(from_core.at[1, g], core_recv.at[1, g]).wait()
        landed(from_z.at[g], z_recv.at[g]).wait()
        part = pl.ds(g * size, size)
        for tile in range(tiles):
            edge = jnp.zeros((size, cols), F32)
            for k in range(32):
                r = tile * 32 + k
                flux = (
                    mine[1, g, r].astype(F32)
                    + from_core[1, g, r].astype(F32)
                    + from_z[g, r].astype(F32)
                )
                v = (atmos[r, part].astype(F32) + flux).astype(BF16)
                first[r, part] = v
                rolled = pltpu.roll(v.astype(F32), (4 * k + 2) % cols, 1)
                edge = jnp.where(lane // 4 == k, rolled, edge)
            edges[tile, part] = edge.astype(BF16)
    lo, hi = edges.at[0], edges.at[tiles - 1]
    moves = [
        (edges, right.at[pl.ds(1, tiles)], lat, west, always, always),
        (edges, left.at[pl.ds(1, tiles)], lat, east, always, always),
        (first.at[pl.ds(0, 2)], bottom, lat - 1, lon, up, down),
        (first.at[pl.ds(rows - 2, 2)], top, lat + 1, lon, down, up),
        (lo, right.at[tiles + 1], lat - 1, west, up, down),
        (lo, left.at[tiles + 1], lat - 1, east, up, down),
        (hi, right.at[0], lat + 1, west, down, up),
        (hi, left.at[0], lat + 1, east, down, up),
    ]
    copies = [
        remote(src, dst, halo_send.at[i], halo_recv.at[i], a, b)
        for i, (src, dst, a, b, _, _) in enumerate(moves)
    ]
    for copy, move in zip(copies, moves):
        pl.when(move[4])(copy.start)
    for copy in core_copies + z_copies:
        copy.wait_send()
    for g in range(groups):
        pl.when(down)(to_south[g].wait_send)
        pl.when(up)(to_north[g].wait_send)
    for i, (copy, move) in enumerate(zip(copies, moves)):
        pl.when(move[4])(copy.wait_send)
        pl.when(move[5])(landed(move[1], halo_recv.at[i]).wait)


def couple(index, north_index, south_index, slots, atmos, count, collective_id, lat_count, lon_count):
    groups, total, size, cols = slots.shape
    rows, channels, cols = atmos.shape
    tiles = rows // 32
    vmem = pl.BlockSpec(memory_space=pltpu.VMEM)
    smem = pl.BlockSpec(memory_space=pltpu.SMEM)
    dma = pltpu.SemaphoreType.DMA
    shapes = [(rows, channels, cols)] + [(2, channels, cols)] * 2 + [(tiles + 2, channels, cols)] * 2
    received = pltpu.VMEM((total + 1, size, cols), BF16)
    one = pltpu.VMEM((groups, rows, size, cols), BF16)
    two = pltpu.VMEM((2, groups, rows, size, cols), BF16)
    return pl.pallas_call(
        functools.partial(couple_kernel, lat_count, lon_count, count),
        out_shape=[jax.ShapeDtypeStruct(s, BF16) for s in shapes],
        in_specs=[smem] * 3 + whole_any(1) + [vmem],
        out_specs=[vmem] + whole_any(4),
        scratch_shapes=[received] * (3 * groups)
        + [two] * 3
        + [one] * 2
        + [pltpu.VMEM((tiles, channels, cols), BF16)]
        + [dma((groups,))]
        + [dma((2, groups))] * 4
        + [dma((groups,))] * 2
        + [dma((8,))] * 2,
        compiler_params=pltpu.CompilerParams(
            collective_id=collective_id, has_side_effects=True, vmem_limit_bytes=VMEM_LIMIT
        ),
        name="couple",
    )(index, north_index, south_index, slots, atmos)


def atmos_kernel(
    lat_count, a_ref, top_ref, bottom_ref, left_ref, right_ref, w1_ref, b1_ref, w2_ref, b2_ref, out_ref, tall, second
):
    count, channels, cols = a_ref.shape
    group = 2
    lat = lax.axis_index("lat")
    b1, b2 = column(b1_ref[...]), column(b2_ref[...])

    tall[2 : 2 + count, :, 0:cols] = a_ref[...]
    lane = lax.broadcasted_iota(jnp.int32, (channels, cols), 1)
    for tile in range(count // 32 + 2):
        side = jnp.where(lane % 4 < 2, left_ref[tile], right_ref[tile]).astype(F32)
        for k in range(32):
            r = tile * 32 - 32 + k
            if r < -2 or r >= count + 2:
                continue
            v = pltpu.roll(side, (126 - 4 * k) % cols, 1).astype(BF16)
            if r < 0 or r >= count:
                inside = lat > 0 if r < 0 else lat < lat_count - 1
                main = top_ref[r + 2] if r < 0 else bottom_ref[r - count]
                tall[r + 2, :, 0:cols] = jnp.where(inside, main, jnp.zeros_like(main))
                v = jnp.where(inside, v, jnp.zeros_like(v))
            tall[r + 2, :, cols:] = v

    def conv(source, weight, start):
        fields = [
            jnp.concatenate([source[start + i + d] for d in range(3)], axis=0)
            for i in range(group)
        ]
        return jnp.dot(weight, jnp.concatenate(fields, axis=1), preferred_element_type=F32)

    def first(step, carry):
        start = step * group
        taps = conv(tall, w1_ref[...], start)
        for i in range(group):
            j = start + i
            value = silu(shifted_sum(taps[:, i * 2 * cols : (i + 1) * 2 * cols]) + b1)
            outside = jnp.logical_or(
                jnp.logical_and(j == 0, lat == 0),
                jnp.logical_and(j == count + 1, lat == lat_count - 1),
            )
            second[j] = jnp.where(outside, 0.0, value).astype(BF16)
        return carry

    lax.fori_loop(0, (count + 2) // group, first, 0)

    def last(step, carry):
        start = step * group
        taps = conv(second, w2_ref[...], start)
        for i in range(group):
            j = start + i
            value = shifted_sum(taps[:, i * 2 * cols : (i + 1) * 2 * cols])[:, :cols]
            out_ref[j] = (a_ref[j].astype(F32) + (value + b2)).astype(BF16)
        return carry

    lax.fori_loop(0, count // group, last, 0)


def atmos_step(a, top, bottom, left, right, w1, b1, w2, b2, lat_count):
    count, channels, cols = a.shape
    vmem = pl.BlockSpec(memory_space=pltpu.VMEM)
    return pl.pallas_call(
        functools.partial(atmos_kernel, lat_count),
        out_shape=jax.ShapeDtypeStruct(a.shape, BF16),
        in_specs=[vmem] * 9,
        out_specs=vmem,
        scratch_shapes=[
            pltpu.VMEM((count + 4, channels, 2 * cols), BF16),
            pltpu.VMEM((count + 2, channels, 2 * cols), BF16),
        ],
        compiler_params=pltpu.CompilerParams(vmem_limit_bytes=VMEM_LIMIT),
        name="atmos",
    )(a, top, bottom, left, right, w1, b1, w2, b2)


def per_device(
    ocean_state,
    sea_mask,
    ocean_w1,
    ocean_b1,
    ocean_w2,
    ocean_b2,
    regrid_weight,
    route_dev,
    route_row,
    atmos_state,
    atmos_w1,
    atmos_b1,
    atmos_w2,
    atmos_b2,
):
    lat_count, lon_count = lax.axis_size("lat"), lax.axis_size("lon")
    lat = lax.axis_index("lat")
    atmos_rows = atmos_state.shape[1]

    field = jnp.concatenate(
        [
            ocean_state,
            sea_mask.astype(BF16)[None],
            jnp.zeros((3,) + sea_mask.shape, BF16),
        ],
        axis=0,
    ).transpose(1, 0, 2)
    key = ((route_dev - (lat - 1) * lon_count) * atmos_rows + route_row).reshape(-1)
    count = key.shape[0]
    order = jnp.arange(count, dtype=jnp.int32)
    place = jnp.sum((key[None, :] < key[:, None]).astype(jnp.int32), axis=1)
    again = (key[None, :] == key[:, None]) & (order[None, :] < order[:, None])
    meta = place * 2 + 1 - jnp.max(again.astype(jnp.int32), axis=1)
    per_step = lon_count * atmos_rows
    lanes = jnp.arange(8 * 128, dtype=jnp.int32)
    number = jnp.where(lanes < per_step, lanes, -4 * per_step).reshape(1, 8, 128)
    number = number + jnp.arange(3, dtype=jnp.int32)[:, None, None] * per_step
    index = jnp.min(
        jnp.where(number[..., None] == key[None, None, None, :], place[None, None, None, :], count),
        axis=3,
    )
    top, bottom, left, right, north_index, south_index = ocean_halo(
        field, index, lat_count, lon_count
    )
    ocean_next, slots = ocean_step(
        meta,
        field,
        top,
        bottom,
        left,
        right,
        stacked_weight(ocean_w1, 80),
        ocean_b1[None, :],
        stacked_weight(ocean_w2, 64),
        ocean_b2[None, :],
        regrid_weight.reshape(-1, 256, 128),
        lat_count,
    )
    first, top, bottom, left, right = couple(
        index,
        north_index,
        south_index,
        slots,
        atmos_state.transpose(1, 0, 2),
        count,
        1,
        lat_count,
        lon_count,
    )
    atmos_next = atmos_step(
        first,
        top,
        bottom,
        left,
        right,
        stacked_weight(atmos_w1, 64),
        atmos_b1[None, :],
        stacked_weight(atmos_w2, 64),
        atmos_b2[None, :],
        lat_count,
    )
    return ocean_next.transpose(1, 0, 2), atmos_next.transpose(1, 0, 2)


def solution(mesh):
    in_specs = (
        P(None, "lat", "lon"),
        P("lat", "lon"),
        P(),
        P(),
        P(),
        P(),
        P(("lat", "lon"), None, None, None),
        P(("lat", "lon"), None),
        P(("lat", "lon"), None),
        P(None, "lat", "lon"),
        P(),
        P(),
        P(),
        P(),
    )
    out_specs = (P(None, "lat", "lon"), P(None, "lat", "lon"))
    return jax.shard_map(
        per_device, mesh=mesh, in_specs=in_specs, out_specs=out_specs, check_vma=False
    )
```

time: 171 us -> 160 us (0.936)
  Pallas kernels: 153 us -> 141 us
    pallas_call x3 -> x1, Pallas kernels: 94.7 us -> 82.2 us  [couple(): pl.pallas_call(functools.partial(couple_kernel, lat_count, lon_count, cou...]
    unnamed x14 -> x18, local copies, waits for them, and re-layouts: 9.3 us -> 8.16 us
where the time goes in v2:
time: 160 us; the launch traced here: 159 us
  Pallas kernels  141 us (88%)
  local copies, waits for them, and re-layouts  12.3 us (8%)
  other arithmetic  4.73 us (3%)
    pallas_call x1, Pallas kernels, couple(): pl.pallas_call(functools.partial(couple_kernel, lat_count, lon_count, cou...  82.2 us
    pallas_call x1, Pallas kernels, atmos_step(): pl.pallas_call(functools.partial(atmos_kernel, lat_count), out_shape=jax....  22.6 us
    pallas_call x1, Pallas kernels, ocean_halo(): pl.pallas_call(functools.partial(ocean_halo_kernel, lat_count, lon_count)...  21.8 us
    pallas_call x1, Pallas kernels, ocean_step(): pl.pallas_call(functools.partial(ocean_kernel, lat_count), out_shape=(jax...  14.8 us
    unnamed x18, local copies, waits for them, and re-layouts  8.16 us

profile of v2, /device:TPU:3, one launch (start us, length us, event | category | flops | bytes accessed | tf_op | source)
XLA Modules:
  0.0 159.2 jit_solution(3389798863907419094)
XLA Ops:
  0.6 0.0 copy-start.6
  0.6 0.7 multiply_add_fusion
  1.3 0.1 copy.35
  1.4 0.1 lt.38
  1.6 0.2 convert_reduce_fusion.1
  1.8 0.1 broadcast_add_fusion
  1.9 1.6 %select_reduce_fusion.index.own_index = s32[3,8,128]{2,1,0:T(8,128)} fusion(s32[128]{0:T(128)S(1)} %get-tuple-element.34, s32[128]{0:T(128)S(1)} %lt.38, s32[3,8,128]{2,1,0:T(8,128)S(1)} %broadcast_add_fusion), kind=kLoop, calls=%fused_computation | loop fusion | flops 1176576 | bytes 25600 | tf_op jit(solution)/shard_map/reduce_min | solution.py:553
  3.5 2.0 %copy.36 = bf16[76,8,1024]{2,0,1:T(8,128)(2,1)S(1)} copy(bf16[76,8,1024]{2,1,0:T(8,128)(2,1)} %param.14) | data formatting | bytes 2490368 | tf_op args[0]
  5.5 0.0 copy-done.6
  5.5 0.1 pad.7.clone
  5.6 0.0 copy-start.2
  5.6 1.6 maximum_bitcast_fusion.field.x_ref
  7.2 0.0 copy-start.3
  7.2 21.8 %ocean_halo.1 = (bf16[2,80,1024]{2,1,0:T(8,128)(2,1)}, bf16[2,80,1024]{2,1,0:T(8,128)(2,1)}, bf16[12,80,128]{2,1,0:T(8,128)(2,1)}, bf16[12,80,128]{2,1,0:T(8,128...) custom-call(bf16[8,80,1024]{2,1,0:T(8,128)(2,1)} %maximum_bitcast_fusion.field.x_ref, ...), custom_call_target="tpu_custom_call" | custom-call | tf_op jit(solution)/shard_map/ocean_halo/pallas_call | solution.py:131
  29.0 0.6 add_subtract_fusion.meta
  29.5 0.0 copy-done.2
  29.6 0.1 copy.38
  29.7 0.8 reshape.40.w1_ref
  30.5 0.0 copy-done.3
  30.5 0.1 copy.39
  30.6 0.8 reshape.41.w2_ref
  31.4 0.0 copy-start
  31.4 14.8 %ocean.1 = (bf16[8,64,1024]{2,1,0:T(8,128)(2,1)}, bf16[4,128,16,128]{3,2,1,0:T(8,128)(2,1)}) custom-call(s32[128]{0:T(128)} %add_subtract_fusion.meta, bf16[8,80,1024]{2,1,0:T(8,128)(2,1)} %maximum_bitcast_fusion.field.x_ref, bf16[2,80,1024]{2,1,0:T(8,128)(2,1)} %get-tuple-element.15.top_ref, bf16[2,80,1024]{2,1,0:T(8,128)(2,1)} %get-tuple-element.16.bottom_ref, ...), custom_call_target="tpu_custom_call" | custom-call | tf_op jit(solution)/shard_map/ocean/pallas_call | solution.py:229
  46.2 0.0 copy-done
  46.2 1.6 %copy.46 = bf16[64,64,128]{2,0,1:T(8,128)(2,1)} copy(bf16[64,64,128]{2,1,0:T(8,128)(2,1)S(1)} %copy-done) | data formatting | bytes 2097152 | tf_op args[9]
  47.9 0.0 copy-start.4
  47.9 0.0 copy-start.5
  47.9 82.2 %couple.1 = (bf16[64,64,128]{2,1,0:T(8,128)(2,1)}, bf16[2,64,128]{2,1,0:T(8,128)(2,1)}, bf16[2,64,128]{2,1,0:T(8,128)(2,1)}, bf16[4,64,128]{2,1,0:T(8,128)(2,1)}, bf16[4,64,128]{2,1,0:T(8,128)(2,1)}) custom-call(s32[3,8,128]{2,1,0:T(8,128)} %select_reduce_fusion.index.own_index, s32[8,128]{1,0:T(8,128)} %get-tuple-element.20.north_index, ...), custom_call_target="tpu_custom_call" | custom-call | tf_op jit(solution)/shard_map/couple/pallas_call | solution.py:420
  130.1 0.0 copy-done.4
  130.1 0.1 copy.41
  130.3 0.8 reshape.43.w1_ref
  131.1 0.0 copy-done.5
  131.1 0.1 copy.42
  131.2 0.8 reshape.44.w2_ref
  132.0 22.6 %atmos.1 = bf16[64,64,128]{2,1,0:T(8,128)(2,1)} custom-call(bf16[64,64,128]{2,1,0:T(8,128)(2,1)} %get-tuple-element.23.a_ref, bf16[2,64,128]{2,1,0:T(8,128)(2,1)} %get-tuple-element.24.top_ref, bf16[2,64,128]{2,1,0:T(8,128)(2,1)} %get-tuple-element.25.bottom_ref, bf16[4,64,128]{2,1,0:T(8,128)(2,1)} %get-tuple-element.26.left_ref, ...), custom_call_target="tpu_custom_call" | custom-call | tf_op jit(solution)/shard_map/atmos/pallas_call | solution.py:501
  154.6 0.0 copy-start.1
  154.6 3.0 %copy.44 = bf16[64,64,128]{2,1,0:T(8,128)(2,1)} copy(bf16[64,64,128]{2,0,1:T(8,128)(2,1)} %bitcast.21) | data formatting | bytes 2097152
  157.6 0.0 copy-done.1
  157.6 1.5 copy.43
  (6 shorter events, 0.1 us)
Async XLA Ops:
  0.6 4.8 %copy-start.6 = (s32[8,1024]{1,0:T(8,128)S(1)}, s32[8,1024]{1,0:T(8,128)}, u32[]{:S(2)}) copy-start(s32[8,1024]{1,0:T(8,128)} %param.15) | copy-start | bytes 98308
  5.6 23.9 %copy-start.2 = (bf16[64,76,3,3]{1,0,3,2:T(8,128)(2,1)S(1)}, bf16[64,76,3,3]{1,0,3,2:T(8,128)(2,1)}, u32[]{:S(2)}) copy-start(bf16[64,76,3,3]{1,0,3,2:T(8,128)(2,1)} %param.16) | copy-start | bytes 262660
  7.2 23.3 %copy-start.3 = (bf16[64,64,3,3]{1,0,3,2:T(8,128)(2,1)S(1)}, bf16[64,64,3,3]{1,0,3,2:T(8,128)(2,1)}, u32[]{:S(2)}) copy-start(bf16[64,64,3,3]{1,0,3,2:T(8,128)(2,1)} %param.18) | copy-start | bytes 221188
  31.4 14.8 %copy-start = (bf16[64,64,128]{2,1,0:T(8,128)(2,1)S(1)}, bf16[64,64,128]{2,1,0:T(8,128)(2,1)}, u32[]{:S(2)}) copy-start(bf16[64,64,128]{2,1,0:T(8,128)(2,1)} %param.23) | copy-start | bytes 3145732
  47.9 82.3 %copy-start.4 = (bf16[64,64,3,3]{1,0,3,2:T(8,128)(2,1)S(1)}, bf16[64,64,3,3]{1,0,3,2:T(8,128)(2,1)}, u32[]{:S(2)}) copy-start(bf16[64,64,3,3]{1,0,3,2:T(8,128)(2,1)} %param.24) | copy-start | bytes 221188
  47.9 83.2 %copy-start.5 = (bf16[64,64,3,3]{1,0,3,2:T(8,128)(2,1)S(1)}, bf16[64,64,3,3]{1,0,3,2:T(8,128)(2,1)}, u32[]{:S(2)}) copy-start(bf16[64,64,3,3]{1,0,3,2:T(8,128)(2,1)} %param.26) | copy-start | bytes 221188
  154.6 3.0 %copy-start.1 = (bf16[8,64,1024]{2,1,0:T(8,128)(2,1)S(1)}, bf16[8,64,1024]{2,1,0:T(8,128)(2,1)}, u32[]{:S(2)}) copy-start(bf16[8,64,1024]{2,1,0:T(8,128)(2,1)} %get-tuple-element.19) | copy-start | bytes 3145732

commit v3 on v2

--- a/solution.py
+++ b/solution.py
@@ -12,6 +12,9 @@
 BF16 = jnp.bfloat16
 VMEM_LIMIT = 56 * 1024 * 1024
 GROUPS = 4
+FIRST_ROWS = 11
+LAST_ROWS = 16
+LENGTHS = (32, 48, 64)
 
 
 def silu(v):
@@ -441,7 +444,6 @@
     lat_count, a_ref, top_ref, bottom_ref, left_ref, right_ref, w1_ref, b1_ref, w2_ref, b2_ref, out_ref, tall, second
 ):
     count, channels, cols = a_ref.shape
-    group = 2
     lat = lax.axis_index("lat")
     b1, b2 = column(b1_ref[...]), column(b2_ref[...])
 
@@ -461,7 +463,7 @@
                 v = jnp.where(inside, v, jnp.zeros_like(v))
             tall[r + 2, :, cols:] = v
 
-    def conv(source, weight, start):
+    def conv(source, weight, start, group):
         fields = [
             jnp.concatenate([source[start + i + d] for d in range(3)], axis=0)
             for i in range(group)
@@ -469,8 +471,9 @@
         return jnp.dot(weight, jnp.concatenate(fields, axis=1), preferred_element_type=F32)
 
     def first(step, carry):
+        group = FIRST_ROWS
         start = step * group
-        taps = conv(tall, w1_ref[...], start)
+        taps = conv(tall, w1_ref[...], start, group)
         for i in range(group):
             j = start + i
             value = silu(shifted_sum(taps[:, i * 2 * cols : (i + 1) * 2 * cols]) + b1)
@@ -481,18 +484,19 @@
             second[j] = jnp.where(outside, 0.0, value).astype(BF16)
         return carry
 
-    lax.fori_loop(0, (count + 2) // group, first, 0)
+    lax.fori_loop(0, (count + 2) // FIRST_ROWS, first, 0)
 
     def last(step, carry):
+        group = LAST_ROWS
         start = step * group
-        taps = conv(second, w2_ref[...], start)
+        taps = conv(second, w2_ref[...], start, group)
         for i in range(group):
             j = start + i
             value = shifted_sum(taps[:, i * 2 * cols : (i + 1) * 2 * cols])[:, :cols]
             out_ref[j] = (a_ref[j].astype(F32) + (value + b2)).astype(BF16)
         return carry
 
-    lax.fori_loop(0, count // group, last, 0)
+    lax.fori_loop(0, count // LAST_ROWS, last, 0)
 
 
 def atmos_step(a, top, bottom, left, right, w1, b1, w2, b2, lat_count):
@@ -547,6 +551,11 @@
     again = (key[None, :] == key[:, None]) & (order[None, :] < order[:, None])
     meta = place * 2 + 1 - jnp.max(again.astype(jnp.int32), axis=1)
     per_step = lon_count * atmos_rows
+    longest = jnp.maximum(
+        jnp.sum((key < per_step).astype(jnp.int32)), jnp.sum((key >= 2 * per_step).astype(jnp.int32))
+    )
+    longest = lax.pmax(longest, ("lat", "lon"))
+    which = sum((longest > n).astype(jnp.int32) for n in LENGTHS if n < count)
     lanes = jnp.arange(8 * 128, dtype=jnp.int32)
     number = jnp.where(lanes < per_step, lanes, -4 * per_step).reshape(1, 8, 128)
     number = number + jnp.arange(3, dtype=jnp.int32)[:, None, None] * per_step
@@ -571,16 +580,22 @@
         regrid_weight.reshape(-1, 256, 128),
         lat_count,
     )
-    first, top, bottom, left, right = couple(
+    lengths = [n for n in LENGTHS if n < count] + [count]
+
+    def coupled(at):
+        def branch(*operands):
+            return tuple(couple(*operands, lengths[at], 1 + at, lat_count, lon_count))
+
+        return branch
+
+    first, top, bottom, left, right = lax.switch(
+        which,
+        [coupled(at) for at in range(len(lengths))],
         index,
         north_index,
         south_index,
         slots,
         atmos_state.transpose(1, 0, 2),
-        count,
-        1,
-        lat_count,
-        lon_count,
     )
     atmos_next = atmos_step(
         first,

time: 160 us -> 185 us (1.16)
  blocking collectives: 0 us -> 63.6 us
  Pallas kernels: 141 us -> 99.2 us
  between operations: 0.77 us -> 3.96 us
    pmax x0 -> x1, blocking collectives: none -> 63.6 us  [per_device(): longest = lax.pmax(longest, ('lat', 'lon'))]
    pallas_call x1, Pallas kernels: 82.2 us -> 53.9 us  [couple(): pl.pallas_call(functools.partial(couple_kernel, lat_count, lon_count, cou...]
    pallas_call x1, Pallas kernels: 22.6 us -> 9.51 us  [atmos_step(): pl.pallas_call(functools.partial(atmos_kernel, lat_count), out_shape=jax....]
    unnamed x18 -> x14, local copies, waits for them, and re-layouts: 8.16 us -> 8.42 us
where the time goes in v3:
time: 185 us
  Pallas kernels  99.2 us (54%)
  blocking collectives  63.6 us (34%)
  local copies, waits for them, and re-layouts  12.5 us (7%)
  other arithmetic  5.5 us (3%)
  between operations  3.96 us (2%)
    pmax x1, blocking collectives, per_device(): longest = lax.pmax(longest, ('lat', 'lon'))  63.6 us
    pallas_call x1, Pallas kernels, couple(): pl.pallas_call(functools.partial(couple_kernel, lat_count, lon_count, cou...  53.9 us
    pallas_call x1, Pallas kernels, ocean_halo(): pl.pallas_call(functools.partial(ocean_halo_kernel, lat_count, lon_count)...  21.9 us
    pallas_call x1, Pallas kernels, ocean_step(): pl.pallas_call(functools.partial(ocean_kernel, lat_count), out_shape=(jax...  13.9 us
    pallas_call x1, Pallas kernels, atmos_step(): pl.pallas_call(functools.partial(atmos_kernel, lat_count), out_shape=jax....  9.51 us
    unnamed x14, local copies, waits for them, and re-layouts  8.42 us

profile of v3, /device:TPU:3, one launch (start us, length us, event | category | flops | bytes accessed | tf_op | source)
XLA Modules:
  0.0 185.0 jit_solution(6225765284683495486)
XLA Ops:
  0.6 1.4 fusion.2
  2.0 0.1 copy.35
  2.1 0.1 lt.45
  2.2 0.2 convert_reduce_fusion.1
  2.4 0.5 add_subtract_fusion.meta
  2.9 0.8 convert_bitcast_fusion
  3.7 2.0 %copy.36 = bf16[76,8,1024]{2,0,1:T(8,128)(2,1)S(1)} copy(bf16[76,8,1024]{2,1,0:T(8,128)(2,1)} %param.18) | data formatting | bytes 2490368 | tf_op args[0]
  5.7 0.1 pad.7.clone
  5.8 0.0 copy-start.1
  5.8 1.6 maximum_bitcast_fusion.field.x_ref
  7.4 0.0 copy-start.2
  7.4 0.1 broadcast_add_fusion
  7.5 1.0 select_reduce_fusion.index
  8.5 21.9 %ocean_halo.1 = (bf16[2,80,1024]{2,1,0:T(8,128)(2,1)}, bf16[2,80,1024]{2,1,0:T(8,128)(2,1)}, bf16[12,80,128]{2,1,0:T(8,128)(2,1)}, bf16[12,80,128]{2,1,0:T(8,128...) custom-call(bf16[8,80,1024]{2,1,0:T(8,128)(2,1)} %maximum_bitcast_fusion.field.x_ref, ...), custom_call_target="tpu_custom_call" | custom-call | tf_op jit(solution)/shard_map/ocean_halo/pallas_call | solution.py:134
  30.4 0.0 copy-done.1
  30.4 0.1 copy.38
  30.6 0.8 reshape.41.w1_ref
  31.4 0.0 copy-done.2
  31.4 0.1 copy.39
  31.5 0.8 reshape.42.w2_ref
  32.3 13.9 %ocean.1 = (bf16[8,64,1024]{2,1,0:T(8,128)(2,1)}, bf16[4,128,16,128]{3,2,1,0:T(8,128)(2,1)S(1)}) custom-call(s32[128]{0:T(128)} %add_subtract_fusion.meta, bf16[8,80,1024]{2,1,0:T(8,128)(2,1)} %maximum_bitcast_fusion.field.x_ref, bf16[2,80,1024]{2,1,0:T(8,128)(2,1)} %get-tuple-element.75.top_ref, bf16[2,80,1024]{2,1,0:T(8,128)(2,1)} %get-tuple-element.76.bottom_ref, ...), custom_call_target="tpu_custom_call" | custom-call | tf_op jit(solution)/shard_map/ocean/pallas_call | solution.py:232
  46.2 0.0 copy-start
  46.2 2.9 %copy.43 = bf16[64,8,1024]{2,1,0:T(8,128)(2,1)} copy(bf16[64,8,1024]{2,0,1:T(8,128)(2,1)} %bitcast.25) | data formatting | bytes 2097152
  50.3 63.6 %pmax.7 = s32[]{:T(128)} all-reduce(s32[]{:T(128)S(6)} %max.5), channel_id=1, replica_groups=mesh['lat'=32,'lon'=4] {'lat','lon'}, use_global_device_ids=true, to_apply=%region_5.6 | all-reduce | flops 1 | bytes 8 | tf_op jit(solution)/shard_map/pmax | solution.py:557
  115.8 0.0 copy-done
  115.8 0.7 copy.46
  116.5 0.0 copy-start.3
  116.5 0.0 copy-start.4
  116.5 54.2 %conditional.1 = ((bf16[64,64,128]{2,1,0:T(8,128)(2,1)S(1)}, bf16[2,64,128]{2,1,0:T(8,128)(2,1)}, bf16[2,64,128]{2,1,0:T(8,128)(2,1)}, bf16[4,64,128]{2,1,0:T(8,128)(2,1)S(1)}, bf16[4,64,128]{2,1,0:T(8,128)(2,1)})) conditional(s32[]{:T(128)} %clamp.3, (s32[3,8,128]{2,1,0:T(8,128)S(1)}, s32[8,128]{1,0:T(8,128)S(1)}, ...), branch_computations={%region_6.7_spmd, %region_7.8_spmd, %region_8.9_spmd, %region_9.10... | conditional | bytes 8 | solution.py:591
  116.5 53.9 %couple.5 = (bf16[64,64,128]{2,1,0:T(8,128)(2,1)S(1)}, bf16[2,64,128]{2,1,0:T(8,128)(2,1)}, bf16[2,64,128]{2,1,0:T(8,128)(2,1)}, bf16[4,64,128]{2,1,0:T(8,128)(2,1)S(1)}, bf16[4,64,128]{2,1,0:T(8,128)(2,1)}) custom-call(s32[3,8,128]{2,1,0:T(8,128)S(1)} %get-tuple-element.45.own_index, s32[8,128]{1,0:T(8,128)S(1)} %get-tuple-element.46.north_index, ...), custom_call_target="tpu_custom_call" | custom-call | tf_op jit(solution)/shard_map/cond/branch_1_fun/couple/pallas_call | solution.py:423
  170.7 0.0 copy-done.3
  170.7 0.1 copy.41
  170.9 0.8 reshape.44.w1_ref
  171.7 0.0 copy-done.4
  171.7 0.1 copy.42
  171.8 0.8 reshape.45.w2_ref
  172.6 9.5 %atmos.1 = bf16[64,64,128]{2,1,0:T(8,128)(2,1)} custom-call(bf16[64,64,128]{2,1,0:T(8,128)(2,1)S(1)} %get-tuple-element.83.a_ref, bf16[2,64,128]{2,1,0:T(8,128)(2,1)} %get-tuple-element.84.top_ref, bf16[2,64,128]{2,1,0:T(8,128)(2,1)} %get-tuple-element.85.bottom_ref, bf16[4,64,128]{2,1,0:T(8,128)(2,1)S(1)} %get-tuple-element.86.left_ref, ...), custom_call_target="tpu_custom_call" | custom-call | tf_op jit(solution)/shard_map/atmos/pallas_call | solution.py:505
  182.1 2.9 %copy.44 = bf16[64,64,128]{2,1,0:T(8,128)(2,1)} copy(bf16[64,64,128]{2,0,1:T(8,128)(2,1)} %bitcast.24) | data formatting | bytes 2097152
  (5 shorter events, 0.1 us)
Async XLA Ops:
  5.8 24.6 %copy-start.1 = (bf16[64,76,3,3]{1,0,3,2:T(8,128)(2,1)S(1)}, bf16[64,76,3,3]{1,0,3,2:T(8,128)(2,1)}, u32[]{:S(2)}) copy-start(bf16[64,76,3,3]{1,0,3,2:T(8,128)(2,1)} %param.20) | copy-start | bytes 262660
  7.4 24.0 %copy-start.2 = (bf16[64,64,3,3]{1,0,3,2:T(8,128)(2,1)S(1)}, bf16[64,64,3,3]{1,0,3,2:T(8,128)(2,1)}, u32[]{:S(2)}) copy-start(bf16[64,64,3,3]{1,0,3,2:T(8,128)(2,1)} %param.22) | copy-start | bytes 221188
  46.2 69.6 %copy-start = (bf16[64,64,128]{2,1,0:T(8,128)(2,1)S(1)}, bf16[64,64,128]{2,1,0:T(8,128)(2,1)}, u32[]{:S(2)}) copy-start(bf16[64,64,128]{2,1,0:T(8,128)(2,1)} %param.27) | copy-start | bytes 3145732
  116.5 54.2 %copy-start.3 = (bf16[64,64,3,3]{1,0,3,2:T(8,128)(2,1)S(1)}, bf16[64,64,3,3]{1,0,3,2:T(8,128)(2,1)}, u32[]{:S(2)}) copy-start(bf16[64,64,3,3]{1,0,3,2:T(8,128)(2,1)} %param.28) | copy-start | bytes 221188
  116.5 55.2 %copy-start.4 = (bf16[64,64,3,3]{1,0,3,2:T(8,128)(2,1)S(1)}, bf16[64,64,3,3]{1,0,3,2:T(8,128)(2,1)}, u32[]{:S(2)}) copy-start(bf16[64,64,3,3]{1,0,3,2:T(8,128)(2,1)} %param.30) | copy-start | bytes 221188

commit v4 on v3

--- a/solution.py
+++ b/solution.py
@@ -80,14 +80,20 @@
     lon_count,
     field,
     index,
+    longest,
     top,
     bottom,
     left,
     right,
     north_index,
     south_index,
+    longest_of_all,
+    gathered,
+    partial,
     send_sem,
     recv_sem,
+    max_send,
+    max_recv,
 ):
     lat, lon = lax.axis_index("lat"), lax.axis_index("lon")
     rows, _, cols = field.shape
@@ -98,7 +104,15 @@
     partners = [(lat, west, always), (lat, east, always)]
     for there, ok in ((lat - 1, up), (lat + 1, down)):
         partners += [(there, side, ok) for side in (west, lon, east)]
-    greet(partners, jnp.where(edge, 5, 8))
+    four, inner = lat // 4, lax.rem(lat, 4)
+    fours = lat_count // 4
+    rounds = [
+        [(lat, lax.rem(lon + k, lon_count)) for k in range(1, lon_count)],
+        [(four * 4 + lax.rem(inner + k, 4), lon) for k in range(1, 4)],
+        [(lax.rem(four + k, fours) * 4 + inner, lon) for k in range(1, fours)],
+    ]
+    partners += [(a, b, always) for peers in rounds for a, b in peers]
+    greet(partners, jnp.where(edge, 5, 8) + sum(len(peers) for peers in rounds))
 
     lo, hi = pl.ds(0, 128), pl.ds(cols - 128, 128)
     first, last = pl.ds(0, 2), pl.ds(rows - 2, 2)
@@ -122,24 +136,48 @@
     ]
     for copy, ok in copies:
         pl.when(ok)(copy.start)
+    held, at, small = longest, 0, []
+    for number, peers in enumerate(rounds):
+        slots = range(at, at + len(peers))
+        for i, (a, b) in zip(slots, peers):
+            small.append(remote(held, gathered.at[i], max_send.at[i], max_recv.at[i], a, b))
+            small[-1].start()
+        value = held[...]
+        for i in slots:
+            landed(gathered.at[i], max_recv.at[i]).wait()
+            value = jnp.maximum(value, gathered[i])
+        held = longest_of_all if number == 2 else partial.at[number]
+        held[...] = value
+        at += len(peers)
+    for copy in small:
+        copy.wait_send()
     for i, (copy, ok) in enumerate(copies):
         pl.when(ok)(copy.wait_send)
         pl.when(arrives[i])(landed(moves[i][1], recv_sem.at[i]).wait)
 
 
-def ocean_halo(field, index, lat_count, lon_count):
+def ocean_halo(field, index, longest, lat_count, lon_count):
     rows, channels, cols = field.shape
     shapes = [(2, channels, cols)] * 2 + [(rows + 4, channels, 128)] * 2
     table = jax.ShapeDtypeStruct(index.shape[1:], jnp.int32)
+    vmem = pl.BlockSpec(memory_space=pltpu.VMEM)
+    peers = lon_count - 1 + 3 + lat_count // 4 - 1
     return pl.pallas_call(
         functools.partial(ocean_halo_kernel, lat_count, lon_count),
-        out_shape=[jax.ShapeDtypeStruct(s, BF16) for s in shapes] + [table] * 2,
-        in_specs=whole_any(2),
-        out_specs=whole_any(6),
-        scratch_shapes=[pltpu.SemaphoreType.DMA((10,))] * 2,
+        out_shape=[jax.ShapeDtypeStruct(s, BF16) for s in shapes] + [table] * 3,
+        in_specs=whole_any(2) + [vmem],
+        out_specs=whole_any(6) + [vmem],
+        scratch_shapes=[
+            pltpu.VMEM((peers, 8, 128), jnp.int32),
+            pltpu.VMEM((2, 8, 128), jnp.int32),
+            pltpu.SemaphoreType.DMA((10,)),
+            pltpu.SemaphoreType.DMA((10,)),
+            pltpu.SemaphoreType.DMA((peers,)),
+            pltpu.SemaphoreType.DMA((peers,)),
+        ],
         compiler_params=pltpu.CompilerParams(collective_id=0, has_side_effects=True),
         name="ocean_halo",
-    )(field, index)
+    )(field, index, longest)
 
 
 def ocean_kernel(
@@ -554,8 +592,6 @@
     longest = jnp.maximum(
         jnp.sum((key < per_step).astype(jnp.int32)), jnp.sum((key >= 2 * per_step).astype(jnp.int32))
     )
-    longest = lax.pmax(longest, ("lat", "lon"))
-    which = sum((longest > n).astype(jnp.int32) for n in LENGTHS if n < count)
     lanes = jnp.arange(8 * 128, dtype=jnp.int32)
     number = jnp.where(lanes < per_step, lanes, -4 * per_step).reshape(1, 8, 128)
     number = number + jnp.arange(3, dtype=jnp.int32)[:, None, None] * per_step
@@ -563,9 +599,10 @@
         jnp.where(number[..., None] == key[None, None, None, :], place[None, None, None, :], count),
         axis=3,
     )
-    top, bottom, left, right, north_index, south_index = ocean_halo(
-        field, index, lat_count, lon_count
-    )
+    top, bottom, left, right, north_index, south_index, longest = ocean_halo(
+        field, index, jnp.full((8, 128), longest, jnp.int32), lat_count, lon_count
+    )
+    which = sum((longest[0, 0] > n).astype(jnp.int32) for n in LENGTHS if n < count)
     ocean_next, slots = ocean_step(
         meta,
         field,

time: 185 us -> 133 us (0.72)
  blocking collectives: 63.6 us -> 0 us
  Pallas kernels: 99.2 us -> 108 us
    pmax x1 -> x0, blocking collectives: 63.6 us -> none  [per_device(): longest = lax.pmax(longest, ('lat', 'lon'))]
    pallas_call x1, Pallas kernels: 21.9 us -> 28.4 us  [ocean_halo(): pl.pallas_call(functools.partial(ocean_halo_kernel, lat_count, lon_count)...]
    pallas_call x1, Pallas kernels: 53.9 us -> 56.4 us  [couple(): pl.pallas_call(functools.partial(couple_kernel, lat_count, lon_count, cou...]
where the time goes in v4:
time: 133 us; the launch traced here: 132 us
  Pallas kernels  108 us (81%)
  local copies, waits for them, and re-layouts  14.3 us (11%)
  other arithmetic  5.48 us (4%)
  between operations  4.01 us (3%)
    pallas_call x1, Pallas kernels, couple(): pl.pallas_call(functools.partial(couple_kernel, lat_count, lon_count, cou...  56.4 us
    pallas_call x1, Pallas kernels, ocean_halo(): pl.pallas_call(functools.partial(ocean_halo_kernel, lat_count, lon_count)...  28.4 us
    pallas_call x1, Pallas kernels, ocean_step(): pl.pallas_call(functools.partial(ocean_kernel, lat_count), out_shape=(jax...  13.9 us
    pallas_call x1, Pallas kernels, atmos_step(): pl.pallas_call(functools.partial(atmos_kernel, lat_count), out_shape=jax....  9.49 us
    unnamed x14, local copies, waits for them, and re-layouts  8.42 us
    reshape x4, local copies, waits for them, and re-layouts, stacked_weight(): return weight.transpose(3, 0, 2, 1).reshape(3 * out, 3 * padded_in)  3.19 us

profile of v4, /device:TPU:3, one launch (start us, length us, event | category | flops | bytes accessed | tf_op | source)
XLA Modules:
  0.0 132.3 jit_solution(1287181538494392188)
XLA Ops:
  0.6 1.3 %fusion.2 = (s32[]{:T(128)}, s32[]{:T(128)}, s32[64,2]{0,1:T(2,128)S(1)}) fusion(s32[64,2]{0,1:T(2,128)} %param.26, s32[64,2]{0,1:T(2,128)} %param.25, s32[]{:T(128)S(6)} %mul.23), kind=kLoop, calls=%fused_computation.14 | loop fusion | flops 1150 | bytes 1548 | tf_op jit(solution)/shard_map/reduce_sum | solution.py:593
  2.0 0.1 copy.35
  2.1 0.1 lt.45
  2.2 0.2 convert_reduce_fusion.1
  2.4 0.5 add_subtract_fusion.meta
  2.9 0.8 convert_bitcast_fusion
  3.7 2.0 %copy.36 = bf16[76,8,1024]{2,0,1:T(8,128)(2,1)S(1)} copy(bf16[76,8,1024]{2,1,0:T(8,128)(2,1)} %param.18) | data formatting | bytes 2490368 | tf_op args[0]
  5.7 0.1 pad.7.clone
  5.8 0.0 copy-start.1
  5.8 1.6 %maximum_bitcast_fusion.field.x_ref = bf16[8,80,1024]{2,1,0:T(8,128)(2,1)} fusion(bf16[1,8,1024]{2,0,1:T(2,128)(2,1)S(1)} %copy.37, bf16[76,8,1024]{2,0,1:T(8,128)(2,1)S(1)} %copy.36, bf16[80]{0:T(256)(128)(2,1)S(1)} %pad.7.clone), kind=kLoop, calls=%fused_computation.1 | loop fusion | flops 3932160 | bytes 2572448 | tf_op jit(solution)/shard_map/transpose | solution.py:584
  7.4 0.0 copy-start.2
  7.4 0.1 broadcast_add_fusion
  7.4 1.0 select_reduce_fusion.index
  9.8 0.6 broadcast_in_dim.47.longest
  10.4 28.4 %ocean_halo.1 = (bf16[2,80,1024]{2,1,0:T(8,128)(2,1)}, bf16[2,80,1024]{2,1,0:T(8,128)(2,1)}, bf16[12,80,128]{2,1,0:T(8,128)(2,1)}, bf16[12,80,128]{2,1,0:T(8,128...) custom-call(bf16[8,80,1024]{2,1,0:T(8,128)(2,1)} %maximum_bitcast_fusion.field.x_ref, ...), custom_call_target="tpu_custom_call" | custom-call | tf_op jit(solution)/shard_map/ocean_halo/pallas_call | solution.py:165
  38.8 0.0 copy-done.1
  38.8 0.1 copy.38
  39.0 0.8 reshape.52.w1_ref
  39.7 0.0 copy-done.2
  39.7 0.1 copy.39
  39.9 0.8 reshape.53.w2_ref
  40.7 13.9 %ocean.1 = (bf16[8,64,1024]{2,1,0:T(8,128)(2,1)}, bf16[4,128,16,128]{3,2,1,0:T(8,128)(2,1)S(1)}) custom-call(s32[128]{0:T(128)} %add_subtract_fusion.meta, bf16[8,80,1024]{2,1,0:T(8,128)(2,1)} %maximum_bitcast_fusion.field.x_ref, bf16[2,80,1024]{2,1,0:T(8,128)(2,1)} %get-tuple-element.76.top_ref, bf16[2,80,1024]{2,1,0:T(8,128)(2,1)} %get-tuple-element.77.bottom_ref, ...), custom_call_target="tpu_custom_call" | custom-call | tf_op jit(solution)/shard_map/ocean/pallas_call | solution.py:270
  54.6 0.0 copy-start
  54.6 2.9 %copy.43 = bf16[64,8,1024]{2,1,0:T(8,128)(2,1)} copy(bf16[64,8,1024]{2,0,1:T(8,128)(2,1)} %bitcast.26) | data formatting | bytes 2097152
  57.5 1.2 slice.2
  60.6 0.0 copy-done
  60.6 0.7 copy.46
  61.3 0.0 copy-start.3
  61.3 0.0 copy-start.4
  61.3 56.7 %conditional.1 = ((bf16[64,64,128]{2,1,0:T(8,128)(2,1)S(1)}, bf16[2,64,128]{2,1,0:T(8,128)(2,1)S(1)}, bf16[2,64,128]{2,1,0:T(8,128)(2,1)S(1)}, bf16[4,64,128]{2,1,0:T(8,128)(2,1)S(1)}, bf16[4,64,128]{2,1,0:T(8,128)(2,1)S(1)})) conditional(s32[]{:T(128)} %bitcast.8, (s32[3,8,128]{2,1,0:T(8,128)S(1)}, ...), branch_computations={%region_5.6_spmd, %region_6.7_spmd, %region_7.8_spmd, %region_8.9_... | conditional | bytes 8 | solution.py:628
  61.3 56.4 %couple.5 = (bf16[64,64,128]{2,1,0:T(8,128)(2,1)S(1)}, bf16[2,64,128]{2,1,0:T(8,128)(2,1)S(1)}, bf16[2,64,128]{2,1,0:T(8,128)(2,1)S(1)}, bf16[4,64,128]{2,1,0:T(8,128)(2,1)S(1)}, bf16[4,64,128]{2,1,0:T(8,128)(2,1)S(1)}) custom-call(s32[3,8,128]{2,1,0:T(8,128)S(1)} %get-tuple-element.45.own_index, s32[8,128]{1,0:T(8,128)S(1)} %get-tuple-element.46.north_index, ...), custom_call_target="tpu_custom_call" | custom-call | tf_op jit(solution)/shard_map/cond/branch_1_fun/couple/pallas_call | solution.py:461
  118.0 0.0 copy-done.3
  118.0 0.1 copy.41
  118.1 0.8 reshape.55.w1_ref
  119.0 0.0 copy-done.4
  119.0 0.1 copy.42
  119.1 0.8 reshape.56.w2_ref
  119.9 9.5 %atmos.1 = bf16[64,64,128]{2,1,0:T(8,128)(2,1)} custom-call(bf16[64,64,128]{2,1,0:T(8,128)(2,1)S(1)} %get-tuple-element.85.a_ref, bf16[2,64,128]{2,1,0:T(8,128)(2,1)S(1)} %get-tuple-element.86.top_ref, bf16[2,64,128]{2,1,0:T(8,128)(2,1)S(1)} %get-tuple-element.87.bottom_ref, bf16[4,64,128]{2,1,0:T(8,128)(2,1)S(1)} %get-tuple-element.88.left_ref, ...), custom_call_target="tpu_custom_call" | custom-call | tf_op jit(solution)/shard_map/atmos/pallas_call | solution.py:543
  129.4 2.9 %copy.44 = bf16[64,64,128]{2,1,0:T(8,128)(2,1)} copy(bf16[64,64,128]{2,0,1:T(8,128)(2,1)} %bitcast.25) | data formatting | bytes 2097152
  (5 shorter events, 0.1 us)
Async XLA Ops:
  5.8 33.0 %copy-start.1 = (bf16[64,76,3,3]{1,0,3,2:T(8,128)(2,1)S(1)}, bf16[64,76,3,3]{1,0,3,2:T(8,128)(2,1)}, u32[]{:S(2)}) copy-start(bf16[64,76,3,3]{1,0,3,2:T(8,128)(2,1)} %param.20) | copy-start | bytes 262660
  7.4 32.4 %copy-start.2 = (bf16[64,64,3,3]{1,0,3,2:T(8,128)(2,1)S(1)}, bf16[64,64,3,3]{1,0,3,2:T(8,128)(2,1)}, u32[]{:S(2)}) copy-start(bf16[64,64,3,3]{1,0,3,2:T(8,128)(2,1)} %param.22) | copy-start | bytes 221188
  54.6 6.0 %copy-start = (bf16[64,64,128]{2,1,0:T(8,128)(2,1)S(1)}, bf16[64,64,128]{2,1,0:T(8,128)(2,1)}, u32[]{:S(2)}) copy-start(bf16[64,64,128]{2,1,0:T(8,128)(2,1)} %param.27) | copy-start | bytes 3145732
  61.3 56.7 %copy-start.3 = (bf16[64,64,3,3]{1,0,3,2:T(8,128)(2,1)S(1)}, bf16[64,64,3,3]{1,0,3,2:T(8,128)(2,1)}, u32[]{:S(2)}) copy-start(bf16[64,64,3,3]{1,0,3,2:T(8,128)(2,1)} %param.28) | copy-start | bytes 221188
  61.3 57.7 %copy-start.4 = (bf16[64,64,3,3]{1,0,3,2:T(8,128)(2,1)S(1)}, bf16[64,64,3,3]{1,0,3,2:T(8,128)(2,1)}, u32[]{:S(2)}) copy-start(bf16[64,64,3,3]{1,0,3,2:T(8,128)(2,1)} %param.30) | copy-start | bytes 221188

commit v5 on v3

--- a/solution.py
+++ b/solution.py
@@ -14,7 +14,7 @@
 GROUPS = 4
 FIRST_ROWS = 11
 LAST_ROWS = 16
-LENGTHS = (32, 48, 64)
+SHORT = 48
 
 
 def silu(v):
@@ -40,7 +40,7 @@
 def column(bias):
     n = bias.shape[1]
     at = lax.broadcasted_iota(jnp.int32, (n, n), 0) == lax.broadcasted_iota(jnp.int32, (n, n), 1)
-    return jnp.sum(jnp.where(at, bias, 0.0), axis=1, keepdims=True)
+    return jnp.sum(jnp.where(at, bias, jnp.zeros_like(bias)), axis=1, keepdims=True)
 
 
 def remote(src, dst, send_sem, recv_sem, lat, lon):
@@ -78,19 +78,24 @@
 def ocean_halo_kernel(
     lat_count,
     lon_count,
+    atmos_rows,
     field,
-    index,
+    key_ref,
     top,
     bottom,
     left,
     right,
+    index,
     north_index,
     south_index,
+    meta,
+    longest,
+    edges,
     send_sem,
     recv_sem,
 ):
     lat, lon = lax.axis_index("lat"), lax.axis_index("lon")
-    rows, _, cols = field.shape
+    rows, channels, cols = field.shape
     west = lax.rem(lon + lon_count - 1, lon_count)
     east = lax.rem(lon + 1, lon_count)
     up, down, always = lat > 0, lat < lat_count - 1, lat >= 0
@@ -98,48 +103,85 @@
     partners = [(lat, west, always), (lat, east, always)]
     for there, ok in ((lat - 1, up), (lat + 1, down)):
         partners += [(there, side, ok) for side in (west, lon, east)]
+
+    key = key_ref[...]
+    count = key.shape[1]
+    key_down = column(key)
+    across = lax.broadcasted_iota(jnp.int32, (count, count), 1)
+    along = lax.broadcasted_iota(jnp.int32, (count, count), 0)
+    place = jnp.sum((key_down < key).astype(jnp.int32), axis=0, keepdims=True)
+    again = jnp.logical_and(key_down == key, along < across).astype(jnp.int32)
+    meta[...] = place * 2 + 1 - jnp.max(again, axis=0, keepdims=True)
+    place_down = column(place)
+    per_step = lon_count * atmos_rows
+    lane = lax.broadcasted_iota(jnp.int32, (1, count), 1)
+    for step in range(3):
+        for row in range(8):
+            if row * count < per_step:
+                number = lane + (step * per_step + row * count)
+                places = jnp.min(
+                    jnp.where(key_down == number, place_down, count), axis=0, keepdims=True
+                )
+                index[step, row : row + 1, :] = places
+            else:
+                index[step, row : row + 1, :] = jnp.full((1, count), count, jnp.int32)
+    low = jnp.sum((key < per_step).astype(jnp.int32), axis=1, keepdims=True)
+    high = jnp.sum((key >= 2 * per_step).astype(jnp.int32), axis=1, keepdims=True)
+    longest[...] = jnp.broadcast_to(jnp.maximum(low, high), longest.shape)
+
+    lane = lax.broadcasted_iota(jnp.int32, (channels, 128), 1)
+    tile = jnp.zeros((channels, 128), F32)
+    for k in range(rows):
+        both = jnp.where(lane < 64, field[k, :, 0:128], field[k, :, cols - 128 :]).astype(F32)
+        tile = jnp.where(lane // 4 == k, pltpu.roll(both, (4 * k + 2) % 128, 1), tile)
+    edges[...] = tile.astype(BF16)
+
     greet(partners, jnp.where(edge, 5, 8))
-
-    lo, hi = pl.ds(0, 128), pl.ds(cols - 128, 128)
-    first, last = pl.ds(0, 2), pl.ds(rows - 2, 2)
-    own, above, below = pl.ds(2, rows), pl.ds(0, 2), pl.ds(rows + 2, 2)
     moves = [
-        (field.at[:, :, lo], right.at[own], lat, west, always),
-        (field.at[:, :, hi], left.at[own], lat, east, always),
-        (field.at[first], bottom, lat - 1, lon, up),
-        (field.at[last], top, lat + 1, lon, down),
-        (field.at[first, :, lo], right.at[below], lat - 1, west, up),
-        (field.at[first, :, hi], left.at[below], lat - 1, east, up),
-        (field.at[last, :, lo], right.at[above], lat + 1, west, down),
-        (field.at[last, :, hi], left.at[above], lat + 1, east, down),
-        (index.at[0], south_index, lat - 1, lon, up),
-        (index.at[2], north_index, lat + 1, lon, down),
+        (field.at[pl.ds(0, 2)], bottom, lat - 1, lon, up, down),
+        (field.at[pl.ds(rows - 2, 2)], top, lat + 1, lon, down, up),
+        (edges, right.at[1], lat, west, always, always),
+        (edges, left.at[1], lat, east, always, always),
+        (edges, right.at[2], lat - 1, west, up, down),
+        (edges, left.at[2], lat - 1, east, up, down),
+        (edges, right.at[0], lat + 1, west, down, up),
+        (edges, left.at[0], lat + 1, east, down, up),
+        (index.at[0], south_index, lat - 1, lon, up, down),
+        (index.at[2], north_index, lat + 1, lon, down, up),
     ]
-    arrives = [always, always, down, up, down, down, up, up, down, up]
     copies = [
-        (remote(src, dst, send_sem.at[i], recv_sem.at[i], a, b), ok)
-        for i, (src, dst, a, b, ok) in enumerate(moves)
+        remote(src, dst, send_sem.at[i], recv_sem.at[i], a, b)
+        for i, (src, dst, a, b, _, _) in enumerate(moves)
     ]
-    for copy, ok in copies:
-        pl.when(ok)(copy.start)
-    for i, (copy, ok) in enumerate(copies):
-        pl.when(ok)(copy.wait_send)
-        pl.when(arrives[i])(landed(moves[i][1], recv_sem.at[i]).wait)
-
-
-def ocean_halo(field, index, lat_count, lon_count):
+    for copy, move in zip(copies, moves):
+        pl.when(move[4])(copy.start)
+    for i, (copy, move) in enumerate(zip(copies, moves)):
+        pl.when(move[4])(copy.wait_send)
+        pl.when(move[5])(landed(move[1], recv_sem.at[i]).wait)
+
+
+def ocean_halo(field, key, lat_count, lon_count, atmos_rows):
     rows, channels, cols = field.shape
-    shapes = [(2, channels, cols)] * 2 + [(rows + 4, channels, 128)] * 2
-    table = jax.ShapeDtypeStruct(index.shape[1:], jnp.int32)
+    shapes = [(2, channels, cols)] * 2 + [(3, channels, 128)] * 2
+    table = jax.ShapeDtypeStruct((8, key.shape[1]), jnp.int32)
+    vmem = pl.BlockSpec(memory_space=pltpu.VMEM)
     return pl.pallas_call(
-        functools.partial(ocean_halo_kernel, lat_count, lon_count),
-        out_shape=[jax.ShapeDtypeStruct(s, BF16) for s in shapes] + [table] * 2,
-        in_specs=whole_any(2),
-        out_specs=whole_any(6),
-        scratch_shapes=[pltpu.SemaphoreType.DMA((10,))] * 2,
-        compiler_params=pltpu.CompilerParams(collective_id=0, has_side_effects=True),
+        functools.partial(ocean_halo_kernel, lat_count, lon_count, atmos_rows),
+        out_shape=[jax.ShapeDtypeStruct(s, BF16) for s in shapes]
+        + [jax.ShapeDtypeStruct((3,) + table.shape, jnp.int32), table, table]
+        + [jax.ShapeDtypeStruct(key.shape, jnp.int32), table],
+        in_specs=[vmem] * 2,
+        out_specs=whole_any(4) + [vmem] + whole_any(2) + [vmem] * 2,
+        scratch_shapes=[
+            pltpu.VMEM((channels, 128), BF16),
+            pltpu.SemaphoreType.DMA((10,)),
+            pltpu.SemaphoreType.DMA((10,)),
+        ],
+        compiler_params=pltpu.CompilerParams(
+            collective_id=0, has_side_effects=True, vmem_limit_bytes=VMEM_LIMIT
+        ),
         name="ocean_halo",
-    )(field, index)
+    )(field, key)
 
 
 def ocean_kernel(
@@ -177,14 +219,19 @@
         lat = lax.axis_index("lat")
         lane = lax.broadcasted_iota(jnp.int32, (channels, 128), 1)
         tall[2 : 2 + rows, :, 0:cols] = x_ref[...]
-        for j in range(rows + 4):
-            side = jnp.where(lane < 64, right_ref[j], left_ref[j])
-            if j < 2 or j >= rows + 2:
-                inside = lat > 0 if j < 2 else lat < lat_count - 1
-                main = top_ref[j] if j < 2 else bottom_ref[j - rows - 2]
-                tall[j, :, 0:cols] = jnp.where(inside, main, jnp.zeros_like(main))
-                side = jnp.where(inside, side, jnp.zeros_like(side))
-            tall[j, :, cols:] = side
+        for tile in range(3):
+            both = jnp.where(lane % 4 < 2, left_ref[tile], right_ref[tile]).astype(F32)
+            for k in range(rows):
+                j = (tile - 1) * rows + k + 2
+                if j < 0 or j >= rows + 4:
+                    continue
+                side = pltpu.roll(both, (126 - 4 * k) % 128, 1).astype(BF16)
+                if tile != 1:
+                    inside = lat > 0 if tile == 0 else lat < lat_count - 1
+                    main = top_ref[j] if tile == 0 else bottom_ref[j - rows - 2]
+                    tall[j, :, 0:cols] = jnp.where(inside, main, jnp.zeros_like(main))
+                    side = jnp.where(inside, side, jnp.zeros_like(side))
+                tall[j, :, cols:] = side
         first_conv(0)
         first_conv(1)
 
@@ -201,7 +248,7 @@
             field, regrid_ref[q], (((1,), (1,)), ((), ())), preferred_element_type=F32
         ).astype(BF16)
         for k in range(2):
-            what = meta[(row * blocks + q) * 2 + k]
+            what = meta[0, (row * blocks + q) * 2 + k]
             at = what // 2
             value = both[:, k * 128 : (k + 1) * 128].astype(F32)
             sums[at] = jnp.where(lax.rem(what, 2) == 1, value, sums[at] + value)
@@ -222,7 +269,7 @@
     rows, channels, cols = x.shape
     wide = cols + 128
     out = w2.shape[0] // 3
-    slots = meta.shape[0]
+    slots = meta.shape[1]
 
     def whole(array):
         zeros = (0,) * array.ndim
@@ -264,11 +311,13 @@
     south_index,
     slots,
     atmos,
+    longest,
     first,
     top,
     bottom,
     left,
     right,
+    longest_of_all,
     *scratch,
 ):
     lat, lon = lax.axis_index("lat"), lax.axis_index("lon")
@@ -282,15 +331,43 @@
     partners = [(lat, there, always) for there in (west, east, across)]
     for there, ok in ((lat - 1, up), (lat + 1, down)):
         partners += [(there, side, ok) for side in (west, lon, east)]
-    greet(partners, jnp.where(edge, 6, 9))
+    four, inner = lat // 4, lax.rem(lat, 4)
+    fours = lat_count // 4
+    rounds = [
+        [(lat, lax.rem(lon + k, lon_count)) for k in range(1, lon_count)],
+        [(four * 4 + lax.rem(inner + k, 4), lon) for k in range(1, 4)],
+        [(lax.rem(four + k, fours) * 4 + inner, lon) for k in range(1, fours)],
+    ]
+    partners += [(a, b, always) for peers in rounds[1:] for a, b in peers]
+    greet(partners, jnp.where(edge, 6, 9) + sum(len(peers) for peers in rounds[1:]))
 
     groups, total, size, cols = slots.shape
     rows, channels = first.shape[:2]
     own, north, south = (scratch[i * groups : (i + 1) * groups] for i in range(3))
     away, mine, from_core, to_z, from_z, edges = scratch[3 * groups : 3 * groups + 6]
     load_sem, y_send, y_recv, core_send, core_recv, z_send, z_recv, halo_send, halo_recv = scratch[
-        3 * groups + 6 :
+        3 * groups + 6 : 3 * groups + 15
     ]
+    gathered, partial, max_send, max_recv = scratch[3 * groups + 15 :]
+    held, waiting, small = longest, [], []
+
+    def send_maximum(number):
+        begin = sum(len(peers) for peers in rounds[:number])
+        for i, (a, b) in enumerate(rounds[number], begin):
+            small.append(remote(held, gathered.at[i], max_send.at[i], max_recv.at[i], a, b))
+            small[-1].start()
+            waiting.append(i)
+
+    def receive_maximum(target):
+        value = held[...]
+        for i in waiting:
+            landed(gathered.at[i], max_recv.at[i]).wait()
+            value = jnp.maximum(value, gathered[i])
+        waiting.clear()
+        target[...] = value
+        return target
+
+    send_maximum(0)
     low, high = pl.ds(0, count), pl.ds(total - count, count)
     everything = pl.ds(0, total)
     to_south, to_north, loads = [], [], []
@@ -361,6 +438,9 @@
                 )
                 copy.start()
                 z_copies.append(copy)
+        if g < 2:
+            held = receive_maximum(partial.at[g])
+            send_maximum(g + 1)
 
     lane = lax.broadcasted_iota(jnp.int32, (size, cols), 1)
     tiles = edges.shape[0]
@@ -399,7 +479,8 @@
     ]
     for copy, move in zip(copies, moves):
         pl.when(move[4])(copy.start)
-    for copy in core_copies + z_copies:
+    receive_maximum(longest_of_all)
+    for copy in core_copies + z_copies + small:
         copy.wait_send()
     for g in range(groups):
         pl.when(down)(to_south[g].wait_send)
@@ -409,7 +490,9 @@
         pl.when(move[5])(landed(move[1], halo_recv.at[i]).wait)
 
 
-def couple(index, north_index, south_index, slots, atmos, count, collective_id, lat_count, lon_count):
+def couple(
+    index, north_index, south_index, slots, atmos, longest, count, collective_id, lat_count, lon_count
+):
     groups, total, size, cols = slots.shape
     rows, channels, cols = atmos.shape
     tiles = rows // 32
@@ -418,13 +501,15 @@
     dma = pltpu.SemaphoreType.DMA
     shapes = [(rows, channels, cols)] + [(2, channels, cols)] * 2 + [(tiles + 2, channels, cols)] * 2
     received = pltpu.VMEM((total + 1, size, cols), BF16)
+    peers = lon_count - 1 + 3 + lat_count // 4 - 1
     one = pltpu.VMEM((groups, rows, size, cols), BF16)
     two = pltpu.VMEM((2, groups, rows, size, cols), BF16)
     return pl.pallas_call(
         functools.partial(couple_kernel, lat_count, lon_count, count),
-        out_shape=[jax.ShapeDtypeStruct(s, BF16) for s in shapes],
-        in_specs=[smem] * 3 + whole_any(1) + [vmem],
-        out_specs=[vmem] + whole_any(4),
+        out_shape=[jax.ShapeDtypeStruct(s, BF16) for s in shapes]
+        + [jax.ShapeDtypeStruct(longest.shape, jnp.int32)],
+        in_specs=[smem] * 3 + whole_any(1) + [vmem] * 2,
+        out_specs=[vmem] + whole_any(4) + [vmem],
         scratch_shapes=[received] * (3 * groups)
         + [two] * 3
         + [one] * 2
@@ -432,12 +517,15 @@
         + [dma((groups,))]
         + [dma((2, groups))] * 4
         + [dma((groups,))] * 2
-        + [dma((8,))] * 2,
+        + [dma((8,))] * 2
+        + [pltpu.VMEM((peers,) + longest.shape, jnp.int32)]
+        + [pltpu.VMEM((2,) + longest.shape, jnp.int32)]
+        + [dma((peers,))] * 2,
         compiler_params=pltpu.CompilerParams(
             collective_id=collective_id, has_side_effects=True, vmem_limit_bytes=VMEM_LIMIT
         ),
         name="couple",
-    )(index, north_index, south_index, slots, atmos)
+    )(index, north_index, south_index, slots, atmos, longest)
 
 
 def atmos_kernel(
@@ -544,27 +632,10 @@
         ],
         axis=0,
     ).transpose(1, 0, 2)
-    key = ((route_dev - (lat - 1) * lon_count) * atmos_rows + route_row).reshape(-1)
-    count = key.shape[0]
-    order = jnp.arange(count, dtype=jnp.int32)
-    place = jnp.sum((key[None, :] < key[:, None]).astype(jnp.int32), axis=1)
-    again = (key[None, :] == key[:, None]) & (order[None, :] < order[:, None])
-    meta = place * 2 + 1 - jnp.max(again.astype(jnp.int32), axis=1)
-    per_step = lon_count * atmos_rows
-    longest = jnp.maximum(
-        jnp.sum((key < per_step).astype(jnp.int32)), jnp.sum((key >= 2 * per_step).astype(jnp.int32))
-    )
-    longest = lax.pmax(longest, ("lat", "lon"))
-    which = sum((longest > n).astype(jnp.int32) for n in LENGTHS if n < count)
-    lanes = jnp.arange(8 * 128, dtype=jnp.int32)
-    number = jnp.where(lanes < per_step, lanes, -4 * per_step).reshape(1, 8, 128)
-    number = number + jnp.arange(3, dtype=jnp.int32)[:, None, None] * per_step
-    index = jnp.min(
-        jnp.where(number[..., None] == key[None, None, None, :], place[None, None, None, :], count),
-        axis=3,
-    )
-    top, bottom, left, right, north_index, south_index = ocean_halo(
-        field, index, lat_count, lon_count
+    key = ((route_dev - (lat - 1) * lon_count) * atmos_rows + route_row).reshape(1, -1)
+    count = key.shape[1]
+    top, bottom, left, right, index, north_index, south_index, meta, longest = ocean_halo(
+        field, key, lat_count, lon_count, atmos_rows
     )
     ocean_next, slots = ocean_step(
         meta,
@@ -580,22 +651,14 @@
         regrid_weight.reshape(-1, 256, 128),
         lat_count,
     )
-    lengths = [n for n in LENGTHS if n < count] + [count]
-
-    def coupled(at):
-        def branch(*operands):
-            return tuple(couple(*operands, lengths[at], 1 + at, lat_count, lon_count))
-
-        return branch
-
-    first, top, bottom, left, right = lax.switch(
-        which,
-        [coupled(at) for at in range(len(lengths))],
-        index,
-        north_index,
-        south_index,
-        slots,
-        atmos_state.transpose(1, 0, 2),
+    operands = (index, north_index, south_index, slots, atmos_state.transpose(1, 0, 2), longest)
+    *coupled, longest = couple(*operands, SHORT, 1, lat_count, lon_count)
+    first, top, bottom, left, right = lax.cond(
+        longest[0, 0] > SHORT,
+        lambda short, operands: tuple(couple(*operands, count, 2, lat_count, lon_count)[:5]),
+        lambda short, operands: short,
+        tuple(coupled),
+        operands,
     )
     atmos_next = atmos_step(
         first,

time: 185 us -> 118 us (0.64)
  blocking collectives: 63.6 us -> 0 us
  other arithmetic: 5.5 us -> 2.35 us
  between operations: 3.96 us -> 1.39 us
  local copies, waits for them, and re-layouts: 12.5 us -> 14.9 us
    pmax x1 -> x0, blocking collectives: 63.6 us -> none  [per_device(): longest = lax.pmax(longest, ('lat', 'lon'))]
    pallas_call x1, Pallas kernels: 21.9 us -> 19.8 us  [ocean_halo(): pl.pallas_call(functools.partial(ocean_halo_kernel, lat_count, lon_count,...]
    unnamed x14 -> x18, local copies, waits for them, and re-layouts: 8.42 us -> 9.08 us
where the time goes in v5:
time: 118 us; the launch traced here: 117 us
  Pallas kernels  98.6 us (84%)
  local copies, waits for them, and re-layouts  14.9 us (13%)
  other arithmetic  2.35 us (2%)
  between operations  1.39 us (1%)
    pallas_call x1, Pallas kernels, couple(): pl.pallas_call(functools.partial(couple_kernel, lat_count, lon_count, cou...  55.7 us
    pallas_call x1, Pallas kernels, ocean_halo(): pl.pallas_call(functools.partial(ocean_halo_kernel, lat_count, lon_count,...  19.8 us
    pallas_call x1, Pallas kernels, ocean_step(): pl.pallas_call(functools.partial(ocean_kernel, lat_count), out_shape=(jax...  13.7 us
    pallas_call x1, Pallas kernels, atmos_step(): pl.pallas_call(functools.partial(atmos_kernel, lat_count), out_shape=jax....  9.47 us
    unnamed x18, local copies, waits for them, and re-layouts  9.08 us
    reshape x4, local copies, waits for them, and re-layouts, stacked_weight(): return weight.transpose(3, 0, 2, 1).reshape(3 * out, 3 * padded_in)  3.18 us

profile of v5, /device:TPU:3, one launch (start us, length us, event | category | flops | bytes accessed | tf_op | source)
XLA Modules:
  0.0 117.5 jit_solution(4807499896064384306)
XLA Ops:
  0.6 0.8 convert_bitcast_fusion
  1.4 2.0 %copy.25 = bf16[76,8,1024]{2,0,1:T(8,128)(2,1)S(1)} copy(bf16[76,8,1024]{2,1,0:T(8,128)(2,1)} %param.16) | data formatting | bytes 2490368 | tf_op args[0]
  3.4 0.1 pad.7.clone
  3.5 0.0 copy-start.5
  3.5 0.0 copy-start.6
  3.5 1.6 %maximum_bitcast_fusion.field.x_ref = bf16[8,80,1024]{2,1,0:T(8,128)(2,1)} fusion(bf16[1,8,1024]{2,0,1:T(2,128)(2,1)S(1)} %copy.26, bf16[76,8,1024]{2,0,1:T(8,128)(2,1)S(1)} %copy.25, bf16[80]{0:T(256)(128)(2,1)S(1)} %pad.7.clone), kind=kLoop, calls=%fused_computation | loop fusion | flops 3932160 | bytes 2572448 | tf_op jit(solution)/shard_map/transpose | solution.py:634
  5.1 0.0 copy-start.1
  5.1 0.0 copy-start.2
  5.1 0.0 copy-done.5
  5.1 0.0 copy-done.6
  5.1 0.1 copy.27
  5.2 0.7 reshape.26.key_ref
  5.9 19.8 %ocean_halo.1 = (bf16[2,80,1024]{2,1,0:T(8,128)(2,1)}, bf16[2,80,1024]{2,1,0:T(8,128)(2,1)}, bf16[3,80,128]{2,1,0:T(8,128)(2,1)}, bf16[3,80,128]{2,1,0:T(8,128)(...) custom-call(bf16[8,80,1024]{2,1,0:T(8,128)(2,1)} %maximum_bitcast_fu, ...), custom_call_target="tpu_custom_call" | custom-call | tf_op jit(solution)/shard_map/ocean_halo/pallas_call | solution.py:168
  25.6 0.0 copy-done.1
  25.7 0.1 copy.28
  25.8 0.8 reshape.27.w1_ref
  26.6 0.0 copy-done.2
  26.6 0.1 copy.29
  26.8 0.8 reshape.28.w2_ref
  27.6 13.7 %ocean.1 = (bf16[8,64,1024]{2,1,0:T(8,128)(2,1)}, bf16[4,128,16,128]{3,2,1,0:T(8,128)(2,1)S(1)}) custom-call(s32[1,128]{1,0:T(1,128)} %get-tuple-element.57.meta, bf16[8,80,1024]{2,1,0:T(8,128)(2,1)} %maximum_bitcast_fusion.field.x_ref, bf16[2,80,1024]{2,1,0:T(8,128)(2,1)} %get-tuple-element.58.top_ref, bf16[2,80,1024]{2,1,0:T(8,128)(2,1)} %get-tuple-element.59.bottom_ref, ...), custom_call_target="tpu_custom_call" | custom-call | tf_op jit(solution)/shard_map/ocean/pallas_call | solution.py:279
  41.3 0.0 copy-start
  41.3 2.9 %copy.33 = bf16[64,8,1024]{2,1,0:T(8,128)(2,1)} copy(bf16[64,8,1024]{2,0,1:T(8,128)(2,1)} %bitcast.24) | data formatting | bytes 2097152
  44.1 0.0 copy-done
  44.1 0.7 copy.36
  44.8 55.7 %couple.3 = (bf16[64,64,128]{2,1,0:T(8,128)(2,1)S(1)}, bf16[2,64,128]{2,1,0:T(8,128)(2,1)S(1)}, bf16[2,64,128]{2,1,0:T(8,128)(2,1)S(1)}, bf16[4,64,128]{2,1,0:T(...) custom-call(s32[3,8,128]{2,1,0:T(8,128)S(1)} %get-tuple-element.63.own_index, ...), custom_call_target="tpu_custom_call" | custom-call | tf_op jit(solution)/shard_map/couple/pallas_call | solution.py:507
  100.5 1.2 %slice.3 = s32[1,1]{1,0:T(1,128)} slice(s32[8,128]{1,0:T(8,128)} %get-tuple-element.68), slice={[0:1], [0:1]} | slice | bytes 8 | tf_op jit(solution)/shard_map/slice | solution.py:657
  102.3 0.0 copy-start.3
  102.3 0.0 copy-start.4
  102.4 0.2 conditional.1
  102.6 0.7 copy-done.3
  103.3 0.1 copy.31
  103.4 0.8 reshape.30.w1_ref
  104.2 0.0 copy-done.4
  104.2 0.1 copy.32
  104.3 0.8 reshape.31.w2_ref
  105.1 9.5 %atmos.1 = bf16[64,64,128]{2,1,0:T(8,128)(2,1)} custom-call(bf16[64,64,128]{2,1,0:T(8,128)(2,1)S(1)} %get-tuple-element.74.a_ref, bf16[2,64,128]{2,1,0:T(8,128)(2,1)S(1)} %get-tuple-element.75.top_ref, bf16[2,64,128]{2,1,0:T(8,128)(2,1)S(1)} %get-tuple-element.76.bottom_ref, bf16[4,64,128]{2,1,0:T(8,128)(2,1)S(1)} %get-tuple-element.77.left_ref, ...), custom_call_target="tpu_custom_call" | custom-call | tf_op jit(solution)/shard_map/atmos/pallas_call | solution.py:593
  114.6 2.9 %copy.34 = bf16[64,64,128]{2,1,0:T(8,128)(2,1)} copy(bf16[64,64,128]{2,0,1:T(8,128)(2,1)} %bitcast.23) | data formatting | bytes 2097152
  (4 shorter events, 0.1 us)
Async XLA Ops:
  3.5 1.6 %copy-start.5 = (s32[64,2]{0,1:T(2,128)S(1)}, s32[64,2]{0,1:T(2,128)}, u32[]{:S(2)}) copy-start(s32[64,2]{0,1:T(2,128)} %param.24) | copy-start | bytes 1540
  3.5 1.6 %copy-start.6 = (s32[64,2]{0,1:T(2,128)S(1)}, s32[64,2]{0,1:T(2,128)}, u32[]{:S(2)}) copy-start(s32[64,2]{0,1:T(2,128)} %param.23) | copy-start | bytes 1540
  5.1 20.6 %copy-start.1 = (bf16[64,76,3,3]{1,0,3,2:T(8,128)(2,1)S(1)}, bf16[64,76,3,3]{1,0,3,2:T(8,128)(2,1)}, u32[]{:S(2)}) copy-start(bf16[64,76,3,3]{1,0,3,2:T(8,128)(2,1)} %param.18) | copy-start | bytes 262660
  5.1 21.5 %copy-start.2 = (bf16[64,64,3,3]{1,0,3,2:T(8,128)(2,1)S(1)}, bf16[64,64,3,3]{1,0,3,2:T(8,128)(2,1)}, u32[]{:S(2)}) copy-start(bf16[64,64,3,3]{1,0,3,2:T(8,128)(2,1)} %param.20) | copy-start | bytes 221188
  41.3 2.9 %copy-start = (bf16[64,64,128]{2,1,0:T(8,128)(2,1)S(1)}, bf16[64,64,128]{2,1,0:T(8,128)(2,1)}, u32[]{:S(2)}) copy-start(bf16[64,64,128]{2,1,0:T(8,128)(2,1)} %param.25) | copy-start | bytes 3145732
  102.3 0.9 copy-start.3
  102.3 1.8 %copy-start.4 = (bf16[64,64,3,3]{1,0,3,2:T(8,128)(2,1)S(1)}, bf16[64,64,3,3]{1,0,3,2:T(8,128)(2,1)}, u32[]{:S(2)}) copy-start(bf16[64,64,3,3]{1,0,3,2:T(8,128)(2,1)} %param.28) | copy-start | bytes 221188

commit v6 on v5

--- a/solution.py
+++ b/solution.py
@@ -14,7 +14,8 @@
 GROUPS = 4
 FIRST_ROWS = 11
 LAST_ROWS = 16
-SHORT = 48
+SHORT = 32
+EDGE_SHORT = 48
 
 
 def silu(v):
@@ -31,10 +32,16 @@
     )
 
 
-def stacked_weight(weight, padded_in):
-    out, inn = weight.shape[:2]
-    weight = jnp.pad(weight, ((0, 0), (0, padded_in - inn), (0, 0), (0, 0)))
-    return weight.transpose(3, 0, 2, 1).reshape(3 * out, 3 * padded_in)
+def stack_weight(weight_ref, out_ref):
+    out, inn = weight_ref.shape[2:]
+    padded = out_ref.shape[1] // 3
+    for dc in range(3):
+        pieces = []
+        for dr in range(3):
+            pieces.append(weight_ref[dr, dc].astype(F32))
+            if padded > inn:
+                pieces.append(jnp.zeros((out, padded - inn), F32))
+        out_ref[dc * out : (dc + 1) * out, :] = jnp.concatenate(pieces, axis=1).astype(BF16)
 
 
 def column(bias):
@@ -58,7 +65,7 @@
     return pltpu.make_async_copy(ref, ref, sem)
 
 
-def greet(partners, waits):
+def greet(partners):
     barrier = pltpu.get_barrier_semaphore()
     for lat, lon, ok in partners:
 
@@ -68,7 +75,9 @@
                 barrier, inc=1, device_id={"lat": lat, "lon": lon}, device_id_type=MESH
             )
 
-    pl.semaphore_wait(barrier, waits)
+
+def greeted(waits):
+    pl.semaphore_wait(pltpu.get_barrier_semaphore(), waits)
 
 
 def whole_any(count):
@@ -80,7 +89,12 @@
     lon_count,
     atmos_rows,
     field,
-    key_ref,
+    dev_ref,
+    row_ref,
+    w1_ref,
+    w2_ref,
+    w3_ref,
+    w4_ref,
     top,
     bottom,
     left,
@@ -89,7 +103,11 @@
     north_index,
     south_index,
     meta,
-    longest,
+    overflow,
+    w1_out,
+    w2_out,
+    w3_out,
+    w4_out,
     edges,
     send_sem,
     recv_sem,
@@ -103,12 +121,17 @@
     partners = [(lat, west, always), (lat, east, always)]
     for there, ok in ((lat - 1, up), (lat + 1, down)):
         partners += [(there, side, ok) for side in (west, lon, east)]
-
-    key = key_ref[...]
+    greet(partners)
+
+    keys = (dev_ref[...] - (lat - 1) * lon_count) * atmos_rows + row_ref[...]
+    key = jnp.concatenate([keys[k : k + 1] for k in range(keys.shape[0])], axis=1)
     count = key.shape[1]
     key_down = column(key)
+    blocks = keys.shape[1]
     across = lax.broadcasted_iota(jnp.int32, (count, count), 1)
+    across = lax.rem(across, blocks) * keys.shape[0] + lax.div(across, blocks)
     along = lax.broadcasted_iota(jnp.int32, (count, count), 0)
+    along = lax.rem(along, blocks) * keys.shape[0] + lax.div(along, blocks)
     place = jnp.sum((key_down < key).astype(jnp.int32), axis=0, keepdims=True)
     again = jnp.logical_and(key_down == key, along < across).astype(jnp.int32)
     meta[...] = place * 2 + 1 - jnp.max(again, axis=0, keepdims=True)
@@ -127,7 +150,9 @@
                 index[step, row : row + 1, :] = jnp.full((1, count), count, jnp.int32)
     low = jnp.sum((key < per_step).astype(jnp.int32), axis=1, keepdims=True)
     high = jnp.sum((key >= 2 * per_step).astype(jnp.int32), axis=1, keepdims=True)
-    longest[...] = jnp.broadcast_to(jnp.maximum(low, high), longest.shape)
+    most = jnp.where(edge, EDGE_SHORT, SHORT)
+    long = (jnp.maximum(low, high) > most).astype(jnp.int32)
+    overflow[...] = jnp.broadcast_to(long, overflow.shape)
 
     lane = lax.broadcasted_iota(jnp.int32, (channels, 128), 1)
     tile = jnp.zeros((channels, 128), F32)
@@ -136,7 +161,7 @@
         tile = jnp.where(lane // 4 == k, pltpu.roll(both, (4 * k + 2) % 128, 1), tile)
     edges[...] = tile.astype(BF16)
 
-    greet(partners, jnp.where(edge, 5, 8))
+    greeted(jnp.where(edge, 5, 8))
     moves = [
         (field.at[pl.ds(0, 2)], bottom, lat - 1, lon, up, down),
         (field.at[pl.ds(rows - 2, 2)], top, lat + 1, lon, down, up),
@@ -155,23 +180,31 @@
     ]
     for copy, move in zip(copies, moves):
         pl.when(move[4])(copy.start)
+    for weight, out in ((w1_ref, w1_out), (w2_ref, w2_out), (w3_ref, w3_out), (w4_ref, w4_out)):
+        stack_weight(weight, out)
     for i, (copy, move) in enumerate(zip(copies, moves)):
         pl.when(move[4])(copy.wait_send)
         pl.when(move[5])(landed(move[1], recv_sem.at[i]).wait)
 
 
-def ocean_halo(field, key, lat_count, lon_count, atmos_rows):
+def ocean_halo(field, route_dev, route_row, weights, lat_count, lon_count, atmos_rows):
     rows, channels, cols = field.shape
+    count = route_dev.size
+    weights = [w.transpose(2, 3, 0, 1) for w in weights]
+    stacked = [
+        jax.ShapeDtypeStruct((3 * w.shape[2], 3 * (-(-w.shape[3] // 16) * 16)), BF16) for w in weights
+    ]
     shapes = [(2, channels, cols)] * 2 + [(3, channels, 128)] * 2
-    table = jax.ShapeDtypeStruct((8, key.shape[1]), jnp.int32)
+    table = jax.ShapeDtypeStruct((8, count), jnp.int32)
     vmem = pl.BlockSpec(memory_space=pltpu.VMEM)
     return pl.pallas_call(
         functools.partial(ocean_halo_kernel, lat_count, lon_count, atmos_rows),
         out_shape=[jax.ShapeDtypeStruct(s, BF16) for s in shapes]
         + [jax.ShapeDtypeStruct((3,) + table.shape, jnp.int32), table, table]
-        + [jax.ShapeDtypeStruct(key.shape, jnp.int32), table],
-        in_specs=[vmem] * 2,
-        out_specs=whole_any(4) + [vmem] + whole_any(2) + [vmem] * 2,
+        + [jax.ShapeDtypeStruct((1, count), jnp.int32), table]
+        + stacked,
+        in_specs=[vmem] * 7,
+        out_specs=whole_any(4) + [vmem] + whole_any(2) + [vmem] * 6,
         scratch_shapes=[
             pltpu.VMEM((channels, 128), BF16),
             pltpu.SemaphoreType.DMA((10,)),
@@ -181,7 +214,7 @@
             collective_id=0, has_side_effects=True, vmem_limit_bytes=VMEM_LIMIT
         ),
         name="ocean_halo",
-    )(field, key)
+    )(field, route_dev.T, route_row.T, *weights)
 
 
 def ocean_kernel(
@@ -248,7 +281,7 @@
             field, regrid_ref[q], (((1,), (1,)), ((), ())), preferred_element_type=F32
         ).astype(BF16)
         for k in range(2):
-            what = meta[0, (row * blocks + q) * 2 + k]
+            what = meta[0, k * (rows * blocks) + row * blocks + q]
             at = what // 2
             value = both[:, k * 128 : (k + 1) * 128].astype(F32)
             sums[at] = jnp.where(lax.rem(what, 2) == 1, value, sums[at] + value)
@@ -306,18 +339,19 @@
     lat_count,
     lon_count,
     count,
+    edge_count,
     own_index,
     north_index,
     south_index,
     slots,
     atmos,
-    longest,
+    overflow,
     first,
     top,
     bottom,
     left,
     right,
-    longest_of_all,
+    overflow_of_all,
     *scratch,
 ):
     lat, lon = lax.axis_index("lat"), lax.axis_index("lon")
@@ -339,7 +373,7 @@
         [(lax.rem(four + k, fours) * 4 + inner, lon) for k in range(1, fours)],
     ]
     partners += [(a, b, always) for peers in rounds[1:] for a, b in peers]
-    greet(partners, jnp.where(edge, 6, 9) + sum(len(peers) for peers in rounds[1:]))
+    greet(partners)
 
     groups, total, size, cols = slots.shape
     rows, channels = first.shape[:2]
@@ -349,7 +383,7 @@
         3 * groups + 6 : 3 * groups + 15
     ]
     gathered, partial, max_send, max_recv = scratch[3 * groups + 15 :]
-    held, waiting, small = longest, [], []
+    held, waiting, small = overflow, [], []
 
     def send_maximum(number):
         begin = sum(len(peers) for peers in rounds[:number])
@@ -367,30 +401,58 @@
         target[...] = value
         return target
 
-    send_maximum(0)
-    low, high = pl.ds(0, count), pl.ds(total - count, count)
     everything = pl.ds(0, total)
-    to_south, to_north, loads = [], [], []
+    loads = []
     for g in range(groups):
-        to_south.append(
-            remote(
-                slots.at[g, high], north[g].at[high], y_send.at[0, g], y_recv.at[0, g], lat + 1, lon
-            )
-        )
-        to_north.append(
-            remote(
-                slots.at[g, low], south[g].at[low], y_send.at[1, g], y_recv.at[1, g], lat - 1, lon
-            )
-        )
         loads.append(
             pltpu.make_async_copy(slots.at[g], own[g].at[everything], load_sem.at[g])
         )
-        pl.when(down)(to_south[g].start)
-        pl.when(up)(to_north[g].start)
         loads[g].start()
     for buffer in (own, north, south):
         for g in range(groups):
             buffer[g][total] = jnp.zeros((size, cols), BF16)
+    greeted(jnp.where(edge, 6, 9) + sum(len(peers) for peers in rounds[1:]))
+    send_maximum(0)
+
+    last = lat_count - 1
+    lists = []
+    for g in range(groups):
+        lists.append([])
+        for length, sends_down, sends_up, north_comes, south_comes in (
+            (count, lat > 0, lat < last, lat > 1, lat < last - 1),
+            (edge_count, lat == 0, lat == last, lat == 1, lat == last - 1),
+        ):
+            low, high = pl.ds(0, length), pl.ds(total - length, length)
+            lists[g] += [
+                (
+                    remote(
+                        slots.at[g, high],
+                        north[g].at[high],
+                        y_send.at[0, g],
+                        y_recv.at[0, g],
+                        lat + 1,
+                        lon,
+                    ),
+                    landed(north[g].at[high], y_recv.at[0, g]),
+                    jnp.logical_and(down, sends_down),
+                    jnp.logical_and(up, north_comes),
+                ),
+                (
+                    remote(
+                        slots.at[g, low],
+                        south[g].at[low],
+                        y_send.at[1, g],
+                        y_recv.at[1, g],
+                        lat - 1,
+                        lon,
+                    ),
+                    landed(south[g].at[low], y_recv.at[1, g]),
+                    jnp.logical_and(up, sends_up),
+                    jnp.logical_and(down, south_comes),
+                ),
+            ]
+        for copy, _, sends, _ in lists[g]:
+            pl.when(sends)(copy.start)
 
     def dense(g, lon_there, store):
         def row(t, carry):
@@ -408,8 +470,8 @@
     core_copies, z_copies = [], []
     for g in range(groups):
         loads[g].wait()
-        pl.when(up)(landed(north[g].at[high], y_recv.at[0, g]).wait)
-        pl.when(down)(landed(south[g].at[low], y_recv.at[1, g]).wait)
+        for _, arrival, _, comes in lists[g]:
+            pl.when(comes)(arrival.wait)
         for part, (theirs, ours) in enumerate(((beside_across, across), (beside, lon))):
 
             def put_away(t, value):
@@ -479,20 +541,19 @@
     ]
     for copy, move in zip(copies, moves):
         pl.when(move[4])(copy.start)
-    receive_maximum(longest_of_all)
+    receive_maximum(overflow_of_all)
     for copy in core_copies + z_copies + small:
         copy.wait_send()
     for g in range(groups):
-        pl.when(down)(to_south[g].wait_send)
-        pl.when(up)(to_north[g].wait_send)
+        for copy, _, sends, _ in lists[g]:
+            pl.when(sends)(copy.wait_send)
     for i, (copy, move) in enumerate(zip(copies, moves)):
         pl.when(move[4])(copy.wait_send)
         pl.when(move[5])(landed(move[1], halo_recv.at[i]).wait)
 
 
-def couple(
-    index, north_index, south_index, slots, atmos, longest, count, collective_id, lat_count, lon_count
-):
+def couple(operands, count, edge_count, collective_id, lat_count, lon_count):
+    _, _, _, slots, atmos, overflow = operands
     groups, total, size, cols = slots.shape
     rows, channels, cols = atmos.shape
     tiles = rows // 32
@@ -505,9 +566,9 @@
     one = pltpu.VMEM((groups, rows, size, cols), BF16)
     two = pltpu.VMEM((2, groups, rows, size, cols), BF16)
     return pl.pallas_call(
-        functools.partial(couple_kernel, lat_count, lon_count, count),
+        functools.partial(couple_kernel, lat_count, lon_count, count, edge_count),
         out_shape=[jax.ShapeDtypeStruct(s, BF16) for s in shapes]
-        + [jax.ShapeDtypeStruct(longest.shape, jnp.int32)],
+        + [jax.ShapeDtypeStruct(overflow.shape, jnp.int32)],
         in_specs=[smem] * 3 + whole_any(1) + [vmem] * 2,
         out_specs=[vmem] + whole_any(4) + [vmem],
         scratch_shapes=[received] * (3 * groups)
@@ -518,14 +579,14 @@
         + [dma((2, groups))] * 4
         + [dma((groups,))] * 2
         + [dma((8,))] * 2
-        + [pltpu.VMEM((peers,) + longest.shape, jnp.int32)]
-        + [pltpu.VMEM((2,) + longest.shape, jnp.int32)]
+        + [pltpu.VMEM((peers,) + overflow.shape, jnp.int32)]
+        + [pltpu.VMEM((2,) + overflow.shape, jnp.int32)]
         + [dma((peers,))] * 2,
         compiler_params=pltpu.CompilerParams(
             collective_id=collective_id, has_side_effects=True, vmem_limit_bytes=VMEM_LIMIT
         ),
         name="couple",
-    )(index, north_index, south_index, slots, atmos, longest)
+    )(*operands)
 
 
 def atmos_kernel(
@@ -578,10 +639,12 @@
         group = LAST_ROWS
         start = step * group
         taps = conv(second, w2_ref[...], start, group)
+        rows = []
         for i in range(group):
-            j = start + i
             value = shifted_sum(taps[:, i * 2 * cols : (i + 1) * 2 * cols])[:, :cols]
-            out_ref[j] = (a_ref[j].astype(F32) + (value + b2)).astype(BF16)
+            rows.append(a_ref[start + i].astype(F32) + (value + b2))
+        block = jnp.swapaxes(jnp.stack(rows), 0, 1).astype(BF16)
+        out_ref[:, pl.ds(pl.multiple_of(start, group), group), :] = block
         return carry
 
     lax.fori_loop(0, count // LAST_ROWS, last, 0)
@@ -592,7 +655,7 @@
     vmem = pl.BlockSpec(memory_space=pltpu.VMEM)
     return pl.pallas_call(
         functools.partial(atmos_kernel, lat_count),
-        out_shape=jax.ShapeDtypeStruct(a.shape, BF16),
+        out_shape=jax.ShapeDtypeStruct((channels, count, cols), BF16),
         in_specs=[vmem] * 9,
         out_specs=vmem,
         scratch_shapes=[
@@ -621,7 +684,6 @@
     atmos_b2,
 ):
     lat_count, lon_count = lax.axis_size("lat"), lax.axis_size("lon")
-    lat = lax.axis_index("lat")
     atmos_rows = atmos_state.shape[1]
 
     field = jnp.concatenate(
@@ -632,10 +694,10 @@
         ],
         axis=0,
     ).transpose(1, 0, 2)
-    key = ((route_dev - (lat - 1) * lon_count) * atmos_rows + route_row).reshape(1, -1)
-    count = key.shape[1]
-    top, bottom, left, right, index, north_index, south_index, meta, longest = ocean_halo(
-        field, key, lat_count, lon_count, atmos_rows
+    count = route_dev.size
+    weights = (ocean_w1, ocean_w2, atmos_w1, atmos_w2)
+    top, bottom, left, right, index, north_index, south_index, meta, overflow, *weights = ocean_halo(
+        field, route_dev, route_row, weights, lat_count, lon_count, atmos_rows
     )
     ocean_next, slots = ocean_step(
         meta,
@@ -644,18 +706,18 @@
         bottom,
         left,
         right,
-        stacked_weight(ocean_w1, 80),
+        weights[0],
         ocean_b1[None, :],
-        stacked_weight(ocean_w2, 64),
+        weights[1],
         ocean_b2[None, :],
         regrid_weight.reshape(-1, 256, 128),
         lat_count,
     )
-    operands = (index, north_index, south_index, slots, atmos_state.transpose(1, 0, 2), longest)
-    *coupled, longest = couple(*operands, SHORT, 1, lat_count, lon_count)
+    operands = (index, north_index, south_index, slots, atmos_state.transpose(1, 0, 2), overflow)
+    *coupled, overflow = couple(operands, SHORT, EDGE_SHORT, 1, lat_count, lon_count)
     first, top, bottom, left, right = lax.cond(
-        longest[0, 0] > SHORT,
-        lambda short, operands: tuple(couple(*operands, count, 2, lat_count, lon_count)[:5]),
+        overflow[0, 0] > 0,
+        lambda short, operands: tuple(couple(operands, count, count, 2, lat_count, lon_count)[:5]),
         lambda short, operands: short,
         tuple(coupled),
         operands,
@@ -666,13 +728,13 @@
         bottom,
         left,
         right,
-        stacked_weight(atmos_w1, 64),
+        weights[2],
         atmos_b1[None, :],
-        stacked_weight(atmos_w2, 64),
+        weights[3],
         atmos_b2[None, :],
         lat_count,
     )
-    return ocean_next.transpose(1, 0, 2), atmos_next.transpose(1, 0, 2)
+    return ocean_next.transpose(1, 0, 2), atmos_next
 
 
 def solution(mesh):

time: 118 us -> 103 us (0.87)
  local copies, waits for them, and re-layouts: 14.9 us -> 6.66 us
  Pallas kernels: 98.6 us -> 92 us
    pallas_call x1, Pallas kernels: 55.7 us -> 48.6 us  [couple(): pl.pallas_call(functools.partial(couple_kernel, lat_count, lon_count, cou...]
    reshape x5 -> x0, local copies, waits for them, and re-layouts: 3.83 us -> none  [the longest x4 3.18 us: stacked_weight(): return weight.transpose(3, 0, 2, 1).reshape(3 * out, 3 * padded_in)]
    unnamed x18 -> x5, local copies, waits for them, and re-layouts: 9.08 us -> 5.37 us
where the time goes in v6:
time: 103 us; the launch traced here: 102 us
  Pallas kernels  92 us (89%)
  local copies, waits for them, and re-layouts  6.66 us (6%)
  other arithmetic  2.42 us (2%)
  between operations  1.34 us (1%)
    pallas_call x1, Pallas kernels, couple(): pl.pallas_call(functools.partial(couple_kernel, lat_count, lon_count, cou...  48.6 us
    pallas_call x1, Pallas kernels, ocean_halo(): pl.pallas_call(functools.partial(ocean_halo_kernel, lat_count, lon_count,...  19.9 us
    pallas_call x1, Pallas kernels, ocean_step(): pl.pallas_call(functools.partial(ocean_kernel, lat_count), out_shape=(jax...  13.7 us
    pallas_call x1, Pallas kernels, atmos_step(): pl.pallas_call(functools.partial(atmos_kernel, lat_count), out_shape=jax....  9.77 us
    unnamed x5, local copies, waits for them, and re-layouts  5.37 us

profile of v6, /device:TPU:3, one launch (start us, length us, event | category | flops | bytes accessed | tf_op | source)
XLA Modules:
  0.0 102.4 jit_solution(9571990950909581968)
XLA Ops:
  0.6 0.0 copy-start
  0.6 0.1 pad.2.clone
  0.7 0.8 convert_bitcast_fusion
  1.6 1.9 %copy.24 = bf16[64,64,128]{2,0,1:T(8,128)(2,1)S(1)} copy(bf16[64,64,128]{2,1,0:T(8,128)(2,1)} %param.25) | data formatting | bytes 2097152 | tf_op args[9]
  3.5 0.0 copy-done
  3.5 0.7 copy.19
  4.2 1.6 %maximum_bitcast_fusion.field.x_ref = bf16[8,80,1024]{2,1,0:T(8,128)(2,1)} fusion(bf16[1,8,1024]{2,0,1:T(2,128)(2,1)S(1)} %copy.20, bf16[76,8,1024]{2,0,1:T(8,128)(2,1)S(1)} %copy.19, bf16[80]{0:T(256)(128)(2,1)S(1)} %pad.2.clone), kind=kLoop, calls=%fused_computation | loop fusion | flops 3932160 | bytes 2572448 | tf_op jit(solution)/shard_map/transpose | solution.py:696
  5.8 19.9 %ocean_halo.1 = (bf16[2,80,1024]{2,1,0:T(8,128)(2,1)}, bf16[2,80,1024]{2,1,0:T(8,128)(2,1)}, bf16[3,80,128]{2,1,0:T(8,128)(2,1)}, bf16[3,80,128]{2,1,0:T(8,128)(...) custom-call(bf16[8,80,1024]{2,1,0:T(8,128)(2,1)} %maximum_bitcast_fu, ...), custom_call_target="tpu_custom_call" | custom-call | tf_op jit(solution)/shard_map/ocean_halo/pallas_call | solution.py:200
  25.7 13.7 %ocean.1 = (bf16[8,64,1024]{2,1,0:T(8,128)(2,1)}, bf16[4,128,16,128]{3,2,1,0:T(8,128)(2,1)S(1)}) custom-call(s32[1,128]{1,0:T(1,128)} %get-tuple-element.61.meta, bf16[8,80,1024]{2,1,0:T(8,128)(2,1)} %maximum_bitcast_fusion.field.x_ref, bf16[2,80,1024]{2,1,0:T(8,128)(2,1)} %get-tuple-element.62.top_ref, bf16[2,80,1024]{2,1,0:T(8,128)(2,1)} %get-tuple-element.63.bottom_ref, ...), custom_call_target="tpu_custom_call" | custom-call | tf_op jit(solution)/shard_map/ocean/pallas_call | solution.py:312
  39.4 2.8 %copy.22 = bf16[64,8,1024]{2,1,0:T(8,128)(2,1)} copy(bf16[64,8,1024]{2,0,1:T(8,128)(2,1)} %bitcast.23) | data formatting | bytes 2097152
  42.2 48.6 %couple.3 = (bf16[64,64,128]{2,1,0:T(8,128)(2,1)S(1)}, bf16[2,64,128]{2,1,0:T(8,128)(2,1)S(1)}, bf16[2,64,128]{2,1,0:T(8,128)(2,1)S(1)}, bf16[4,64,128]{2,1,0:T(...) custom-call(s32[3,8,128]{2,1,0:T(8,128)S(1)} %get-tuple-element.69.own_index, ...), custom_call_target="tpu_custom_call" | custom-call | tf_op jit(solution)/shard_map/couple/pallas_call | solution.py:568
  90.8 1.2 %slice.3 = s32[1,1]{1,0:T(1,128)} slice(s32[8,128]{1,0:T(8,128)} %get-tuple-element.74), slice={[0:1], [0:1]} | slice | bytes 8 | tf_op jit(solution)/shard_map/slice | solution.py:719
  92.6 9.8 %atmos.1 = bf16[64,64,128]{2,1,0:T(8,128)(2,1)} custom-call(bf16[64,64,128]{2,1,0:T(8,128)(2,1)S(1)} %get-tuple-element.80.a_ref, bf16[2,64,128]{2,1,0:T(8,128)(2,1)S(1)} %get-tuple-element.81.top_ref, bf16[2,64,128]{2,1,0:T(8,128)(2,1)S(1)} %get-tuple-element.82.bottom_ref, bf16[4,64,128]{2,1,0:T(8,128)(2,1)S(1)} %get-tuple-element.83.left_ref, ...), custom_call_target="tpu_custom_call" | custom-call | tf_op jit(solution)/shard_map/atmos/pallas_call | solution.py:656
  (3 shorter events, 0.0 us)
Async XLA Ops:
  0.6 2.9 %copy-start = (bf16[76,8,1024]{2,1,0:T(8,128)(2,1)S(1)}, bf16[76,8,1024]{2,1,0:T(8,128)(2,1)}, u32[]{:S(2)}) copy-start(bf16[76,8,1024]{2,1,0:T(8,128)(2,1)} %param.16) | copy-start | bytes 3735556

commit v7 on v6

--- a/solution.py
+++ b/solution.py
@@ -12,6 +12,7 @@
 BF16 = jnp.bfloat16
 VMEM_LIMIT = 56 * 1024 * 1024
 GROUPS = 4
+MASK_AT = 76
 FIRST_ROWS = 11
 LAST_ROWS = 16
 SHORT = 32
@@ -95,20 +96,23 @@
     w2_ref,
     w3_ref,
     w4_ref,
-    top,
-    bottom,
-    left,
-    right,
+    b1_ref,
+    hidden,
     index,
     north_index,
     south_index,
     meta,
     overflow,
-    w1_out,
     w2_out,
     w3_out,
     w4_out,
+    top,
+    bottom,
+    left,
+    right,
     edges,
+    tall,
+    w1_out,
     send_sem,
     recv_sem,
 ):
@@ -161,10 +165,12 @@
         tile = jnp.where(lane // 4 == k, pltpu.roll(both, (4 * k + 2) % 128, 1), tile)
     edges[...] = tile.astype(BF16)
 
+    stack_weight(w1_ref, w1_out)
+    b1 = column(b1_ref[...])
+    tall[2 : 2 + rows, :, 0:cols] = field[...]
+
     greeted(jnp.where(edge, 5, 8))
     moves = [
-        (field.at[pl.ds(0, 2)], bottom, lat - 1, lon, up, down),
-        (field.at[pl.ds(rows - 2, 2)], top, lat + 1, lon, down, up),
         (edges, right.at[1], lat, west, always, always),
         (edges, left.at[1], lat, east, always, always),
         (edges, right.at[2], lat - 1, west, up, down),
@@ -173,6 +179,8 @@
         (edges, left.at[0], lat + 1, east, down, up),
         (index.at[0], south_index, lat - 1, lon, up, down),
         (index.at[2], north_index, lat + 1, lon, down, up),
+        (field.at[pl.ds(0, 2)], bottom, lat - 1, lon, up, down),
+        (field.at[pl.ds(rows - 2, 2)], top, lat + 1, lon, down, up),
     ]
     copies = [
         remote(src, dst, send_sem.at[i], recv_sem.at[i], a, b)
@@ -180,33 +188,83 @@
     ]
     for copy, move in zip(copies, moves):
         pl.when(move[4])(copy.start)
-    for weight, out in ((w1_ref, w1_out), (w2_ref, w2_out), (w3_ref, w3_out), (w4_ref, w4_out)):
+    for weight, out in ((w2_ref, w2_out), (w3_ref, w3_out), (w4_ref, w4_out)):
         stack_weight(weight, out)
-    for i, (copy, move) in enumerate(zip(copies, moves)):
+
+    def arrive(numbers):
+        for i in numbers:
+            pl.when(moves[i][5])(landed(moves[i][1], recv_sem.at[i]).wait)
+
+    def sides(tile, some):
+        both = jnp.where(lane % 4 < 2, left[tile], right[tile]).astype(F32)
+        for k in some:
+            side = pltpu.roll(both, (126 - 4 * k) % 128, 1).astype(BF16)
+            if tile != 1:
+                inside = lat > 0 if tile == 0 else lat < lat_count - 1
+                side = jnp.where(inside, side, jnp.zeros_like(side))
+            tall[(tile - 1) * rows + k + 2, :, cols:] = side
+
+    def conv(start):
+        for i in range(2):
+            j = start + i
+            fields = jnp.concatenate([tall[j], tall[j + 1], tall[j + 2]], axis=0)
+            taps = jnp.dot(w1_out[...], fields, preferred_element_type=F32)
+            mask = tall[j + 1, MASK_AT : MASK_AT + 1, :].astype(F32)
+            hidden[j] = (silu(shifted_sum(taps) + b1) * mask).astype(BF16)
+
+    def inner(step, carry):
+        conv(2 * step + 2)
+        return carry
+
+    def outer(step, carry):
+        conv(step * rows)
+        return carry
+
+    arrive((0, 1))
+    sides(1, range(rows))
+    lax.fori_loop(0, rows // 2 - 1, inner, 0)
+    arrive(range(2, len(moves)))
+    sides(0, range(rows - 2, rows))
+    sides(2, range(2))
+    for i in range(2):
+        tall[i, :, 0:cols] = jnp.where(up, top[i], jnp.zeros_like(top[i]))
+        tall[rows + 2 + i, :, 0:cols] = jnp.where(down, bottom[i], jnp.zeros_like(bottom[i]))
+    lax.fori_loop(0, 2, outer, 0)
+    for copy, move in zip(copies, moves):
         pl.when(move[4])(copy.wait_send)
-        pl.when(move[5])(landed(move[1], recv_sem.at[i]).wait)
-
-
-def ocean_halo(field, route_dev, route_row, weights, lat_count, lon_count, atmos_rows):
+
+
+def ocean_halo(field, route_dev, route_row, weights, b1, lat_count, lon_count, atmos_rows):
     rows, channels, cols = field.shape
     count = route_dev.size
     weights = [w.transpose(2, 3, 0, 1) for w in weights]
     stacked = [
         jax.ShapeDtypeStruct((3 * w.shape[2], 3 * (-(-w.shape[3] // 16) * 16)), BF16) for w in weights
     ]
-    shapes = [(2, channels, cols)] * 2 + [(3, channels, 128)] * 2
     table = jax.ShapeDtypeStruct((8, count), jnp.int32)
     vmem = pl.BlockSpec(memory_space=pltpu.VMEM)
+    out = weights[0].shape[2]
     return pl.pallas_call(
         functools.partial(ocean_halo_kernel, lat_count, lon_count, atmos_rows),
-        out_shape=[jax.ShapeDtypeStruct(s, BF16) for s in shapes]
-        + [jax.ShapeDtypeStruct((3,) + table.shape, jnp.int32), table, table]
-        + [jax.ShapeDtypeStruct((1, count), jnp.int32), table]
-        + stacked,
-        in_specs=[vmem] * 7,
-        out_specs=whole_any(4) + [vmem] + whole_any(2) + [vmem] * 6,
+        out_shape=[
+            jax.ShapeDtypeStruct((rows + 2, out, cols + 128), BF16),
+            jax.ShapeDtypeStruct((3,) + table.shape, jnp.int32),
+            table,
+            table,
+            jax.ShapeDtypeStruct((1, count), jnp.int32),
+            table,
+        ]
+        + stacked[1:],
+        in_specs=[vmem] * 8,
+        out_specs=[vmem] * 2 + whole_any(2) + [vmem] * 5,
         scratch_shapes=[
+            pltpu.VMEM((2, channels, cols), BF16),
+            pltpu.VMEM((2, channels, cols), BF16),
+            pltpu.VMEM((3, channels, 128), BF16),
+            pltpu.VMEM((3, channels, 128), BF16),
             pltpu.VMEM((channels, 128), BF16),
+            pltpu.VMEM((rows + 4, channels, cols + 128), BF16),
+            pltpu.VMEM(stacked[0].shape, BF16),
             pltpu.SemaphoreType.DMA((10,)),
             pltpu.SemaphoreType.DMA((10,)),
         ],
@@ -214,79 +272,45 @@
             collective_id=0, has_side_effects=True, vmem_limit_bytes=VMEM_LIMIT
         ),
         name="ocean_halo",
-    )(field, route_dev.T, route_row.T, *weights)
+    )(field, route_dev.T, route_row.T, *weights, b1)
 
 
 def ocean_kernel(
-    lat_count,
-    meta,
-    x_ref,
-    top_ref,
-    bottom_ref,
-    left_ref,
-    right_ref,
-    w1_ref,
-    b1_ref,
-    w2_ref,
-    b2_ref,
-    regrid_ref,
-    next_ref,
-    slots_ref,
-    tall,
-    hidden,
-    sums,
+    meta, hidden, mask_ref, w2_ref, b2_ref, regrid_ref, next_ref, slots_ref, sums, before, kept
 ):
-    row = lax.rem(pl.program_id(0), 16)
-    rows, channels, cols = x_ref.shape
-    mask_at = 76
-    b1, b2 = column(b1_ref[...]), column(b2_ref[...])
-
-    def first_conv(j):
-        field = jnp.concatenate([tall[j], tall[j + 1], tall[j + 2]], axis=0)
-        taps = jnp.dot(w1_ref[...], field, preferred_element_type=F32)
-        mask = tall[j + 1, mask_at : mask_at + 1, :].astype(F32)
-        hidden[j] = (silu(shifted_sum(taps) + b1) * mask).astype(BF16)
-
-    @pl.when(row == 0)
-    def _():
-        lat = lax.axis_index("lat")
-        lane = lax.broadcasted_iota(jnp.int32, (channels, 128), 1)
-        tall[2 : 2 + rows, :, 0:cols] = x_ref[...]
-        for tile in range(3):
-            both = jnp.where(lane % 4 < 2, left_ref[tile], right_ref[tile]).astype(F32)
-            for k in range(rows):
-                j = (tile - 1) * rows + k + 2
-                if j < 0 or j >= rows + 4:
-                    continue
-                side = pltpu.roll(both, (126 - 4 * k) % 128, 1).astype(BF16)
-                if tile != 1:
-                    inside = lat > 0 if tile == 0 else lat < lat_count - 1
-                    main = top_ref[j] if tile == 0 else bottom_ref[j - rows - 2]
-                    tall[j, :, 0:cols] = jnp.where(inside, main, jnp.zeros_like(main))
-                    side = jnp.where(inside, side, jnp.zeros_like(side))
-                tall[j, :, cols:] = side
-        first_conv(0)
-        first_conv(1)
-
-    first_conv(lax.rem(row + 2, 16))
+    step = lax.rem(pl.program_id(0), 16)
+    rows = next_ref.shape[1]
+    cols = next_ref.shape[2]
+    row = jnp.minimum(step, rows - 1)
+    done = jnp.maximum(step - 1, 0)
+    blocks = regrid_ref.shape[0]
+
+    previous = before[...]
+    values = []
+    for q in range(blocks):
+        both = lax.dot_general(
+            previous[:, q * 128 : (q + 1) * 128],
+            regrid_ref[q],
+            (((1,), (1,)), ((), ())),
+            preferred_element_type=F32,
+        ).astype(BF16)
+        values += [both[:, 0:128], both[:, 128:256]]
+
     field = jnp.concatenate([hidden[row], hidden[row + 1], hidden[row + 2]], axis=0)
     taps = jnp.dot(w2_ref[...], field, preferred_element_type=F32)
-    mask = tall[row + 2, mask_at : mask_at + 1, :].astype(F32)
-    result = ((shifted_sum(taps) + b2) * mask).astype(BF16)[:, :cols]
-    next_ref[0] = result
-    blocks = regrid_ref.shape[0]
+    mask = mask_ref[pl.ds(row, 1), :].astype(F32)
+    result = (shifted_sum(taps)[:, :cols] + column(b2_ref[...])) * mask
+    before[...] = result.astype(BF16)
+    kept[row] = result
+
     for q in range(blocks):
-        field = result[:, q * 128 : (q + 1) * 128]
-        both = lax.dot_general(
-            field, regrid_ref[q], (((1,), (1,)), ((), ())), preferred_element_type=F32
-        ).astype(BF16)
         for k in range(2):
-            what = meta[0, k * (rows * blocks) + row * blocks + q]
+            what = meta[0, k * (rows * blocks) + done * blocks + q]
             at = what // 2
-            value = both[:, k * 128 : (k + 1) * 128].astype(F32)
+            value = values[2 * q + k].astype(F32)
             sums[at] = jnp.where(lax.rem(what, 2) == 1, value, sums[at] + value)
 
-    @pl.when(row == rows - 1)
+    @pl.when(step == rows)
     def _():
         groups, slots, size = slots_ref.shape[:3]
 
@@ -295,12 +319,15 @@
                 slots_ref[g, i] = sums[i, g * size : (g + 1) * size].astype(BF16)
             return carry
 
-        lax.fori_loop(0, slots, rounded, 0)
-
-
-def ocean_step(meta, x, top, bottom, left, right, w1, b1, w2, b2, regrid, lat_count):
-    rows, channels, cols = x.shape
-    wide = cols + 128
+        lax.fori_loop(0, slots, rounded, 0, unroll=4)
+        for q in range(cols // 128):
+            part = slice(q * 128, (q + 1) * 128)
+            block = jnp.stack([kept[r, :, part] for r in range(rows)])
+            next_ref[:, :, part] = jnp.swapaxes(block, 0, 1).astype(BF16)
+
+
+def ocean_step(meta, hidden, mask, w2, b2, regrid):
+    rows, cols = mask.shape
     out = w2.shape[0] // 3
     slots = meta.shape[1]
 
@@ -310,29 +337,29 @@
 
     blocks = regrid.shape[0] // rows
     return pl.pallas_call(
-        functools.partial(ocean_kernel, lat_count),
+        ocean_kernel,
         out_shape=(
-            jax.ShapeDtypeStruct((rows, out, cols), BF16),
+            jax.ShapeDtypeStruct((out, rows, cols), BF16),
             jax.ShapeDtypeStruct((GROUPS, slots, out // GROUPS, 128), BF16),
         ),
         grid_spec=pltpu.PrefetchScalarGridSpec(
             num_scalar_prefetch=1,
-            grid=(rows,),
-            in_specs=[whole(a) for a in (x, top, bottom, left, right, w1, b1, w2, b2)]
-            + [pl.BlockSpec((blocks, 256, 128), lambda r, meta: (r, 0, 0))],
+            grid=(rows + 1,),
+            in_specs=[whole(a) for a in (hidden, mask, w2, b2)]
+            + [pl.BlockSpec((blocks, 256, 128), lambda r, meta: (jnp.maximum(r - 1, 0), 0, 0))],
             out_specs=[
-                pl.BlockSpec((1, out, cols), lambda r, meta: (r, 0, 0)),
+                pl.BlockSpec((out, rows, cols), lambda r, meta: (0, 0, 0)),
                 pl.BlockSpec((GROUPS, slots, out // GROUPS, 128), lambda r, meta: (0, 0, 0, 0)),
             ],
             scratch_shapes=[
-                pltpu.VMEM((rows + 4, channels, wide), BF16),
-                pltpu.VMEM((rows + 2, out, wide), BF16),
                 pltpu.VMEM((slots, out, 128), F32),
+                pltpu.VMEM((out, cols), BF16),
+                pltpu.VMEM((rows, out, cols), F32),
             ],
         ),
         compiler_params=pltpu.CompilerParams(vmem_limit_bytes=VMEM_LIMIT),
         name="ocean",
-    )(meta, x, top, bottom, left, right, w1, b1, w2, b2, regrid)
+    )(meta, hidden, mask, w2, b2, regrid)
 
 
 def couple_kernel(
@@ -696,22 +723,16 @@
     ).transpose(1, 0, 2)
     count = route_dev.size
     weights = (ocean_w1, ocean_w2, atmos_w1, atmos_w2)
-    top, bottom, left, right, index, north_index, south_index, meta, overflow, *weights = ocean_halo(
-        field, route_dev, route_row, weights, lat_count, lon_count, atmos_rows
+    hidden, index, north_index, south_index, meta, overflow, *weights = ocean_halo(
+        field, route_dev, route_row, weights, ocean_b1[None, :], lat_count, lon_count, atmos_rows
     )
     ocean_next, slots = ocean_step(
         meta,
-        field,
-        top,
-        bottom,
-        left,
-        right,
+        hidden,
+        sea_mask,
         weights[0],
-        ocean_b1[None, :],
-        weights[1],
         ocean_b2[None, :],
         regrid_weight.reshape(-1, 256, 128),
-        lat_count,
     )
     operands = (index, north_index, south_index, slots, atmos_state.transpose(1, 0, 2), overflow)
     *coupled, overflow = couple(operands, SHORT, EDGE_SHORT, 1, lat_count, lon_count)
@@ -728,13 +749,13 @@
         bottom,
         left,
         right,
+        weights[1],
+        atmos_b1[None, :],
         weights[2],
-        atmos_b1[None, :],
-        weights[3],
         atmos_b2[None, :],
         lat_count,
     )
-    return ocean_next.transpose(1, 0, 2), atmos_next
+    return ocean_next, atmos_next
 
 
 def solution(mesh):

time: 103 us -> 101 us (0.981)
  local copies, waits for them, and re-layouts: 6.66 us -> 3.89 us
    pallas_call x1, Pallas kernels: 19.9 us -> 22.9 us  [ocean_halo(): pl.pallas_call(functools.partial(ocean_halo_kernel, lat_count, lon_count,...]
    unnamed x5 -> x4, local copies, waits for them, and re-layouts: 5.37 us -> 2.6 us
    pallas_call x1, Pallas kernels: 13.7 us -> 11.1 us  [ocean_step(): pl.pallas_call(ocean_kernel, out_shape=(jax.ShapeDtypeStruct((out, rows,...]
where the time goes in v7:
time: 101 us
  Pallas kernels  93 us (92%)
  local copies, waits for them, and re-layouts  3.89 us (4%)
  other arithmetic  2.42 us (2%)
  between operations  1.34 us (1%)
    pallas_call x1, Pallas kernels, couple(): pl.pallas_call(functools.partial(couple_kernel, lat_count, lon_count, cou...  49.2 us
    pallas_call x1, Pallas kernels, ocean_halo(): pl.pallas_call(functools.partial(ocean_halo_kernel, lat_count, lon_count,...  22.9 us
    pallas_call x1, Pallas kernels, ocean_step(): pl.pallas_call(ocean_kernel, out_shape=(jax.ShapeDtypeStruct((out, rows,...  11.1 us
    pallas_call x1, Pallas kernels, atmos_step(): pl.pallas_call(functools.partial(atmos_kernel, lat_count), out_shape=jax....  9.77 us
    unnamed x4, local copies, waits for them, and re-layouts  2.6 us

profile of v7, /device:TPU:3, one launch (start us, length us, event | category | flops | bytes accessed | tf_op | source)
XLA Modules:
  0.0 100.7 jit_solution(13551700039650224478)
XLA Ops:
  0.6 0.0 copy-start
  0.6 0.1 pad.2.clone
  0.7 0.8 convert_bitcast_fusion
  1.6 1.9 %copy.22 = bf16[64,64,128]{2,0,1:T(8,128)(2,1)S(1)} copy(bf16[64,64,128]{2,1,0:T(8,128)(2,1)} %param.25) | data formatting | bytes 2097152 | tf_op args[9]
  3.5 0.0 copy-done
  3.5 0.7 copy.18
  4.2 1.6 %maximum_bitcast_fusion.field = bf16[8,80,1024]{2,1,0:T(8,128)(2,1)} fusion(bf16[1,8,1024]{2,0,1:T(2,128)(2,1)S(1)} %copy.19, bf16[76,8,1024]{2,0,1:T(8,128)(2,1)S(1)} %copy.18, bf16[80]{0:T(256)(128)(2,1)S(1)} %pad.2.clone), kind=kLoop, calls=%fused_computation | loop fusion | flops 3932160 | bytes 2572448 | tf_op jit(solution)/shard_map/transpose | solution.py:723
  5.8 22.9 %ocean_halo.1 = (bf16[10,64,1152]{2,1,0:T(8,128)(2,1)}, s32[3,8,128]{2,1,0:T(8,128)S(1)}, s32[8,128]{1,0:T(8,128)S(1)}, s32[8,128]{1,0:T(8,128)S(1)}, s32[1,128]...) custom-call(bf16[8,80,1024]{2,1,0:T(8,128)(2,1)} %maximum_bitcast_fu, ...), custom_call_target="tpu_custom_call" | custom-call | tf_op jit(solution)/shard_map/ocean_halo/pallas_call | solution.py:247
  28.7 11.1 %ocean.1 = (bf16[64,8,1024]{2,1,0:T(8,128)(2,1)}, bf16[4,128,16,128]{3,2,1,0:T(8,128)(2,1)S(1)}) custom-call(s32[1,128]{1,0:T(1,128)} %get-tuple-element.57.meta, bf16[10,64,1152]{2,1,0:T(8,128)(2,1)} %get-tuple-element.58.hidden, s32[8,1024]{1,0:T(8,128)} %mask_ref.1, bf16[192,192]{1,0:T(8,128)(2,1)} %get-tuple-element.59.w2_ref, f32[1,64]{1,0:T(1,128)} %bitcast.29, ...), custom_call_target="tpu_custom_call" | custom-call | tf_op jit(solution)/shard_map/ocean/pallas_call | solution.py:339
  39.8 49.2 %couple.3 = (bf16[64,64,128]{2,1,0:T(8,128)(2,1)S(1)}, bf16[2,64,128]{2,1,0:T(8,128)(2,1)S(1)}, bf16[2,64,128]{2,1,0:T(8,128)(2,1)S(1)}, bf16[4,64,128]{2,1,0:T(...) custom-call(s32[3,8,128]{2,1,0:T(8,128)S(1)} %get-tuple-element.61.own_index, ...), custom_call_target="tpu_custom_call" | custom-call | tf_op jit(solution)/shard_map/couple/pallas_call | solution.py:595
  89.0 1.2 %slice.3 = s32[1,1]{1,0:T(1,128)} slice(s32[8,128]{1,0:T(8,128)} %get-tuple-element.66), slice={[0:1], [0:1]} | slice | bytes 8 | tf_op jit(solution)/shard_map/slice | solution.py:740
  90.9 9.8 %atmos.1 = bf16[64,64,128]{2,1,0:T(8,128)(2,1)} custom-call(bf16[64,64,128]{2,1,0:T(8,128)(2,1)S(1)} %get-tuple-element.72.a_ref, bf16[2,64,128]{2,1,0:T(8,128)(2,1)S(1)} %get-tuple-element.73.top_ref, bf16[2,64,128]{2,1,0:T(8,128)(2,1)S(1)} %get-tuple-element.74.bottom_ref, bf16[4,64,128]{2,1,0:T(8,128)(2,1)S(1)} %get-tuple-element.75.left_ref, ...), custom_call_target="tpu_custom_call" | custom-call | tf_op jit(solution)/shard_map/atmos/pallas_call | solution.py:683
  (3 shorter events, 0.0 us)
Async XLA Ops:
  0.6 2.9 %copy-start = (bf16[76,8,1024]{2,1,0:T(8,128)(2,1)S(1)}, bf16[76,8,1024]{2,1,0:T(8,128)(2,1)}, u32[]{:S(2)}) copy-start(bf16[76,8,1024]{2,1,0:T(8,128)(2,1)} %param.16) | copy-start | bytes 3735556

commit v8 on v7

--- a/solution.py
+++ b/solution.py
@@ -12,7 +12,6 @@
 BF16 = jnp.bfloat16
 VMEM_LIMIT = 56 * 1024 * 1024
 GROUPS = 4
-MASK_AT = 76
 FIRST_ROWS = 11
 LAST_ROWS = 16
 SHORT = 32
@@ -89,7 +88,8 @@
     lat_count,
     lon_count,
     atmos_rows,
-    field,
+    x_ref,
+    mask_ref,
     dev_ref,
     row_ref,
     w1_ref,
@@ -106,8 +106,6 @@
     w2_out,
     w3_out,
     w4_out,
-    top,
-    bottom,
     left,
     right,
     edges,
@@ -117,7 +115,8 @@
     recv_sem,
 ):
     lat, lon = lax.axis_index("lat"), lax.axis_index("lon")
-    rows, channels, cols = field.shape
+    rows, inputs, cols = x_ref.shape
+    channels = tall.shape[1]
     west = lax.rem(lon + lon_count - 1, lon_count)
     east = lax.rem(lon + 1, lon_count)
     up, down, always = lat > 0, lat < lat_count - 1, lat >= 0
@@ -136,20 +135,22 @@
     across = lax.rem(across, blocks) * keys.shape[0] + lax.div(across, blocks)
     along = lax.broadcasted_iota(jnp.int32, (count, count), 0)
     along = lax.rem(along, blocks) * keys.shape[0] + lax.div(along, blocks)
-    place = jnp.sum((key_down < key).astype(jnp.int32), axis=0, keepdims=True)
     again = jnp.logical_and(key_down == key, along < across).astype(jnp.int32)
-    meta[...] = place * 2 + 1 - jnp.max(again, axis=0, keepdims=True)
+    place = jnp.sum((key_down < key).astype(jnp.int32) + again, axis=0, keepdims=True)
     place_down = column(place)
+    first_down = column(1 - jnp.max(again, axis=0, keepdims=True))
+    lane = lax.broadcasted_iota(jnp.int32, (1, count), 1)
+    meta[0:1, :] = place
+    meta[1:2, :] = jnp.max(jnp.where(place_down == lane, first_down, 0), axis=0, keepdims=True)
     per_step = lon_count * atmos_rows
-    lane = lax.broadcasted_iota(jnp.int32, (1, count), 1)
     for step in range(3):
         for row in range(8):
             if row * count < per_step:
                 number = lane + (step * per_step + row * count)
-                places = jnp.min(
-                    jnp.where(key_down == number, place_down, count), axis=0, keepdims=True
+                places = jnp.max(
+                    jnp.where(key_down == number, place_down, -1), axis=0, keepdims=True
                 )
-                index[step, row : row + 1, :] = places
+                index[step, row : row + 1, :] = jnp.where(places < 0, count, places)
             else:
                 index[step, row : row + 1, :] = jnp.full((1, count), count, jnp.int32)
     low = jnp.sum((key < per_step).astype(jnp.int32), axis=1, keepdims=True)
@@ -159,17 +160,34 @@
     overflow[...] = jnp.broadcast_to(long, overflow.shape)
 
     lane = lax.broadcasted_iota(jnp.int32, (channels, 128), 1)
+    extra = lax.broadcasted_iota(jnp.int32, (channels - inputs, cols), 0)
+    for k in range(rows):
+        tall[k + 2, 0:inputs, 0:cols] = x_ref[k]
+        mask = jnp.where(extra == 0, mask_ref[k : k + 1, :], 0).astype(F32).astype(BF16)
+        tall[k + 2, inputs:, 0:cols] = mask
     tile = jnp.zeros((channels, 128), F32)
     for k in range(rows):
-        both = jnp.where(lane < 64, field[k, :, 0:128], field[k, :, cols - 128 :]).astype(F32)
+        low, high = tall[k + 2, :, 0:128], tall[k + 2, :, cols - 128 : cols]
+        both = jnp.where(lane < 64, low, high).astype(F32)
         tile = jnp.where(lane // 4 == k, pltpu.roll(both, (4 * k + 2) % 128, 1), tile)
     edges[...] = tile.astype(BF16)
 
     stack_weight(w1_ref, w1_out)
     b1 = column(b1_ref[...])
-    tall[2 : 2 + rows, :, 0:cols] = field[...]
+    blank = jnp.zeros((2, channels, cols), BF16)
+
+    @pl.when(jnp.logical_not(up))
+    def _():
+        tall[0:2, :, 0:cols] = blank
+
+    @pl.when(jnp.logical_not(down))
+    def _():
+        tall[rows + 2 :, :, 0:cols] = blank
 
     greeted(jnp.where(edge, 5, 8))
+    def two(start):
+        return tall.at[pl.ds(start, 2), :, pl.ds(0, cols)]
+
     moves = [
         (edges, right.at[1], lat, west, always, always),
         (edges, left.at[1], lat, east, always, always),
@@ -179,8 +197,8 @@
         (edges, left.at[0], lat + 1, east, down, up),
         (index.at[0], south_index, lat - 1, lon, up, down),
         (index.at[2], north_index, lat + 1, lon, down, up),
-        (field.at[pl.ds(0, 2)], bottom, lat - 1, lon, up, down),
-        (field.at[pl.ds(rows - 2, 2)], top, lat + 1, lon, down, up),
+        (two(2), two(rows + 2), lat - 1, lon, up, down),
+        (two(rows), two(0), lat + 1, lon, down, up),
     ]
     copies = [
         remote(src, dst, send_sem.at[i], recv_sem.at[i], a, b)
@@ -209,7 +227,7 @@
             j = start + i
             fields = jnp.concatenate([tall[j], tall[j + 1], tall[j + 2]], axis=0)
             taps = jnp.dot(w1_out[...], fields, preferred_element_type=F32)
-            mask = tall[j + 1, MASK_AT : MASK_AT + 1, :].astype(F32)
+            mask = tall[j + 1, inputs : inputs + 1, :].astype(F32)
             hidden[j] = (silu(shifted_sum(taps) + b1) * mask).astype(BF16)
 
     def inner(step, carry):
@@ -226,16 +244,14 @@
     arrive(range(2, len(moves)))
     sides(0, range(rows - 2, rows))
     sides(2, range(2))
-    for i in range(2):
-        tall[i, :, 0:cols] = jnp.where(up, top[i], jnp.zeros_like(top[i]))
-        tall[rows + 2 + i, :, 0:cols] = jnp.where(down, bottom[i], jnp.zeros_like(bottom[i]))
     lax.fori_loop(0, 2, outer, 0)
     for copy, move in zip(copies, moves):
         pl.when(move[4])(copy.wait_send)
 
 
-def ocean_halo(field, route_dev, route_row, weights, b1, lat_count, lon_count, atmos_rows):
-    rows, channels, cols = field.shape
+def ocean_halo(x, sea_mask, route_dev, route_row, weights, b1, lat_count, lon_count, atmos_rows):
+    rows, inputs, cols = x.shape
+    channels = -(-(inputs + 1) // 16) * 16
     count = route_dev.size
     weights = [w.transpose(2, 3, 0, 1) for w in weights]
     stacked = [
@@ -251,15 +267,13 @@
             jax.ShapeDtypeStruct((3,) + table.shape, jnp.int32),
             table,
             table,
-            jax.ShapeDtypeStruct((1, count), jnp.int32),
+            jax.ShapeDtypeStruct((2, count), jnp.int32),
             table,
         ]
         + stacked[1:],
-        in_specs=[vmem] * 8,
+        in_specs=[vmem] * 9,
         out_specs=[vmem] * 2 + whole_any(2) + [vmem] * 5,
         scratch_shapes=[
-            pltpu.VMEM((2, channels, cols), BF16),
-            pltpu.VMEM((2, channels, cols), BF16),
             pltpu.VMEM((3, channels, 128), BF16),
             pltpu.VMEM((3, channels, 128), BF16),
             pltpu.VMEM((channels, 128), BF16),
@@ -272,11 +286,11 @@
             collective_id=0, has_side_effects=True, vmem_limit_bytes=VMEM_LIMIT
         ),
         name="ocean_halo",
-    )(field, route_dev.T, route_row.T, *weights, b1)
+    )(x, sea_mask, route_dev.T, route_row.T, *weights, b1)
 
 
 def ocean_kernel(
-    meta, hidden, mask_ref, w2_ref, b2_ref, regrid_ref, next_ref, slots_ref, sums, before, kept
+    meta, hidden, mask_ref, w2_ref, b2_ref, regrid_ref, next_ref, slots_ref, listed, before, kept
 ):
     step = lax.rem(pl.program_id(0), 16)
     rows = next_ref.shape[1]
@@ -305,21 +319,21 @@
 
     for q in range(blocks):
         for k in range(2):
-            what = meta[0, k * (rows * blocks) + done * blocks + q]
-            at = what // 2
-            value = values[2 * q + k].astype(F32)
-            sums[at] = jnp.where(lax.rem(what, 2) == 1, value, sums[at] + value)
+            place = meta[0, k * (rows * blocks) + done * blocks + q]
+            listed[place] = values[2 * q + k]
 
     @pl.when(step == rows)
     def _():
         groups, slots, size = slots_ref.shape[:3]
 
-        def rounded(i, carry):
+        def add(i, run):
+            value = listed[i].astype(F32)
+            run = jnp.where(meta[1, i] == 1, value, run + value)
             for g in range(groups):
-                slots_ref[g, i] = sums[i, g * size : (g + 1) * size].astype(BF16)
-            return carry
-
-        lax.fori_loop(0, slots, rounded, 0, unroll=4)
+                slots_ref[g, i] = run[g * size : (g + 1) * size].astype(BF16)
+            return run
+
+        lax.fori_loop(0, slots, add, jnp.zeros(listed.shape[1:], F32), unroll=4)
         for q in range(cols // 128):
             part = slice(q * 128, (q + 1) * 128)
             block = jnp.stack([kept[r, :, part] for r in range(rows)])
@@ -352,7 +366,7 @@
                 pl.BlockSpec((GROUPS, slots, out // GROUPS, 128), lambda r, meta: (0, 0, 0, 0)),
             ],
             scratch_shapes=[
-                pltpu.VMEM((slots, out, 128), F32),
+                pltpu.VMEM((slots, out, 128), BF16),
                 pltpu.VMEM((out, cols), BF16),
                 pltpu.VMEM((rows, out, cols), F32),
             ],
@@ -425,7 +439,10 @@
             landed(gathered.at[i], max_recv.at[i]).wait()
             value = jnp.maximum(value, gathered[i])
         waiting.clear()
-        target[...] = value
+        if target is None:
+            overflow_of_all[0] = jnp.max(value)
+        else:
+            target[...] = value
         return target
 
     everything = pl.ds(0, total)
@@ -568,7 +585,7 @@
     ]
     for copy, move in zip(copies, moves):
         pl.when(move[4])(copy.start)
-    receive_maximum(overflow_of_all)
+    receive_maximum(None)
     for copy in core_copies + z_copies + small:
         copy.wait_send()
     for g in range(groups):
@@ -595,9 +612,9 @@
     return pl.pallas_call(
         functools.partial(couple_kernel, lat_count, lon_count, count, edge_count),
         out_shape=[jax.ShapeDtypeStruct(s, BF16) for s in shapes]
-        + [jax.ShapeDtypeStruct(overflow.shape, jnp.int32)],
+        + [jax.ShapeDtypeStruct((1,), jnp.int32)],
         in_specs=[smem] * 3 + whole_any(1) + [vmem] * 2,
-        out_specs=[vmem] + whole_any(4) + [vmem],
+        out_specs=[vmem] + whole_any(4) + [smem],
         scratch_shapes=[received] * (3 * groups)
         + [two] * 3
         + [one] * 2
@@ -713,18 +730,18 @@
     lat_count, lon_count = lax.axis_size("lat"), lax.axis_size("lon")
     atmos_rows = atmos_state.shape[1]
 
-    field = jnp.concatenate(
-        [
-            ocean_state,
-            sea_mask.astype(BF16)[None],
-            jnp.zeros((3,) + sea_mask.shape, BF16),
-        ],
-        axis=0,
-    ).transpose(1, 0, 2)
     count = route_dev.size
     weights = (ocean_w1, ocean_w2, atmos_w1, atmos_w2)
     hidden, index, north_index, south_index, meta, overflow, *weights = ocean_halo(
-        field, route_dev, route_row, weights, ocean_b1[None, :], lat_count, lon_count, atmos_rows
+        ocean_state.transpose(1, 0, 2),
+        sea_mask,
+        route_dev,
+        route_row,
+        weights,
+        ocean_b1[None, :],
+        lat_count,
+        lon_count,
+        atmos_rows,
     )
     ocean_next, slots = ocean_step(
         meta,
@@ -737,7 +754,7 @@
     operands = (index, north_index, south_index, slots, atmos_state.transpose(1, 0, 2), overflow)
     *coupled, overflow = couple(operands, SHORT, EDGE_SHORT, 1, lat_count, lon_count)
     first, top, bottom, left, right = lax.cond(
-        overflow[0, 0] > 0,
+        overflow[0] > 0,
         lambda short, operands: tuple(couple(operands, count, count, 2, lat_count, lon_count)[:5]),
         lambda short, operands: short,
         tuple(coupled),

time: 101 us -> 98.7 us (0.977)
  other arithmetic: 2.42 us -> 0 us
    transpose x1 -> x0, other arithmetic: 1.58 us -> none  [per_device(): field = jnp.concatenate([ocean_state, sea_mask.astype(BF16)[None], jnp.ze...]
    slice x1 -> x0, local copies, waits for them, and re-layouts: 1.18 us -> none  [per_device(): overflow[0, 0] > 0]
    unnamed x4, local copies, waits for them, and re-layouts: 2.6 us -> 3.78 us
where the time goes in v8:
time: 98.7 us; the launch traced here: 98.3 us
  Pallas kernels  93.3 us (95%)
  local copies, waits for them, and re-layouts  3.78 us (4%)
  between operations  1.23 us (1%)
    pallas_call x1, Pallas kernels, couple(): pl.pallas_call(functools.partial(couple_kernel, lat_count, lon_count, cou...  49.1 us
    pallas_call x1, Pallas kernels, ocean_halo(): pl.pallas_call(functools.partial(ocean_halo_kernel, lat_count, lon_count,...  22.9 us
    pallas_call x1, Pallas kernels, ocean_step(): pl.pallas_call(ocean_kernel, out_shape=(jax.ShapeDtypeStruct((out, rows,...  11.5 us
    pallas_call x1, Pallas kernels, atmos_step(): pl.pallas_call(functools.partial(atmos_kernel, lat_count), out_shape=jax....  9.77 us
    unnamed x4, local copies, waits for them, and re-layouts  3.78 us

profile of v8, /device:TPU:3, one launch (start us, length us, event | category | flops | bytes accessed | tf_op | source)
XLA Modules:
  0.0 98.3 jit_solution(15965613673675339884)
XLA Ops:
  0.6 0.0 copy-start
  0.6 2.0 %copy.21 = bf16[64,64,128]{2,0,1:T(8,128)(2,1)S(1)} copy(bf16[64,64,128]{2,1,0:T(8,128)(2,1)} %param.25) | data formatting | bytes 2097152 | tf_op args[9]
  2.6 0.0 copy-done
  2.7 1.8 %copy.20 = bf16[76,8,1024]{2,0,1:T(8,128)(2,1)} copy(bf16[76,8,1024]{2,1,0:T(8,128)(2,1)S(1)} %copy-done) | data formatting | bytes 2490368 | tf_op args[0]
  4.4 22.9 %ocean_halo.1 = (bf16[10,64,1152]{2,1,0:T(8,128)(2,1)}, s32[3,8,128]{2,1,0:T(8,128)S(1)}, s32[8,128]{1,0:T(8,128)S(1)}, s32[8,128]{1,0:T(8,128)S(1)}, s32[2,128]...) custom-call(bf16[8,76,1024]{2,1,0:T(8,128)(2,1)} %bitcast.20, ...), custom_call_target="tpu_custom_call" | custom-call | tf_op jit(solution)/shard_map/ocean_halo/pallas_call | solution.py:263
  27.4 11.5 %ocean.1 = (bf16[64,8,1024]{2,1,0:T(8,128)(2,1)}, bf16[4,128,16,128]{3,2,1,0:T(8,128)(2,1)S(1)}) custom-call(s32[2,128]{1,0:T(2,128)} %get-tuple-element.57.meta, bf16[10,64,1152]{2,1,0:T(8,128)(2,1)} %get-tuple-element.58.hidden, s32[8,1024]{1,0:T(8,128)} %mask_ref.3, bf16[192,192]{1,0:T(8,128)(2,1)} %get-tuple-element.59.w2_ref, f32[1,64]{1,0:T(1,128)} %bitcast.29, ...), custom_call_target="tpu_custom_call" | custom-call | tf_op jit(solution)/shard_map/ocean/pallas_call | solution.py:353
  38.8 49.1 %couple.3 = (bf16[64,64,128]{2,1,0:T(8,128)(2,1)S(1)}, bf16[2,64,128]{2,1,0:T(8,128)(2,1)S(1)}, bf16[2,64,128]{2,1,0:T(8,128)(2,1)S(1)}, bf16[4,64,128]{2,1,0:T(...) custom-call(s32[3,8,128]{2,1,0:T(8,128)S(1)} %get-tuple-element.61.own_index, ...), custom_call_target="tpu_custom_call" | custom-call | tf_op jit(solution)/shard_map/couple/pallas_call | solution.py:612
  88.5 9.8 %atmos.1 = bf16[64,64,128]{2,1,0:T(8,128)(2,1)} custom-call(bf16[64,64,128]{2,1,0:T(8,128)(2,1)S(1)} %get-tuple-element.72.a_ref, bf16[2,64,128]{2,1,0:T(8,128)(2,1)S(1)} %get-tuple-element.73.top_ref, bf16[2,64,128]{2,1,0:T(8,128)(2,1)S(1)} %get-tuple-element.74.bottom_ref, bf16[4,64,128]{2,1,0:T(8,128)(2,1)S(1)} %get-tuple-element.75.left_ref, ...), custom_call_target="tpu_custom_call" | custom-call | tf_op jit(solution)/shard_map/atmos/pallas_call | solution.py:700
  (1 shorter events, 0.0 us)
Async XLA Ops:
  0.6 2.0 %copy-start = (bf16[76,8,1024]{2,1,0:T(8,128)(2,1)S(1)}, bf16[76,8,1024]{2,1,0:T(8,128)(2,1)}, u32[]{:S(2)}) copy-start(bf16[76,8,1024]{2,1,0:T(8,128)(2,1)} %param.16) | copy-start | bytes 3735556

commit v9 on v8

--- a/solution.py
+++ b/solution.py
@@ -12,8 +12,8 @@
 BF16 = jnp.bfloat16
 VMEM_LIMIT = 56 * 1024 * 1024
 GROUPS = 4
-FIRST_ROWS = 11
-LAST_ROWS = 16
+FIRST_ROWS = 22
+LAST_ROWS = 32
 SHORT = 32
 EDGE_SHORT = 48
 
@@ -63,6 +63,14 @@
 
 def landed(ref, sem):
     return pltpu.make_async_copy(ref, ref, sem)
+
+
+def list_lons(lat, lon):
+    across = lax.rem(lon + 2, 4)
+    odd = lax.rem(lon, 2) == 1
+    up = jnp.where(jnp.logical_and(odd, lax.rem(lat, 4) == 0), across, lon)
+    down = jnp.where(jnp.logical_and(odd, lax.rem(lat, 4) == 3), across, lon)
+    return up, down
 
 
 def greet(partners):
@@ -124,6 +132,8 @@
     partners = [(lat, west, always), (lat, east, always)]
     for there, ok in ((lat - 1, up), (lat + 1, down)):
         partners += [(there, side, ok) for side in (west, lon, east)]
+    up_lon, down_lon = list_lons(lat, lon)
+    partners += [(lat - 1, up_lon, up), (lat + 1, down_lon, down)]
     greet(partners)
 
     keys = (dev_ref[...] - (lat - 1) * lon_count) * atmos_rows + row_ref[...]
@@ -184,7 +194,7 @@
     def _():
         tall[rows + 2 :, :, 0:cols] = blank
 
-    greeted(jnp.where(edge, 5, 8))
+    greeted(jnp.where(edge, 6, 10))
     def two(start):
         return tall.at[pl.ds(start, 2), :, pl.ds(0, cols)]
 
@@ -195,8 +205,8 @@
         (edges, left.at[2], lat - 1, east, up, down),
         (edges, right.at[0], lat + 1, west, down, up),
         (edges, left.at[0], lat + 1, east, down, up),
-        (index.at[0], south_index, lat - 1, lon, up, down),
-        (index.at[2], north_index, lat + 1, lon, down, up),
+        (index.at[0], south_index, lat - 1, up_lon, up, down),
+        (index.at[2], north_index, lat + 1, down_lon, down, up),
         (two(2), two(rows + 2), lat - 1, lon, up, down),
         (two(rows), two(0), lat + 1, lon, down, up),
     ]
@@ -222,29 +232,20 @@
                 side = jnp.where(inside, side, jnp.zeros_like(side))
             tall[(tile - 1) * rows + k + 2, :, cols:] = side
 
-    def conv(start):
-        for i in range(2):
-            j = start + i
+    def conv(some):
+        for j in some:
             fields = jnp.concatenate([tall[j], tall[j + 1], tall[j + 2]], axis=0)
             taps = jnp.dot(w1_out[...], fields, preferred_element_type=F32)
             mask = tall[j + 1, inputs : inputs + 1, :].astype(F32)
             hidden[j] = (silu(shifted_sum(taps) + b1) * mask).astype(BF16)
 
-    def inner(step, carry):
-        conv(2 * step + 2)
-        return carry
-
-    def outer(step, carry):
-        conv(step * rows)
-        return carry
-
     arrive((0, 1))
     sides(1, range(rows))
-    lax.fori_loop(0, rows // 2 - 1, inner, 0)
+    conv(range(2, rows))
     arrive(range(2, len(moves)))
     sides(0, range(rows - 2, rows))
     sides(2, range(2))
-    lax.fori_loop(0, 2, outer, 0)
+    conv((0, 1, rows, rows + 1))
     for copy, move in zip(copies, moves):
         pl.when(move[4])(copy.wait_send)
 
@@ -290,87 +291,69 @@
 
 
 def ocean_kernel(
-    meta, hidden, mask_ref, w2_ref, b2_ref, regrid_ref, next_ref, slots_ref, listed, before, kept
+    meta, hidden, mask_ref, w2_ref, b2_ref, regrid, next_ref, slots_ref, listed, weights, kept, sem
 ):
-    step = lax.rem(pl.program_id(0), 16)
-    rows = next_ref.shape[1]
-    cols = next_ref.shape[2]
-    row = jnp.minimum(step, rows - 1)
-    done = jnp.maximum(step - 1, 0)
-    blocks = regrid_ref.shape[0]
-
-    previous = before[...]
-    values = []
-    for q in range(blocks):
-        both = lax.dot_general(
-            previous[:, q * 128 : (q + 1) * 128],
-            regrid_ref[q],
-            (((1,), (1,)), ((), ())),
-            preferred_element_type=F32,
-        ).astype(BF16)
-        values += [both[:, 0:128], both[:, 128:256]]
-
-    field = jnp.concatenate([hidden[row], hidden[row + 1], hidden[row + 2]], axis=0)
-    taps = jnp.dot(w2_ref[...], field, preferred_element_type=F32)
-    mask = mask_ref[pl.ds(row, 1), :].astype(F32)
-    result = (shifted_sum(taps)[:, :cols] + column(b2_ref[...])) * mask
-    before[...] = result.astype(BF16)
-    kept[row] = result
-
-    for q in range(blocks):
-        for k in range(2):
-            place = meta[0, k * (rows * blocks) + done * blocks + q]
-            listed[place] = values[2 * q + k]
-
-    @pl.when(step == rows)
-    def _():
-        groups, slots, size = slots_ref.shape[:3]
-
-        def add(i, run):
-            value = listed[i].astype(F32)
-            run = jnp.where(meta[1, i] == 1, value, run + value)
-            for g in range(groups):
-                slots_ref[g, i] = run[g * size : (g + 1) * size].astype(BF16)
-            return run
-
-        lax.fori_loop(0, slots, add, jnp.zeros(listed.shape[1:], F32), unroll=4)
-        for q in range(cols // 128):
-            part = slice(q * 128, (q + 1) * 128)
-            block = jnp.stack([kept[r, :, part] for r in range(rows)])
-            next_ref[:, :, part] = jnp.swapaxes(block, 0, 1).astype(BF16)
+    rows, cols = mask_ref.shape
+    blocks = regrid.shape[0] // rows
+    copies = []
+    for r in range(rows):
+        some = pl.ds(r * blocks, blocks)
+        copies.append(pltpu.make_async_copy(regrid.at[some], weights.at[some], sem.at[r]))
+        copies[r].start()
+    b2 = column(b2_ref[...])
+    for r in range(rows):
+        field = jnp.concatenate([hidden[r], hidden[r + 1], hidden[r + 2]], axis=0)
+        taps = jnp.dot(w2_ref[...], field, preferred_element_type=F32)
+        result = (shifted_sum(taps)[:, :cols] + b2) * mask_ref[r : r + 1, :].astype(F32)
+        kept[r] = result
+        result = result.astype(BF16)
+        copies[r].wait()
+        for q in range(blocks):
+            both = lax.dot_general(
+                result[:, q * 128 : (q + 1) * 128],
+                weights[r * blocks + q],
+                (((1,), (1,)), ((), ())),
+                preferred_element_type=F32,
+            ).astype(BF16)
+            for k in range(2):
+                place = meta[0, k * (rows * blocks) + r * blocks + q]
+                listed[place] = both[:, k * 128 : (k + 1) * 128]
+
+    groups, slots, size = slots_ref.shape[:3]
+
+    def add(i, run):
+        value = listed[i].astype(F32)
+        run = jnp.where(meta[1, i] == 1, value, run + value)
+        for g in range(groups):
+            slots_ref[g, i] = run[g * size : (g + 1) * size].astype(BF16)
+        return run
+
+    lax.fori_loop(0, slots, add, jnp.zeros(listed.shape[1:], F32), unroll=8)
+    for q in range(cols // 128):
+        part = slice(q * 128, (q + 1) * 128)
+        block = jnp.stack([kept[r, :, part] for r in range(rows)])
+        next_ref[:, :, part] = jnp.swapaxes(block, 0, 1).astype(BF16)
 
 
 def ocean_step(meta, hidden, mask, w2, b2, regrid):
     rows, cols = mask.shape
     out = w2.shape[0] // 3
     slots = meta.shape[1]
-
-    def whole(array):
-        zeros = (0,) * array.ndim
-        return pl.BlockSpec(array.shape, lambda r, meta: zeros)
-
-    blocks = regrid.shape[0] // rows
+    vmem = pl.BlockSpec(memory_space=pltpu.VMEM)
     return pl.pallas_call(
         ocean_kernel,
         out_shape=(
             jax.ShapeDtypeStruct((out, rows, cols), BF16),
             jax.ShapeDtypeStruct((GROUPS, slots, out // GROUPS, 128), BF16),
         ),
-        grid_spec=pltpu.PrefetchScalarGridSpec(
-            num_scalar_prefetch=1,
-            grid=(rows + 1,),
-            in_specs=[whole(a) for a in (hidden, mask, w2, b2)]
-            + [pl.BlockSpec((blocks, 256, 128), lambda r, meta: (jnp.maximum(r - 1, 0), 0, 0))],
-            out_specs=[
-                pl.BlockSpec((out, rows, cols), lambda r, meta: (0, 0, 0)),
-                pl.BlockSpec((GROUPS, slots, out // GROUPS, 128), lambda r, meta: (0, 0, 0, 0)),
-            ],
-            scratch_shapes=[
-                pltpu.VMEM((slots, out, 128), BF16),
-                pltpu.VMEM((out, cols), BF16),
-                pltpu.VMEM((rows, out, cols), F32),
-            ],
-        ),
+        in_specs=[pl.BlockSpec(memory_space=pltpu.SMEM)] + [vmem] * 4 + whole_any(1),
+        out_specs=[vmem] * 2,
+        scratch_shapes=[
+            pltpu.VMEM((slots, out, 128), BF16),
+            pltpu.VMEM(regrid.shape, BF16),
+            pltpu.VMEM((rows, out, cols), F32),
+            pltpu.SemaphoreType.DMA((rows,)),
+        ],
         compiler_params=pltpu.CompilerParams(vmem_limit_bytes=VMEM_LIMIT),
         name="ocean",
     )(meta, hidden, mask, w2, b2, regrid)
@@ -414,6 +397,8 @@
         [(lax.rem(four + k, fours) * 4 + inner, lon) for k in range(1, fours)],
     ]
     partners += [(a, b, always) for peers in rounds[1:] for a, b in peers]
+    up_lon, down_lon = list_lons(lat, lon)
+    partners += [(lat - 1, up_lon, up), (lat + 1, down_lon, down)]
     greet(partners)
 
     groups, total, size, cols = slots.shape
@@ -455,7 +440,7 @@
     for buffer in (own, north, south):
         for g in range(groups):
             buffer[g][total] = jnp.zeros((size, cols), BF16)
-    greeted(jnp.where(edge, 6, 9) + sum(len(peers) for peers in rounds[1:]))
+    greeted(jnp.where(edge, 7, 11) + sum(len(peers) for peers in rounds[1:]))
     send_maximum(0)
 
     last = lat_count - 1
@@ -475,7 +460,7 @@
                         y_send.at[0, g],
                         y_recv.at[0, g],
                         lat + 1,
-                        lon,
+                        down_lon,
                     ),
                     landed(north[g].at[high], y_recv.at[0, g]),
                     jnp.logical_and(down, sends_down),
@@ -488,7 +473,7 @@
                         y_send.at[1, g],
                         y_recv.at[1, g],
                         lat - 1,
-                        lon,
+                        up_lon,
                     ),
                     landed(south[g].at[low], y_recv.at[1, g]),
                     jnp.logical_and(up, sends_up),

time: 98.7 us -> 91.9 us (0.931)
  Pallas kernels: 93.3 us -> 86 us
    pallas_call x1, Pallas kernels: 49.1 us -> 46.4 us  [couple(): pl.pallas_call(functools.partial(couple_kernel, lat_count, lon_count, cou...]
    pallas_call x1, Pallas kernels: 11.5 us -> 8.78 us  [ocean_step(): pl.pallas_call(ocean_kernel, out_shape=(jax.ShapeDtypeStruct((out, rows,...]
where the time goes in v9:
time: 91.9 us; the launch traced here: 91.1 us
  Pallas kernels  86 us (94%)
  local copies, waits for them, and re-layouts  3.78 us (4%)
  between operations  1.24 us (1%)
    pallas_call x1, Pallas kernels, couple(): pl.pallas_call(functools.partial(couple_kernel, lat_count, lon_count, cou...  46.4 us
    pallas_call x1, Pallas kernels, ocean_halo(): pl.pallas_call(functools.partial(ocean_halo_kernel, lat_count, lon_count,...  22 us
    pallas_call x1, Pallas kernels, atmos_step(): pl.pallas_call(functools.partial(atmos_kernel, lat_count), out_shape=jax....  8.84 us
    pallas_call x1, Pallas kernels, ocean_step(): pl.pallas_call(ocean_kernel, out_shape=(jax.ShapeDtypeStruct((out, rows,...  8.78 us
    unnamed x4, local copies, waits for them, and re-layouts  3.78 us

profile of v9, /device:TPU:3, one launch (start us, length us, event | category | flops | bytes accessed | tf_op | source)
XLA Modules:
  0.0 91.1 jit_solution(13104979577215583819)
XLA Ops:
  0.6 0.0 copy-start
  0.6 2.0 %copy.21 = bf16[64,64,128]{2,0,1:T(8,128)(2,1)S(1)} copy(bf16[64,64,128]{2,1,0:T(8,128)(2,1)} %param.25) | data formatting | bytes 2097152 | tf_op args[9]
  2.6 0.0 copy-done
  2.7 1.8 %copy.20 = bf16[76,8,1024]{2,0,1:T(8,128)(2,1)} copy(bf16[76,8,1024]{2,1,0:T(8,128)(2,1)S(1)} %copy-done) | data formatting | bytes 2490368 | tf_op args[0]
  4.4 22.0 %ocean_halo.1 = (bf16[10,64,1152]{2,1,0:T(8,128)(2,1)}, s32[3,8,128]{2,1,0:T(8,128)S(1)}, s32[8,128]{1,0:T(8,128)S(1)}, s32[8,128]{1,0:T(8,128)S(1)}, s32[2,128]...) custom-call(bf16[8,76,1024]{2,1,0:T(8,128)(2,1)} %bitcast.20, ...), custom_call_target="tpu_custom_call" | custom-call | tf_op jit(solution)/shard_map/ocean_halo/pallas_call | solution.py:264
  26.5 8.8 %ocean.1 = (bf16[64,8,1024]{2,1,0:T(8,128)(2,1)}, bf16[4,128,16,128]{3,2,1,0:T(8,128)(2,1)S(1)}) custom-call(s32[2,128]{1,0:T(2,128)} %get-tuple-element.57.meta, bf16[10,64,1152]{2,1,0:T(8,128)(2,1)} %get-tuple-element.58.hidden, s32[8,1024]{1,0:T(8,128)} %mask_ref.3, bf16[192,192]{1,0:T(8,128)(2,1)} %get-tuple-element.59.w2_ref, f32[1,64]{1,0:T(1,128)} %bitcast.29, ...), custom_call_target="tpu_custom_call" | custom-call | tf_op jit(solution)/shard_map/ocean/pallas_call | solution.py:343
  35.3 46.4 %couple.3 = (bf16[64,64,128]{2,1,0:T(8,128)(2,1)S(1)}, bf16[2,64,128]{2,1,0:T(8,128)(2,1)S(1)}, bf16[2,64,128]{2,1,0:T(8,128)(2,1)S(1)}, bf16[4,64,128]{2,1,0:T(...) custom-call(s32[3,8,128]{2,1,0:T(8,128)S(1)} %get-tuple-element.61.own_index, ...), custom_call_target="tpu_custom_call" | custom-call | tf_op jit(solution)/shard_map/couple/pallas_call | solution.py:597
  82.2 8.8 %atmos.1 = bf16[64,64,128]{2,1,0:T(8,128)(2,1)} custom-call(bf16[64,64,128]{2,1,0:T(8,128)(2,1)S(1)} %get-tuple-element.72.a_ref, bf16[2,64,128]{2,1,0:T(8,128)(2,1)S(1)} %get-tuple-element.73.top_ref, bf16[2,64,128]{2,1,0:T(8,128)(2,1)S(1)} %get-tuple-element.74.bottom_ref, bf16[4,64,128]{2,1,0:T(8,128)(2,1)S(1)} %get-tuple-element.75.left_ref, ...), custom_call_target="tpu_custom_call" | custom-call | tf_op jit(solution)/shard_map/atmos/pallas_call | solution.py:685
  (1 shorter events, 0.0 us)
Async XLA Ops:
  0.6 2.0 %copy-start = (bf16[76,8,1024]{2,1,0:T(8,128)(2,1)S(1)}, bf16[76,8,1024]{2,1,0:T(8,128)(2,1)}, u32[]{:S(2)}) copy-start(bf16[76,8,1024]{2,1,0:T(8,128)(2,1)} %param.16) | copy-start | bytes 3735556

commit v10 on v9

--- a/solution.py
+++ b/solution.py
@@ -123,7 +123,7 @@
     recv_sem,
 ):
     lat, lon = lax.axis_index("lat"), lax.axis_index("lon")
-    rows, inputs, cols = x_ref.shape
+    inputs, rows, cols = x_ref.shape
     channels = tall.shape[1]
     west = lax.rem(lon + lon_count - 1, lon_count)
     east = lax.rem(lon + 1, lon_count)
@@ -170,11 +170,17 @@
     overflow[...] = jnp.broadcast_to(long, overflow.shape)
 
     lane = lax.broadcasted_iota(jnp.int32, (channels, 128), 1)
-    extra = lax.broadcasted_iota(jnp.int32, (channels - inputs, cols), 0)
-    for k in range(rows):
-        tall[k + 2, 0:inputs, 0:cols] = x_ref[k]
-        mask = jnp.where(extra == 0, mask_ref[k : k + 1, :], 0).astype(F32).astype(BF16)
-        tall[k + 2, inputs:, 0:cols] = mask
+    for q in range(cols // 128):
+        part = slice(q * 128, (q + 1) * 128)
+        block = jnp.concatenate(
+            [
+                x_ref[:, :, part].astype(F32),
+                mask_ref[:, part].astype(F32)[None],
+                jnp.zeros((channels - inputs - 1, rows, 128), F32),
+            ],
+            axis=0,
+        )
+        tall[2 : 2 + rows, :, part] = jnp.swapaxes(block, 0, 1).astype(BF16)
     tile = jnp.zeros((channels, 128), F32)
     for k in range(rows):
         low, high = tall[k + 2, :, 0:128], tall[k + 2, :, cols - 128 : cols]
@@ -251,7 +257,7 @@
 
 
 def ocean_halo(x, sea_mask, route_dev, route_row, weights, b1, lat_count, lon_count, atmos_rows):
-    rows, inputs, cols = x.shape
+    inputs, rows, cols = x.shape
     channels = -(-(inputs + 1) // 16) * 16
     count = route_dev.size
     weights = [w.transpose(2, 3, 0, 1) for w in weights]
@@ -408,7 +414,7 @@
     load_sem, y_send, y_recv, core_send, core_recv, z_send, z_recv, halo_send, halo_recv = scratch[
         3 * groups + 6 : 3 * groups + 15
     ]
-    gathered, partial, max_send, max_recv = scratch[3 * groups + 15 :]
+    gathered, partial, max_send, max_recv, base = scratch[3 * groups + 15 :]
     held, waiting, small = overflow, [], []
 
     def send_maximum(number):
@@ -440,6 +446,9 @@
     for buffer in (own, north, south):
         for g in range(groups):
             buffer[g][total] = jnp.zeros((size, cols), BF16)
+    for at in range(0, rows, 16):
+        block = atmos[:, at : at + 16, :].astype(F32)
+        base[at : at + 16] = jnp.swapaxes(block, 0, 1).astype(BF16)
     greeted(jnp.where(edge, 7, 11) + sum(len(peers) for peers in rounds[1:]))
     send_maximum(0)
 
@@ -548,7 +557,7 @@
                     + from_core[1, g, r].astype(F32)
                     + from_z[g, r].astype(F32)
                 )
-                v = (atmos[r, part].astype(F32) + flux).astype(BF16)
+                v = (base[r, part].astype(F32) + flux).astype(BF16)
                 first[r, part] = v
                 rolled = pltpu.roll(v.astype(F32), (4 * k + 2) % cols, 1)
                 edge = jnp.where(lane // 4 == k, rolled, edge)
@@ -584,7 +593,7 @@
 def couple(operands, count, edge_count, collective_id, lat_count, lon_count):
     _, _, _, slots, atmos, overflow = operands
     groups, total, size, cols = slots.shape
-    rows, channels, cols = atmos.shape
+    channels, rows, cols = atmos.shape
     tiles = rows // 32
     vmem = pl.BlockSpec(memory_space=pltpu.VMEM)
     smem = pl.BlockSpec(memory_space=pltpu.SMEM)
@@ -610,7 +619,8 @@
         + [dma((8,))] * 2
         + [pltpu.VMEM((peers,) + overflow.shape, jnp.int32)]
         + [pltpu.VMEM((2,) + overflow.shape, jnp.int32)]
-        + [dma((peers,))] * 2,
+        + [dma((peers,))] * 2
+        + [pltpu.VMEM((rows, channels, cols), BF16)],
         compiler_params=pltpu.CompilerParams(
             collective_id=collective_id, has_side_effects=True, vmem_limit_bytes=VMEM_LIMIT
         ),
@@ -718,7 +728,7 @@
     count = route_dev.size
     weights = (ocean_w1, ocean_w2, atmos_w1, atmos_w2)
     hidden, index, north_index, south_index, meta, overflow, *weights = ocean_halo(
-        ocean_state.transpose(1, 0, 2),
+        ocean_state,
         sea_mask,
         route_dev,
         route_row,
@@ -736,7 +746,7 @@
         ocean_b2[None, :],
         regrid_weight.reshape(-1, 256, 128),
     )
-    operands = (index, north_index, south_index, slots, atmos_state.transpose(1, 0, 2), overflow)
+    operands = (index, north_index, south_index, slots, atmos_state, overflow)
     *coupled, overflow = couple(operands, SHORT, EDGE_SHORT, 1, lat_count, lon_count)
     first, top, bottom, left, right = lax.cond(
         overflow[0] > 0,

time: 91.9 us -> 89.2 us (0.971)
  local copies, waits for them, and re-layouts: 3.78 us -> 0.01 us
  Pallas kernels: 86 us -> 87.1 us
    unnamed x4 -> x2, local copies, waits for them, and re-layouts: 3.78 us -> 0.01 us
where the time goes in v10:
time: 89.2 us; the launch traced here: 88.4 us
  Pallas kernels  87.1 us (98%)
  between operations  1.3 us (1%)
    pallas_call x1, Pallas kernels, couple(): pl.pallas_call(functools.partial(couple_kernel, lat_count, lon_count, cou...  46.8 us
    pallas_call x1, Pallas kernels, ocean_halo(): pl.pallas_call(functools.partial(ocean_halo_kernel, lat_count, lon_count,...  22.1 us
    pallas_call x1, Pallas kernels, atmos_step(): pl.pallas_call(functools.partial(atmos_kernel, lat_count), out_shape=jax....  9.23 us
    pallas_call x1, Pallas kernels, ocean_step(): pl.pallas_call(ocean_kernel, out_shape=(jax.ShapeDtypeStruct((out, rows,...  8.87 us

profile of v10, /device:TPU:3, one launch (start us, length us, event | category | flops | bytes accessed | tf_op | source)
XLA Modules:
  0.0 88.4 jit_solution(5853929788325160802)
XLA Ops:
  0.6 22.1 %ocean_halo.1 = (bf16[10,64,1152]{2,1,0:T(8,128)(2,1)}, s32[3,8,128]{2,1,0:T(8,128)S(1)}, s32[8,128]{1,0:T(8,128)S(1)}, s32[8,128]{1,0:T(8,128)S(1)}, s32[2,128]...) custom-call(bf16[76,8,1024]{2,1,0:T(8,128)(2,1)} %x_ref.1, ...), custom_call_target="tpu_custom_call" | custom-call | tf_op jit(solution)/shard_map/ocean_halo/pallas_call | solution.py:270
  22.8 0.0 copy-start
  22.8 8.9 %ocean.1 = (bf16[64,8,1024]{2,1,0:T(8,128)(2,1)}, bf16[4,128,16,128]{3,2,1,0:T(8,128)(2,1)S(1)}) custom-call(s32[2,128]{1,0:T(2,128)} %get-tuple-element.57.meta, bf16[10,64,1152]{2,1,0:T(8,128)(2,1)} %get-tuple-element.58.hidden, s32[8,1024]{1,0:T(8,128)} %mask_ref.3, bf16[192,192]{1,0:T(8,128)(2,1)} %get-tuple-element.59.w2_ref, f32[1,64]{1,0:T(1,128)} %bitcast.20, ...), custom_call_target="tpu_custom_call" | custom-call | tf_op jit(solution)/shard_map/ocean/pallas_call | solution.py:349
  31.7 0.0 copy-done
  31.7 46.8 %couple.3 = (bf16[64,64,128]{2,1,0:T(8,128)(2,1)}, bf16[2,64,128]{2,1,0:T(8,128)(2,1)S(1)}, bf16[2,64,128]{2,1,0:T(8,128)(2,1)S(1)}, bf16[4,64,128]{2,1,0:T(8,12...) custom-call(s32[3,8,128]{2,1,0:T(8,128)S(1)} %get-tuple-element.61.own_index, ...), custom_call_target="tpu_custom_call" | custom-call | tf_op jit(solution)/shard_map/couple/pallas_call | solution.py:606
  79.2 9.2 %atmos.3 = bf16[64,64,128]{2,1,0:T(8,128)(2,1)} custom-call(bf16[64,64,128]{2,1,0:T(8,128)(2,1)} %get-tuple-element.72.a_ref, bf16[2,64,128]{2,1,0:T(8,128)(2,1)S(1)} %get-tuple-element.73.top_ref, bf16[2,64,128]{2,1,0:T(8,128)(2,1)S(1)} %get-tuple-element.74.bottom_ref, bf16[4,64,128]{2,1,0:T(8,128)(2,1)S(1)} %get-tuple-element.75.left_ref, ...), custom_call_target="tpu_custom_call" | custom-call | tf_op jit(solution)/shard_map/atmos/pallas_call | solution.py:695
  (1 shorter events, 0.0 us)
Async XLA Ops:
  22.8 8.9 %copy-start = (bf16[64,64,128]{2,1,0:T(8,128)(2,1)S(1)}, bf16[64,64,128]{2,1,0:T(8,128)(2,1)}, u32[]{:S(2)}) copy-start(bf16[64,64,128]{2,1,0:T(8,128)(2,1)} %atmos.2) | copy-start | bytes 3145732

commit v11 on v10

--- a/solution.py
+++ b/solution.py
@@ -10,7 +10,6 @@
 MESH = pl.DeviceIdType.MESH
 F32 = jnp.float32
 BF16 = jnp.bfloat16
-VMEM_LIMIT = 56 * 1024 * 1024
 GROUPS = 4
 FIRST_ROWS = 22
 LAST_ROWS = 32
@@ -290,7 +289,7 @@
             pltpu.SemaphoreType.DMA((10,)),
         ],
         compiler_params=pltpu.CompilerParams(
-            collective_id=0, has_side_effects=True, vmem_limit_bytes=VMEM_LIMIT
+            collective_id=0, has_side_effects=True, vmem_limit_bytes=24 * 1024 * 1024
         ),
         name="ocean_halo",
     )(x, sea_mask, route_dev.T, route_row.T, *weights, b1)
@@ -360,7 +359,7 @@
             pltpu.VMEM((rows, out, cols), F32),
             pltpu.SemaphoreType.DMA((rows,)),
         ],
-        compiler_params=pltpu.CompilerParams(vmem_limit_bytes=VMEM_LIMIT),
+        compiler_params=pltpu.CompilerParams(vmem_limit_bytes=52 * 1024 * 1024),
         name="ocean",
     )(meta, hidden, mask, w2, b2, regrid)
 
@@ -622,7 +621,7 @@
         + [dma((peers,))] * 2
         + [pltpu.VMEM((rows, channels, cols), BF16)],
         compiler_params=pltpu.CompilerParams(
-            collective_id=collective_id, has_side_effects=True, vmem_limit_bytes=VMEM_LIMIT
+            collective_id=collective_id, has_side_effects=True, vmem_limit_bytes=40 * 1024 * 1024
         ),
         name="couple",
     )(*operands)
@@ -701,7 +700,7 @@
             pltpu.VMEM((count + 4, channels, 2 * cols), BF16),
             pltpu.VMEM((count + 2, channels, 2 * cols), BF16),
         ],
-        compiler_params=pltpu.CompilerParams(vmem_limit_bytes=VMEM_LIMIT),
+        compiler_params=pltpu.CompilerParams(vmem_limit_bytes=40 * 1024 * 1024),
         name="atmos",
     )(a, top, bottom, left, right, w1, b1, w2, b2)
 

time: 89.2 us -> 94.7 us (1.062)
  local copies, waits for them, and re-layouts: 0.01 us -> 9.12 us
  Pallas kernels: 87.1 us -> 83.1 us
    unnamed x2 -> x28, local copies, waits for them, and re-layouts: 0.01 us -> 9.12 us
    pallas_call x1, Pallas kernels: 22.1 us -> 19.2 us  [ocean_halo(): pl.pallas_call(functools.partial(ocean_halo_kernel, lat_count, lon_count,...]
where the time goes in v11:
time: 94.7 us; the launch traced here: 93.7 us
  Pallas kernels  83.1 us (88%)
  local copies, waits for them, and re-layouts  9.12 us (10%)
  between operations  1.42 us (1%)
    pallas_call x1, Pallas kernels, couple(): pl.pallas_call(functools.partial(couple_kernel, lat_count, lon_count, cou...  46.9 us
    pallas_call x1, Pallas kernels, ocean_halo(): pl.pallas_call(functools.partial(ocean_halo_kernel, lat_count, lon_count,...  19.2 us
    unnamed x28, local copies, waits for them, and re-layouts  9.12 us
    pallas_call x1, Pallas kernels, atmos_step(): pl.pallas_call(functools.partial(atmos_kernel, lat_count), out_shape=jax....  9.12 us
    pallas_call x1, Pallas kernels, ocean_step(): pl.pallas_call(ocean_kernel, out_shape=(jax.ShapeDtypeStruct((out, rows,...  7.93 us

profile of v11, /device:TPU:3, one launch (start us, length us, event | category | flops | bytes accessed | tf_op | source)
XLA Modules:
  0.0 93.7 jit_solution(14261772389377967194)
XLA Ops:
  0.6 0.0 copy-start
  0.6 1.3 %copy-done = bf16[76,8,1024]{2,1,0:T(8,128)(2,1)S(1)} copy-done((bf16[76,8,1024]{2,1,0:T(8,128)(2,1)S(1)}, bf16[76,8,1024]{2,1,0:T(8,128)(2,1)}, u32[]{:S(2)}) %copy-start) | copy-done | bytes 1245208
  1.9 0.0 copy-start.1
  1.9 0.9 copy-done.1
  2.8 0.0 copy-start.2
  2.8 0.9 copy-done.2
  3.7 0.0 copy-start.3
  3.8 0.9 copy-done.3
  4.7 0.0 copy-start.4
  4.7 0.9 copy-done.4
  5.6 0.0 copy-start.5
  5.6 0.8 copy-done.5
  6.3 0.0 copy-start.7
  6.3 0.7 copy-done.7
  7.0 0.0 copy-start.8
  7.0 0.7 copy-done.8
  7.7 0.0 copy-start.9
  7.7 0.7 copy-done.9
  8.3 19.2 %ocean_halo.1 = (bf16[10,64,1152]{2,1,0:T(8,128)(2,1)S(1)}, s32[3,8,128]{2,1,0:T(8,128)S(1)}, s32[8,128]{1,0:T(8,128)S(1)}, s32[8,128]{1,0:T(8,128)S(1)}, s32[2,...) custom-call(bf16[76,8,1024]{2,1,0:T(8,128)(2,1)S(1)} %copy-done, ...), custom_call_target="tpu_custom_call" | custom-call | tf_op jit(solution)/shard_map/ocean_halo/pallas_call | solution.py:269
  27.6 0.0 copy-start.6
  27.6 0.7 copy-done.6
  28.3 0.0 copy-start.10
  28.3 0.7 copy-done.10
  29.0 0.0 copy-start.13
  29.0 7.9 %ocean.1 = (bf16[64,8,1024]{2,1,0:T(8,128)(2,1)}, bf16[4,128,16,128]{3,2,1,0:T(8,128)(2,1)S(1)}) custom-call(s32[2,128]{1,0:T(2,128)S(1)} %get-tuple-element.57.meta, bf16[10,64,1152]{2,1,0:T(8,128)(2,1)S(1)} %get-tuple-element.58.hidden, s32[8,1024]{1,0:T(8,128)S(1)} %copy-done.6, bf16[192,192]{1,0:T(8,128)(2,1)S(1)} %get-tuple-element.59.w2_ref, ...), custom_call_target="tpu_custom_call" | custom-call | tf_op jit(solution)/shard_map/ocean/pallas_call | solution.py:348
  36.9 0.0 copy-done.13
  36.9 46.9 %couple.3 = (bf16[64,64,128]{2,1,0:T(8,128)(2,1)}, bf16[2,64,128]{2,1,0:T(8,128)(2,1)S(1)}, bf16[2,64,128]{2,1,0:T(8,128)(2,1)}, bf16[4,64,128]{2,1,0:T(8,128)(2...) custom-call(s32[3,8,128]{2,1,0:T(8,128)S(1)} %get-tuple-element.61.own_index, ...), custom_call_target="tpu_custom_call" | custom-call | tf_op jit(solution)/shard_map/couple/pallas_call | solution.py:605
  83.8 0.0 copy-start.11
  83.8 0.0 copy-start.12
  84.5 0.0 copy-done.11
  84.6 0.0 copy-done.12
  84.6 9.1 %atmos.3 = bf16[64,64,128]{2,1,0:T(8,128)(2,1)} custom-call(bf16[64,64,128]{2,1,0:T(8,128)(2,1)} %get-tuple-element.72.a_ref, bf16[2,64,128]{2,1,0:T(8,128)(2,1)S(1)} %get-tuple-element.73.top_ref, bf16[2,64,128]{2,1,0:T(8,128)(2,1)} %get-tuple-element.74.bottom_ref, bf16[4,64,128]{2,1,0:T(8,128)(2,1)S(1)} %get-tuple-element.75.left_ref, ...), custom_call_target="tpu_custom_call" | custom-call | tf_op jit(solution)/shard_map/atmos/pallas_call | solution.py:694
  (1 shorter events, 0.0 us)
Async XLA Ops:
  0.6 1.3 %copy-start = (bf16[76,8,1024]{2,1,0:T(8,128)(2,1)S(1)}, bf16[76,8,1024]{2,1,0:T(8,128)(2,1)}, u32[]{:S(2)}) copy-start(bf16[76,8,1024]{2,1,0:T(8,128)(2,1)} %x_ref.1) | copy-start | bytes 3735556
  1.9 0.9 copy-start.1
  2.8 0.9 copy-start.2
  3.7 0.9 copy-start.3
  4.7 0.9 copy-start.4
  5.6 0.8 copy-start.5
  6.3 0.7 copy-start.7
  7.0 0.7 copy-start.8
  7.7 0.7 copy-start.9
  27.6 0.8 copy-start.6
  28.3 0.7 copy-start.10
  29.0 7.9 %copy-start.13 = (bf16[64,64,128]{2,1,0:T(8,128)(2,1)S(1)}, bf16[64,64,128]{2,1,0:T(8,128)(2,1)}, u32[]{:S(2)}) copy-start(bf16[64,64,128]{2,1,0:T(8,128)(2,1)} %atmos.2) | copy-start | bytes 3145732
  83.8 0.7 copy-start.11
  83.8 0.7 copy-start.12

commit v12 on v10

--- a/solution.py
+++ b/solution.py
@@ -96,14 +96,14 @@
     lat_count,
     lon_count,
     atmos_rows,
-    x_ref,
-    mask_ref,
+    x_hbm,
+    mask_hbm,
+    w1_hbm,
+    w2_hbm,
+    w3_hbm,
+    w4_hbm,
     dev_ref,
     row_ref,
-    w1_ref,
-    w2_ref,
-    w3_ref,
-    w4_ref,
     b1_ref,
     hidden,
     index,
@@ -119,6 +119,13 @@
     edges,
     tall,
     w1_out,
+    x_ref,
+    mask_ref,
+    w1_ref,
+    w2_ref,
+    w3_ref,
+    w4_ref,
+    load_sem,
     send_sem,
     recv_sem,
 ):
@@ -135,6 +142,17 @@
     up_lon, down_lon = list_lons(lat, lon)
     partners += [(lat - 1, up_lon, up), (lat + 1, down_lon, down)]
     greet(partners)
+    loads = []
+    for src, dst in (
+        (x_hbm, x_ref),
+        (mask_hbm, mask_ref),
+        (w1_hbm, w1_ref),
+        (w2_hbm, w2_ref),
+        (w3_hbm, w3_ref),
+        (w4_hbm, w4_ref),
+    ):
+        loads.append(pltpu.make_async_copy(src, dst, load_sem.at[len(loads)]))
+        loads[-1].start()
 
     keys = (dev_ref[...] - (lat - 1) * lon_count) * atmos_rows + row_ref[...]
     key = jnp.concatenate([keys[k : k + 1] for k in range(keys.shape[0])], axis=1)
@@ -170,6 +188,8 @@
     overflow[...] = jnp.broadcast_to(long, overflow.shape)
 
     lane = lax.broadcasted_iota(jnp.int32, (channels, 128), 1)
+    loads[0].wait()
+    loads[1].wait()
     for q in range(cols // 128):
         part = slice(q * 128, (q + 1) * 128)
         block = jnp.concatenate(
@@ -188,6 +208,7 @@
         tile = jnp.where(lane // 4 == k, pltpu.roll(both, (4 * k + 2) % 128, 1), tile)
     edges[...] = tile.astype(BF16)
 
+    loads[2].wait()
     stack_weight(w1_ref, w1_out)
     b1 = column(b1_ref[...])
     blank = jnp.zeros((2, channels, cols), BF16)
@@ -222,6 +243,8 @@
     ]
     for copy, move in zip(copies, moves):
         pl.when(move[4])(copy.start)
+    for load in loads[3:]:
+        load.wait()
     for weight, out in ((w2_ref, w2_out), (w3_ref, w3_out), (w4_ref, w4_out)):
         stack_weight(weight, out)
 
@@ -278,7 +301,7 @@
             table,
         ]
         + stacked[1:],
-        in_specs=[vmem] * 9,
+        in_specs=whole_any(6) + [vmem] * 3,
         out_specs=[vmem] * 2 + whole_any(2) + [vmem] * 5,
         scratch_shapes=[
             pltpu.VMEM((3, channels, 128), BF16),
@@ -286,6 +309,10 @@
             pltpu.VMEM((channels, 128), BF16),
             pltpu.VMEM((rows + 4, channels, cols + 128), BF16),
             pltpu.VMEM(stacked[0].shape, BF16),
+            pltpu.VMEM(x.shape, BF16),
+            pltpu.VMEM(sea_mask.shape, jnp.int32),
+            *[pltpu.VMEM(w.shape, BF16) for w in weights],
+            pltpu.SemaphoreType.DMA((6,)),
             pltpu.SemaphoreType.DMA((10,)),
             pltpu.SemaphoreType.DMA((10,)),
         ],
@@ -293,7 +320,7 @@
             collective_id=0, has_side_effects=True, vmem_limit_bytes=VMEM_LIMIT
         ),
         name="ocean_halo",
-    )(x, sea_mask, route_dev.T, route_row.T, *weights, b1)
+    )(x, sea_mask, *weights, route_dev.T, route_row.T, b1)
 
 
 def ocean_kernel(
@@ -374,8 +401,8 @@
     north_index,
     south_index,
     slots,
-    atmos,
-    overflow,
+    atmos_hbm,
+    overflow_hbm,
     first,
     top,
     bottom,
@@ -414,7 +441,12 @@
     load_sem, y_send, y_recv, core_send, core_recv, z_send, z_recv, halo_send, halo_recv = scratch[
         3 * groups + 6 : 3 * groups + 15
     ]
-    gathered, partial, max_send, max_recv, base = scratch[3 * groups + 15 :]
+    gathered, partial, max_send, max_recv, base = scratch[3 * groups + 15 : 3 * groups + 20]
+    atmos, overflow, more_sem = scratch[3 * groups + 20 :]
+    atmos_load = pltpu.make_async_copy(atmos_hbm, atmos, more_sem.at[0])
+    overflow_load = pltpu.make_async_copy(overflow_hbm, overflow, more_sem.at[1])
+    atmos_load.start()
+    overflow_load.start()
     held, waiting, small = overflow, [], []
 
     def send_maximum(number):
@@ -446,6 +478,8 @@
     for buffer in (own, north, south):
         for g in range(groups):
             buffer[g][total] = jnp.zeros((size, cols), BF16)
+    atmos_load.wait()
+    overflow_load.wait()
     for at in range(0, rows, 16):
         block = atmos[:, at : at + 16, :].astype(F32)
         base[at : at + 16] = jnp.swapaxes(block, 0, 1).astype(BF16)
@@ -607,7 +641,7 @@
         functools.partial(couple_kernel, lat_count, lon_count, count, edge_count),
         out_shape=[jax.ShapeDtypeStruct(s, BF16) for s in shapes]
         + [jax.ShapeDtypeStruct((1,), jnp.int32)],
-        in_specs=[smem] * 3 + whole_any(1) + [vmem] * 2,
+        in_specs=[smem] * 3 + whole_any(3),
         out_specs=[vmem] + whole_any(4) + [smem],
         scratch_shapes=[received] * (3 * groups)
         + [two] * 3
@@ -620,7 +654,8 @@
         + [pltpu.VMEM((peers,) + overflow.shape, jnp.int32)]
         + [pltpu.VMEM((2,) + overflow.shape, jnp.int32)]
         + [dma((peers,))] * 2
-        + [pltpu.VMEM((rows, channels, cols), BF16)],
+        + [pltpu.VMEM((rows, channels, cols), BF16)]
+        + [pltpu.VMEM(atmos.shape, BF16), pltpu.VMEM(overflow.shape, jnp.int32), dma((2,))],
         compiler_params=pltpu.CompilerParams(
             collective_id=collective_id, has_side_effects=True, vmem_limit_bytes=VMEM_LIMIT
         ),

time: 89.2 us -> 88.4 us (level)
    pallas_call x1, Pallas kernels: 22.1 us -> 19.9 us  [ocean_halo(): pl.pallas_call(functools.partial(ocean_halo_kernel, lat_count, lon_count,...]
    pallas_call x1, Pallas kernels: 46.8 us -> 48.6 us  [couple(): pl.pallas_call(functools.partial(couple_kernel, lat_count, lon_count, cou...]
where the time goes in v12:
time: 88.4 us; the launch traced here: 88 us
  Pallas kernels  86.7 us (98%)
  between operations  1.3 us (1%)
    pallas_call x1, Pallas kernels, couple(): pl.pallas_call(functools.partial(couple_kernel, lat_count, lon_count, cou...  48.6 us
    pallas_call x1, Pallas kernels, ocean_halo(): pl.pallas_call(functools.partial(ocean_halo_kernel, lat_count, lon_count,...  19.9 us
    pallas_call x1, Pallas kernels, atmos_step(): pl.pallas_call(functools.partial(atmos_kernel, lat_count), out_shape=jax....  9.23 us
    pallas_call x1, Pallas kernels, ocean_step(): pl.pallas_call(ocean_kernel, out_shape=(jax.ShapeDtypeStruct((out, rows,...  8.87 us

profile of v12, /device:TPU:3, one launch (start us, length us, event | category | flops | bytes accessed | tf_op | source)
XLA Modules:
  0.0 88.0 jit_solution(6738181693822416153)
XLA Ops:
  0.6 19.9 %ocean_halo.1 = (bf16[10,64,1152]{2,1,0:T(8,128)(2,1)}, s32[3,8,128]{2,1,0:T(8,128)S(1)}, s32[8,128]{1,0:T(8,128)S(1)}, s32[8,128]{1,0:T(8,128)S(1)}, s32[2,128]...) custom-call(bf16[76,8,1024]{2,1,0:T(8,128)(2,1)} %x_hbm.1, ...), custom_call_target="tpu_custom_call" | custom-call | tf_op jit(solution)/shard_map/ocean_halo/pallas_call | solution.py:293
  20.6 0.0 copy-start
  20.6 8.9 %ocean.1 = (bf16[64,8,1024]{2,1,0:T(8,128)(2,1)}, bf16[4,128,16,128]{3,2,1,0:T(8,128)(2,1)S(1)}) custom-call(s32[2,128]{1,0:T(2,128)} %get-tuple-element.57.meta, bf16[10,64,1152]{2,1,0:T(8,128)(2,1)} %get-tuple-element.58.hidden, s32[8,1024]{1,0:T(8,128)} %mask_ref.1, bf16[192,192]{1,0:T(8,128)(2,1)} %get-tuple-element.59.w2_ref, f32[1,64]{1,0:T(1,128)} %bitcast.20, ...), custom_call_target="tpu_custom_call" | custom-call | tf_op jit(solution)/shard_map/ocean/pallas_call | solution.py:376
  29.5 0.0 copy-done
  29.5 48.6 %couple.3 = (bf16[64,64,128]{2,1,0:T(8,128)(2,1)}, bf16[2,64,128]{2,1,0:T(8,128)(2,1)S(1)}, bf16[2,64,128]{2,1,0:T(8,128)(2,1)S(1)}, bf16[4,64,128]{2,1,0:T(8,12...) custom-call(s32[3,8,128]{2,1,0:T(8,128)S(1)} %get-tuple-element.61.own_index, ...), custom_call_target="tpu_custom_call" | custom-call | tf_op jit(solution)/shard_map/couple/pallas_call | solution.py:640
  78.7 9.2 %atmos.1 = bf16[64,64,128]{2,1,0:T(8,128)(2,1)} custom-call(bf16[64,64,128]{2,1,0:T(8,128)(2,1)} %get-tuple-element.72.a_ref, bf16[2,64,128]{2,1,0:T(8,128)(2,1)S(1)} %get-tuple-element.73.top_ref, bf16[2,64,128]{2,1,0:T(8,128)(2,1)S(1)} %get-tuple-element.74.bottom_ref, bf16[4,64,128]{2,1,0:T(8,128)(2,1)S(1)} %get-tuple-element.75.left_ref, ...), custom_call_target="tpu_custom_call" | custom-call | tf_op jit(solution)/shard_map/atmos/pallas_call | solution.py:730
  (1 shorter events, 0.0 us)
Async XLA Ops:
  20.6 8.9 %copy-start = (bf16[64,64,128]{2,1,0:T(8,128)(2,1)S(1)}, bf16[64,64,128]{2,1,0:T(8,128)(2,1)}, u32[]{:S(2)}) copy-start(bf16[64,64,128]{2,1,0:T(8,128)(2,1)} %atmos_hbm.1) | copy-start | bytes 3145732
